TPU v7x, 128 devices: a whole 4x4x4 slice. The times are simulated.
128 devices in a mesh: visit: 4 (over z), sky: 32 (over y, x, core).
Axes of the slice: x: 4, y: 4, z: 4, core: 2. Of those that a mesh axis runs over, the one named last changes fastest.
Arguments:
- exposure: bfloat16 [4, 4096, 4096], P('visit', 'sky'), may hold values from -6 to 6
- variance: bfloat16 [4, 4096, 4096], P('visit', 'sky'), may hold values from 0.5 to 8
- pixel_mask: int32 [4, 4096, 4096], P('visit', 'sky'), may hold values 0 or 1
- psf_kernel: bfloat16 [4, 2, 21], P('visit'), may hold values from 0.049804688 to 0.19921875
- block_owner: int32 [4, 32, 32], P('visit', 'sky'), may hold values from 0 to 31, as said below
- patch_index: int32 [4, 32, 32, 4], P('visit', 'sky'), may hold values from 0 to 31
- pair_stretch: bfloat16 [4, 32, 32, 4, 2], P('visit', 'sky'), may hold values from -0.019897461 to 0.019897461
- pair_offset: bfloat16 [4, 32, 32, 4, 2], P('visit', 'sky'), may hold values from -1.5 to 1.5
Outputs:
- coadd_image: float32 [1024, 128, 128], P(('visit', 'sky'))
Inputs may be any that keep to these rules, and one draw needn't show every extreme that they name: `block_owner`: among the 32 blocks of one device, at most 2 name the same owner; in every draw one owner is named by exactly 2 blocks of every device.
All inputs are finite; a program needn't handle non-finite values. No bound on the sum of `pixel_mask` on one device may be relied on, other than what follows from the above.
Results may differ from a plain program's by a relative error of at most 0.007.
Values may be sent and summed in bfloat16 or wider, within the bound.
No kernel may reach another device: no remote copies, remote signals or barrier semaphores. Data moves between devices by JAX's collectives and lax.ppermute only.
A program may use at most 128 MiB of HBM per device.

v0:
```python
import jax
import jax.numpy as jnp
from jax import lax
from jax.sharding import PartitionSpec as P

PB_DEV = 8


WINDOW = 3.0


def extended(cells, sides, width):
    for axis, dim in sides:
        count = lax.axis_size(axis)
        ends = count - 1
        head = lax.slice_in_dim(cells, 0, width, axis=dim)
        tail = lax.slice_in_dim(cells, cells.shape[dim] - width, cells.shape[dim], axis=dim)
        cells = jnp.concatenate(
            [
                lax.ppermute(tail, axis, [(i, (i + 1) % count) for i in range(ends)]),
                cells,
                lax.ppermute(head, axis, [((i + 1) % count, i) for i in range(ends)]),
            ],
            axis=dim,
        )
    return cells


def lanczos_maps(stretch, offset, block_side):
    pixels = jnp.arange(block_side).astype(jnp.float32)
    centre = (block_side - 1) / 2.0
    source = (
        (1.0 + stretch.astype(jnp.float32))[..., None] * (pixels - centre)
        + centre
        + offset.astype(jnp.float32)[..., None]
    )
    spread = source[..., :, None] - pixels
    inside = jnp.abs(spread) < WINDOW
    kernel = jnp.sinc(spread) * jnp.sinc(spread / WINDOW)
    return jnp.where(inside, kernel, jnp.zeros_like(kernel)).astype(jnp.bfloat16)


def warp_blocks(planes, maps):
    half_warp = jnp.einsum(
        "npij,ncjk->npcik", maps[:, :, 0], planes, preferred_element_type=jnp.float32
    ).astype(jnp.bfloat16)
    return jnp.einsum(
        "npcij,npkj->npcik", half_warp, maps[:, :, 1], preferred_element_type=jnp.float32
    ).astype(jnp.bfloat16)


def column_toeplitz(tap_values, block_side, kernel_half):
    lag_table = (
        jnp.arange(3 * block_side)[:, None]
        - jnp.arange(block_side)[None, :]
        - block_side
        + kernel_half
    )
    select = (lag_table[:, :, None] == jnp.arange(tap_values.shape[-1])).astype(jnp.float32)
    return jnp.einsum("wct,vt->vwc", select, tap_values.astype(jnp.float32)).astype(jnp.bfloat16)


def row_toeplitz(tap_values, block_side, kernel_half):
    lag_table = jnp.arange(block_side + 2 * kernel_half)[None, :] - jnp.arange(block_side)[:, None]
    select = (lag_table[:, :, None] == jnp.arange(tap_values.shape[-1])).astype(jnp.float32)
    return jnp.einsum("rpt,vt->vrp", select, tap_values.astype(jnp.float32)).astype(jnp.bfloat16)


def local(
    exposure, variance, pixel_mask, psf_kernel, block_owner, patch_index, pair_stretch, pair_offset
):
    visits, block_side, columns = exposure.shape
    kernel_half = (psf_kernel.shape[-1] - 1) // 2
    col_blocks = columns // block_side
    across = psf_kernel[:, 0]
    vertical = psf_kernel[:, 1]
    across_square = (across.astype(jnp.float32) ** 2).astype(jnp.bfloat16)
    down_square = (vertical.astype(jnp.float32) ** 2).astype(jnp.bfloat16)

    def row_pass(surface, tap_values):
        tile_view = surface.reshape(visits, block_side, col_blocks, block_side)
        empty_tile = jnp.zeros_like(tile_view[:, :, :1])
        before = jnp.concatenate([empty_tile, tile_view[:, :, :-1]], axis=2)
        following = jnp.concatenate([tile_view[:, :, 1:], empty_tile], axis=2)
        window = jnp.concatenate([before, tile_view, following], axis=3)
        result = jnp.einsum(
            "vrbw,vwc->vrbc",
            window,
            column_toeplitz(tap_values, block_side, kernel_half),
            preferred_element_type=jnp.float32,
        )
        return result.reshape(visits, block_side, columns).astype(jnp.bfloat16)

    passed = jnp.stack([row_pass(exposure, across), row_pass(variance, across_square)])
    framed = extended(passed, (("sky", 2),), kernel_half)
    toeplitz = jnp.stack(
        [
            row_toeplitz(vertical, block_side, kernel_half),
            row_toeplitz(down_square, block_side, kernel_half),
        ]
    )
    matched = jnp.einsum("avrp,avpx->avrx", toeplitz, framed, preferred_element_type=jnp.float32)
    weight = pixel_mask.astype(jnp.float32) / matched[1]
    planes = jnp.stack(
        [(weight * matched[0]).astype(jnp.bfloat16), weight.astype(jnp.bfloat16)], axis=1
    )
    planes = planes.reshape(visits, 2, block_side, col_blocks, block_side).transpose(0, 3, 1, 2, 4)
    planes = planes.reshape(visits * col_blocks, 2, block_side, block_side)
    owners_count = lax.axis_size("sky")
    block_count = planes.shape[0]
    capacity = 2 * block_count // owners_count
    slots_total = owners_count * capacity
    owner_index = block_owner.reshape(block_count)
    owner_hits = (owner_index[:, None] == jnp.arange(owners_count)[None, :]).astype(jnp.int32)
    slot_rank = jnp.sum((jnp.cumsum(owner_hits, axis=0) - 1) * owner_hits, axis=1)
    slot_index = owner_index * capacity + slot_rank
    claimed = slot_index[None, :] == jnp.arange(slots_total)[:, None]
    filled = jnp.any(claimed, axis=1)
    source_of = jnp.sum(claimed * jnp.arange(block_count)[None, :], axis=1)
    targets = patch_index.reshape(block_count, -1)
    pair_count = targets.shape[1]
    slot_targets = jnp.where(filled[:, None], targets[source_of], -1).astype(jnp.bfloat16)
    slot_targets = slot_targets.reshape(owners_count, capacity, pair_count)
    stretch = pair_stretch.reshape(block_count, pair_count, 2)
    offset = pair_offset.reshape(block_count, pair_count, 2)
    warped = warp_blocks(planes, lanczos_maps(stretch, offset, block_side))
    outgoing = (
        warped[source_of].reshape(owners_count, capacity, pair_count, 2, block_side, block_side),
        slot_targets,
    )
    arrived, arrived_aims = (
        lax.all_to_all(outgoing[0], "sky", split_axis=0, concat_axis=0, tiled=True),
        lax.all_to_all(outgoing[1], "sky", split_axis=0, concat_axis=0, tiled=True),
    )
    patch_own = PB_DEV * lax.axis_size("visit")
    flat_rows = arrived.reshape(-1, 2 * block_side * block_side)
    aim_list = arrived_aims.reshape(-1).astype(jnp.float32)
    routing = (aim_list[None, :] == jnp.arange(patch_own).astype(jnp.float32)[:, None]).astype(
        jnp.bfloat16
    )
    partial_value = jnp.dot(routing, flat_rows, preferred_element_type=jnp.float32).reshape(
        patch_own, 2, block_side, block_side
    )
    summed = lax.psum(partial_value, "visit")
    own_share = lax.dynamic_slice_in_dim(summed, lax.axis_index("visit") * PB_DEV, PB_DEV, 0)
    return own_share[:, 0] / jnp.maximum(own_share[:, 1], 1.0)


def solution(mesh):
    return jax.shard_map(
        local,
        mesh=mesh,
        in_specs=(
            P("visit", "sky", None),
            P("visit", "sky", None),
            P("visit", "sky", None),
            P("visit", None, None),
            P("visit", "sky", None),
            P("visit", "sky", None, None),
            P("visit", "sky", None, None, None),
            P("visit", "sky", None, None, None),
        ),
        out_specs=P(("visit", "sky"), None, None),
        check_vma=False,
    )
```

profile of v0, /device:TPU:0, one launch (start us, length us, event | category | flops | bytes accessed | tf_op | source)
XLA Modules:
  0.0 501.3 jit_solution(10047391523739954223)
XLA Ops:
  11.3 7.4 %all-to-all-start = ((bf16[32,2,4]{2,1,0:T(2,128)(2,1)}), bf16[32,2,4]{2,1,0:T(2,128)(2,1)S(1)}, u32[]{:S(2)}, u32[]{:S(2)}) async-start(bf16[32,2,4]{2,1,0:T(2,128)(2,1)} %select_convert_fusion), calls=%async_computation | async-start | bytes 32768 | tf_op jit(solution)/shard_map/all_to_all | solution.py:133
  19.3 1.7 fusion.58
  21.0 2.3 fusion.60
  24.9 1.6 copy.54
  27.7 1.4 fusion.98
  30.1 1.4 fusion.101
  32.1 2.2 collective-permute-start
  34.3 1.5 collective-permute-start.1
  36.0 4.4 fusion.104
  40.5 3.2 fusion.106
  43.9 4.0 copy.69
  47.9 4.0 copy.68
  52.2 43.7 %fusion.45 = bf16[32,4,2,128,128]{4,3,1,0,2:T(8,128)(2,1)} fusion(f32[128]{0:T(128)S(1)} %iota_convert_fusion, f32[32,4,2,128]{3,1,0,2:T(4,128)S(1)} %add_add_fusion), kind=kLoop, calls=%fused_computation.61 | loop fusion | flops 301989888 | bytes 8520192 | tf_op jit(solution)/shard_map/convert_element_type | solution.py:40
  95.9 1.8 fusion.84
  99.7 8.9 %fusion.49 = bf16[32,4,2,128,128]{4,3,2,1,0:T(8,128)(2,1)} fusion(bf16[32,4,2,128,128]{4,3,1,0,2:T(8,128)(2,1)} %fusion.45, bf16[1,1,128,32,128]{2,4,1,3,0:T(8,128)(2,1)S(1)} %bitcast.140, bf16[1,1,128,32,128]{2,4,1,3,0:T(8,128)(2,1)S(1)} %bitcast.139), kind=kOutput, calls=%fused_computation.65 | convolution fusion | flops 2160066560 | bytes 18874368 | tf_op jit(solution)/shard_map/npcij,npkj->npcik/dot_general | solution.py:47
  108.6 10.8 %gather_fusion.1 = bf16[64,4,2,128,128]{4,3,2,1,0:T(8,128)(2,1)} fusion(bf16[32,4,2,128,128]{4,3,2,1,0:T(8,128)(2,1)} %fusion.49, s32[1024]{0:T(1024)S(1)} %pad_clamp_fusion), kind=kCustom, calls=%fused_computation.1 | custom fusion | bytes 33554688 | tf_op jit(solution)/shard_map/gather | solution.py:128
  119.4 9.6 %all-to-all-start.1 = ((bf16[32,2,4,2,128,128]{5,4,3,2,1,0:T(8,128)(2,1)}), bf16[32,2,4,2,128,128]{5,4,3,2,1,0:T(8,128)(2,1)}, u32[]{:S(2)}, u32[]{:S(2)}) async-start(bf16[32,2,4,2,128,128]{5,4,3,2,1,0:T(8,128)(2,1)} %bitcast.137), calls=%async_computation.1 | async-start | bytes 33554432 | tf_op jit(solution)/shard_map/all_to_all | solution.py:132
  129.2 213.0 %all-to-all-done.1 = bf16[32,2,4,2,128,128]{5,4,3,2,1,0:T(8,128)(2,1)} async-done(((bf16[32,2,4,2,128,128]{5,4,3,2,1,0:T(8,128)(2,1)}), bf16[32,2,4,2,128,128]{5,4,3,2,1,0:T(8,128)(2,1)}, u32[]{:S(2)}, u32[]{:S(2)}) %all-to-all-start.1) | async-done | bytes 16777248 | tf_op jit(solution)/shard_map/all_to_all | solution.py:132
  342.2 25.3 %reshape.227 = bf16[256,32768]{1,0:T(8,128)(2,1)} reshape(bf16[32,2,4,2,128,128]{5,4,3,2,1,0:T(8,128)(2,1)} %all-to-all-done.1) | data formatting | bytes 33554432 | tf_op jit(solution)/shard_map/reshape | solution.py:136
  367.6 22.4 %copy.65 = bf16[256,32768]{0,1:T(8,128)(2,1)} copy(bf16[256,32768]{1,0:T(8,128)(2,1)} %reshape.227) | data formatting | bytes 33554432 | tf_op jit(solution)/shard_map/reshape | solution.py:136
  389.9 11.2 %fusion.117 = f32[32,2,128,128]{3,0,2,1:T(8,128)} fusion(bf16[2,128,128,256]{3,2,1,0:T(8,128)(2,1)} %bitcast.138, f32[256]{0:T(256)S(1)} %reshape.228, f32[32]{0:T(128)S(1)} %iota_convert_fusion.1), kind=kOutput, calls=%fused_computation.141 | convolution fusion | flops 536879104 | bytes 20972672 | tf_op jit(solution)/shard_map/dot_general | solution.py:141
  401.2 91.1 %all-reduce.6.cloned.1.call-done = f32[32,2,128,128]{3,0,2,1:T(8,128)} async-done(((f32[32,2,128,128]{3,0,2,1:T(8,128)}), f32[32,2,128,128]{3,0,2,1:T(8,128)}) %all-reduce.6.cloned.1.call-update) | async-done | bytes 4194320 | tf_op jit(solution)/shard_map/psum | solution.py:144
  492.3 1.3 fusion.108
  493.6 0.9 copy.66
  (54 shorter events, 12.4 us)
Async XLA Ops:
  6.5 17.0 %copy-start.1 = (bf16[1,128,4096]{2,1,0:T(8,128)(2,1)S(1)}, bf16[1,128,4096]{2,1,0:T(8,128)(2,1)}, u32[]{:S(2)}) copy-start(bf16[1,128,4096]{2,1,0:T(8,128)(2,1)} %param.9) | copy-start | bytes 3145732
  11.3 108.1 %all-to-all-start = ((bf16[32,2,4]{2,1,0:T(2,128)(2,1)}), bf16[32,2,4]{2,1,0:T(2,128)(2,1)S(1)}, u32[]{:S(2)}, u32[]{:S(2)}) async-start(bf16[32,2,4]{2,1,0:T(2,128)(2,1)} %select_convert_fusion), calls=%async_computation | async-start | bytes 32768 | tf_op jit(solution)/shard_map/all_to_all | solution.py:133
  30.1 5.9 %copy-start.2 = (bf16[1,2,21]{2,1,0:T(2,128)(2,1)S(1)}, bf16[1,2,21]{2,1,0:T(2,128)(2,1)}, u32[]{:S(2)}) copy-start(bf16[1,2,21]{2,1,0:T(2,128)(2,1)} %param.12) | copy-start | bytes 256
  31.5 12.2 %copy-start.3 = (bf16[1,1,32,4,2]{2,4,3,1,0:T(2,128)(2,1)S(1)}, bf16[1,1,32,4,2]{2,4,3,1,0:T(2,128)(2,1)}, u32[]{:S(2)}) copy-start(bf16[1,1,32,4,2]{2,4,3,1,0:T(2,128)(2,1)} %param.15) | copy-start | bytes 1540
  31.5 12.2 %copy-start.4 = (bf16[1,1,32,4,2]{2,4,3,1,0:T(2,128)(2,1)S(1)}, bf16[1,1,32,4,2]{2,4,3,1,0:T(2,128)(2,1)}, u32[]{:S(2)}) copy-start(bf16[1,1,32,4,2]{2,4,3,1,0:T(2,128)(2,1)} %param.16) | copy-start | bytes 1540
  32.1 63.8 %collective-permute-start = (bf16[2,1,10,4096]{3,2,0,1:T(8,128)(2,1)S(1)}, bf16[2,1,10,4096]{3,2,0,1:T(8,128)(2,1)S(1)}, u32[]{:S(2)}, u32[]{:S(2)}) collective-permute-start(bf16[2,1,10,4096]{3,2,0,1:T(8,128)(2,1)S(1)} %get-tuple-element.8), channel_id=1, source_target_pairs={{0,1},{1,2},{2,3},{3,4},{4,5},{5,6},{6,7},{7,8},{8,9},{9,10},{10,1... | collective-permute-start | bytes 491528 | tf_op jit(solution)/shard_map/ppermute | solution.py:20
  34.3 61.6 %collective-permute-start.1 = (bf16[2,1,10,4096]{3,2,0,1:T(8,128)(2,1)S(1)}, bf16[2,1,10,4096]{3,2,0,1:T(8,128)(2,1)}, u32[]{:S(2)}, u32[]{:S(2)}) collective-permute-start(bf16[2,1,10,4096]{3,2,0,1:T(8,128)(2,1)S(1)} %get-tuple-element.9), channel_id=1, source_target_pairs={{1,0},{2,1},{3,2},{4,3},{5,4},{6,5},{7,6},{8,7},{9,8},{10,9},{11,1... | collective-permute-start | bytes 491528 | tf_op jit(solution)/shard_map/ppermute | solution.py:22
  52.2 45.6 %copy-start = (s32[1,128,4096]{2,1,0:T(8,128)S(1)}, s32[1,128,4096]{2,1,0:T(8,128)}, u32[]{:S(2)}) copy-start(s32[1,128,4096]{2,1,0:T(8,128)} %param.11) | copy-start | bytes 6291460
  119.4 222.8 %all-to-all-start.1 = ((bf16[32,2,4,2,128,128]{5,4,3,2,1,0:T(8,128)(2,1)}), bf16[32,2,4,2,128,128]{5,4,3,2,1,0:T(8,128)(2,1)}, u32[]{:S(2)}, u32[]{:S(2)}) async-start(bf16[32,2,4,2,128,128]{5,4,3,2,1,0:T(8,128)(2,1)} %bitcast.137), calls=%async_computation.1 | async-start | bytes 33554432 | tf_op jit(solution)/shard_map/all_to_all | solution.py:132
  129.0 363.3 %all-reduce.6.cloned.1.call-start = ((), (), s32[]{:S(2)}) async-start(), calls=%async_computation.2 | async-start | bytes 8388608 | tf_op jit(solution)/shard_map/psum | solution.py:144
Sparse Core Ops, SparseCore 0:
  401.3 90.9 all-reduce.5
where the time goes:
time: 504 us; the launch traced here: 501 us
  waiting for transfers between devices  304 us (60%)
  local copies, waits for them, and re-layouts  76.5 us (15%)
  other arithmetic  50 us (10%)
  matrix products  36.2 us (7%)
  starting transfers between devices  20.7 us (4%)
  between operations  13.7 us (3%)
    all_to_all x1, waiting for transfers between devices, local(): lax.all_to_all(outgoing[0], 'sky', split_axis=0, concat_axis=0, tiled=True)  213 us
    psum x1, waiting for transfers between devices, local(): summed = lax.psum(partial_value, 'visit')  91.1 us
    reshape x2, local copies, waits for them, and re-layouts, local(): flat_rows = arrived.reshape(-1, 2 * block_side * block_side)  47.7 us
    convert_element_type x1, other arithmetic, lanczos_maps(): jnp.where(inside, kernel, jnp.zeros_like(kernel)).astype(jnp.bfloat16)  43.7 us
    dot_general x1, matrix products, local(): jnp.dot(routing, flat_rows, preferred_element_type=jnp.float32)  11.2 us
    gather x1, local copies, waits for them, and re-layouts, local(): warped[source_of]  10.8 us
  transfers between devices with their start and end apart: 5, of which 2 were waited for; matrix products, arithmetic and copies ran while one was open for 19% of the time, Pallas kernels for 0%

commit v1 on v0

v1 whole, which is shorter than its diff:
```python
import functools
import math

import jax
import jax.numpy as jnp
from jax import lax
from jax.experimental import pallas as pl
from jax.experimental.pallas import tpu as pltpu
from jax.sharding import PartitionSpec as P

BS = 128
HALO = 16
MARGIN = 16
CAP = 2
PB_DEV = 8
PER_STEP = 4
CUTS = (0, 64, 128)
VMEM = 48 * 1024 * 1024


def spans(cuts):
    result = []
    for part in range(len(cuts) - 1):
        first, last = part == 0, part == len(cuts) - 2
        out_from = 0 if first else cuts[part] - MARGIN
        out_to = cuts[-1] if last else cuts[part + 1] - MARGIN
        read_from = 0 if first else out_from - MARGIN
        result.append((cuts[part], cuts[part + 1], read_from, out_from, out_to))
    return result


def band(rows, columns, shift, taps_ref, which, square):
    lag = (
        lax.broadcasted_iota(jnp.int32, (rows, columns), 0)
        - lax.broadcasted_iota(jnp.int32, (rows, columns), 1)
        + shift
    )
    matrix = jnp.zeros((rows, columns), jnp.float32)
    for tap in range(taps_ref.shape[1]):
        value = taps_ref[which, tap]
        matrix = jnp.where(lag == tap, value * value if square else value, matrix)
    return matrix.astype(jnp.bfloat16)


def filter_kernel(cuts, slot_ref, taps_ref, exp_ref, var_ref, mask_ref, top_ref, bottom_ref, *rest):
    outs, framed, across_ref, down_ref = rest[:-3], rest[-3], rest[-2], rest[-1]
    rows, columns = exp_ref.shape
    half = (taps_ref.shape[1] - 1) // 2
    side = jnp.zeros((rows + 2 * HALO, BS), jnp.bfloat16)
    for plane, ref in enumerate((exp_ref, var_ref)):
        framed[plane, :, :BS] = side
        framed[plane, :, BS + columns :] = side
        framed[plane, :HALO, BS : BS + columns] = top_ref[plane]
        framed[plane, HALO : HALO + rows, BS : BS + columns] = ref[...]
        framed[plane, HALO + rows :, BS : BS + columns] = bottom_ref[plane]
        square = plane == 1
        across_ref[plane] = band(4 * BS, 2 * BS, half - BS, taps_ref, 0, square)
        lag = (
            lax.broadcasted_iota(jnp.int32, (rows, rows + 2 * HALO), 1)
            - lax.broadcasted_iota(jnp.int32, (rows, rows + 2 * HALO), 0)
            + half
            - HALO
        )
        matrix = jnp.zeros(lag.shape, jnp.float32)
        for tap in range(taps_ref.shape[1]):
            value = taps_ref[1, tap]
            matrix = jnp.where(lag == tap, value * value if square else value, matrix)
        down_ref[plane] = matrix.astype(jnp.bfloat16)

    @pl.loop(0, columns // (2 * BS))
    def _(tile):
        start = pl.multiple_of(tile * 2 * BS, 2 * BS)
        matched = []
        for plane in range(2):
            passed = jnp.dot(
                framed[plane, :, pl.ds(start, 4 * BS)],
                across_ref[plane],
                preferred_element_type=jnp.float32,
            ).astype(jnp.bfloat16)
            matched.append(jnp.dot(down_ref[plane], passed, preferred_element_type=jnp.float32))
        weight = mask_ref[:, pl.ds(start, 2 * BS)].astype(jnp.float32) / matched[1]
        weighted = (weight * matched[0]).astype(jnp.bfloat16)
        weight = weight.astype(jnp.bfloat16)
        for block in range(2):
            slot = slot_ref[tile * 2 + block]
            lanes = slice(block * BS, (block + 1) * BS)
            for out, lo, hi in zip(outs, cuts[:-1], cuts[1:]):
                out[slot, 0] = weighted[lo:hi, lanes]
                out[slot, 1] = weight[lo:hi, lanes]


def sine_cosine(angle):
    square = angle * angle
    sine = jnp.zeros_like(angle)
    cosine = jnp.zeros_like(angle)
    for term in range(8, -1, -1):
        sine = sine * square + (-1.0) ** term / math.factorial(2 * term + 1)
        cosine = cosine * square + (-1.0) ** term / math.factorial(2 * term)
    return sine * angle, cosine, sine


def map_kernel(shapes, stretch_ref, offset_ref, column_ref, *rest):
    outs, near_ref, taps = rest[:-2], rest[-2], rest[-1]
    step_slots = column_ref.shape[0]
    pixels = lax.broadcasted_iota(jnp.int32, (step_slots * 8, BS), 1).astype(jnp.float32)
    centre = (BS - 1) / 2.0
    source = (1.0 + stretch_ref[...]) * (pixels - centre) + centre + offset_ref[...]
    near = jnp.round(source)
    fraction = source - near
    near_ref[...] = near
    whole, _, whole_sinc = sine_cosine(math.pi * fraction)
    third, third_cos, third_sinc = sine_cosine((math.pi / 3.0) * fraction)
    for k in range(-3, 4):
        if k == 0:
            value = whole_sinc * third_sinc
        else:
            x = fraction - k
            sign = -1.0 if k % 2 else 1.0
            angle = math.pi * k / 3.0
            slow = third * math.cos(angle) - third_cos * math.sin(angle)
            value = (sign * 3.0 / math.pi**2) * whole * slow / (x * x)
            value = jnp.where(jnp.abs(x) < 3.0, value, 0.0)
        taps[k + 3] = value
    rows = lax.broadcasted_iota(jnp.int32, (BS, BS), 0).astype(jnp.float32)

    @pl.loop(0, step_slots)
    def _(slot):
        base = pl.multiple_of(slot * 8, 8)
        near_slot = near_ref[pl.ds(base, 8), :]
        taps_slot = [taps[k, pl.ds(base, 8), :] for k in range(7)]
        for pair in range(4):
            for direction in range(2):
                row = pair * 2 + direction
                lag = rows - near_slot[row : row + 1, :]
                matrix = jnp.zeros((BS, BS), jnp.float32)
                for k in range(7):
                    matrix = jnp.where(lag == float(k - 3), taps_slot[k][row : row + 1, :], matrix)
                if direction == 1:
                    column_ref[slot, :, pair * BS : (pair + 1) * BS] = matrix.astype(jnp.bfloat16)
                else:
                    turned = matrix.T.astype(jnp.bfloat16)
                    for out, (_, to, read_from, out_from, out_to) in zip(outs, shapes):
                        piece = turned[out_from:out_to, :]
                        if read_from:
                            piece = matrix[read_from:, :].T[out_from:out_to, :].astype(jnp.bfloat16)
                        out[slot, pair, :, : to - read_from] = piece[:, : to - read_from]


def warp_kernel(span, before, aim_ref, *refs):
    cut_from, cut_to, read_from, out_from, out_to = span
    count = len(before) + 1
    blocks, column_ref, row_ref = refs[:count], refs[count], refs[count + 1]
    outs, total = refs[count + 2 : -1], refs[-1]
    step = pl.program_id(0)

    @pl.when(step == 0)
    def _():
        total[...] = jnp.zeros_like(total)

    depth = cut_to - read_from
    for slot in range(PER_STEP):
        pieces = [ref[slot] for ref in blocks]
        planes = jnp.concatenate(
            [piece[plane] for plane in range(2) for piece in pieces], axis=0
        )
        half_warp = jnp.dot(planes, column_ref[slot], preferred_element_type=jnp.float32).astype(
            jnp.bfloat16
        )
        for pair in range(4):
            lanes = slice(pair * BS, (pair + 1) * BS)
            both = jnp.concatenate([half_warp[:depth, lanes], half_warp[depth:, lanes]], axis=1)
            aim = aim_ref[(step * PER_STEP + slot) * 4 + pair]
            total[aim] += jnp.dot(
                row_ref[slot, pair, :, :depth], both, preferred_element_type=jnp.float32
            )

    @pl.when(step == pl.num_programs(0) - 1)
    def _():
        for index, out in enumerate(outs):
            out[...] = total[index * PB_DEV : (index + 1) * PB_DEV].astype(out.dtype)


def local(
    exposure, variance, pixel_mask, psf_kernel, block_owner, patch_index, pair_stretch, pair_offset
):
    shapes = spans(CUTS)
    _, rows, columns = exposure.shape
    block_count = columns // BS
    owners = lax.axis_size("sky")
    groups = lax.axis_size("visit")
    slots = owners * CAP
    pairs = patch_index.shape[-1]
    params = pltpu.CompilerParams(vmem_limit_bytes=VMEM)
    smem = pl.BlockSpec(memory_space=pltpu.SMEM)
    vmem = pl.BlockSpec(memory_space=pltpu.VMEM)

    low = jnp.concatenate([exposure[:, rows - HALO :], variance[:, rows - HALO :]], axis=0)
    high = jnp.concatenate([exposure[:, :HALO], variance[:, :HALO]], axis=0)
    top = lax.ppermute(low, "sky", [(i, i + 1) for i in range(owners - 1)])
    bottom = lax.ppermute(high, "sky", [(i + 1, i) for i in range(owners - 1)])

    owner = block_owner.reshape(block_count)
    order = jnp.arange(block_count)
    rank = jnp.sum((owner[:, None] == owner[None, :]) & (order[None, :] < order[:, None]), axis=1)
    slot = (owner * CAP + rank).astype(jnp.int32)
    claimed = (slot[None, :] == jnp.arange(slots)[:, None]).astype(jnp.bfloat16)
    facts = jnp.concatenate(
        [
            pair_stretch.reshape(block_count, 2 * pairs),
            pair_offset.reshape(block_count, 2 * pairs),
            patch_index.reshape(block_count, pairs).astype(jnp.bfloat16),
            jnp.ones((block_count, 1), jnp.bfloat16),
        ],
        axis=1,
    )
    table = jnp.dot(claimed, facts, preferred_element_type=jnp.float32).astype(jnp.bfloat16)

    planes = pl.pallas_call(
        functools.partial(filter_kernel, CUTS),
        out_shape=[
            jax.ShapeDtypeStruct((slots, 2, hi - lo, BS), jnp.bfloat16)
            for lo, hi in zip(CUTS[:-1], CUTS[1:])
        ],
        in_specs=[smem, smem] + [vmem] * 5,
        out_specs=[vmem] * len(shapes),
        scratch_shapes=[
            pltpu.VMEM((2, rows + 2 * HALO, columns + 2 * BS), jnp.bfloat16),
            pltpu.VMEM((2, 4 * BS, 2 * BS), jnp.bfloat16),
            pltpu.VMEM((2, rows, rows + 2 * HALO), jnp.bfloat16),
        ],
        compiler_params=params,
        name="filter",
    )(
        slot,
        psf_kernel.reshape(2, -1).astype(jnp.float32),
        exposure.reshape(rows, columns),
        variance.reshape(rows, columns),
        pixel_mask.reshape(rows, columns),
        top,
        bottom,
    )

    def exchange(array):
        return lax.all_to_all(array, "sky", split_axis=0, concat_axis=0, tiled=True)

    arrived = [exchange(part) for part in planes]
    known = exchange(table).astype(jnp.float32)

    map_slots = 16
    maps = pl.pallas_call(
        functools.partial(map_kernel, shapes),
        grid=(slots // map_slots,),
        out_shape=[jax.ShapeDtypeStruct((slots, BS, pairs * BS), jnp.bfloat16)]
        + [
            jax.ShapeDtypeStruct((slots, pairs, out_to - out_from, BS), jnp.bfloat16)
            for _, _, _, out_from, out_to in shapes
        ],
        in_specs=[pl.BlockSpec((map_slots * 2 * pairs, 1), lambda i: (i, 0))] * 2,
        out_specs=[pl.BlockSpec((map_slots, BS, pairs * BS), lambda i: (i, 0, 0))]
        + [
            pl.BlockSpec((map_slots, pairs, out_to - out_from, BS), lambda i: (i, 0, 0, 0))
            for _, _, _, out_from, out_to in shapes
        ],
        scratch_shapes=[
            pltpu.VMEM((map_slots * 2 * pairs, BS), jnp.float32),
            pltpu.VMEM((7, map_slots * 2 * pairs, BS), jnp.float32),
        ],
        compiler_params=params,
        name="maps",
    )(
        known[:, : 2 * pairs].reshape(slots * 2 * pairs, 1),
        known[:, 2 * pairs : 4 * pairs].reshape(slots * 2 * pairs, 1),
    )
    column_maps, row_maps = maps[0], maps[1:]

    patch = known[:, 4 * pairs : 5 * pairs].astype(jnp.int32)
    distance = (patch // PB_DEV - lax.axis_index("visit")) % groups
    aims = jnp.where(
        known[:, 5 * pairs :] > 0.5, distance * PB_DEV + patch % PB_DEV, groups * PB_DEV
    )
    aims = aims.reshape(slots * pairs)

    results = []
    for part, span in enumerate(shapes):
        cut_from, cut_to, read_from, out_from, out_to = span
        before = [arrived[part - 1]] if part else []
        height = out_to - out_from
        specs = []
        if part:
            reach = cut_from - read_from
            last = (cut_from - shapes[part - 1][0]) // reach - 1
            specs.append(
                pl.BlockSpec((PER_STEP, 2, reach, BS), functools.partial(lambda q, i, _: (i, 0, q, 0), last))
            )
        specs.append(pl.BlockSpec((PER_STEP, 2, cut_to - cut_from, BS), lambda i, _: (i, 0, 0, 0)))
        specs.append(pl.BlockSpec((PER_STEP, BS, pairs * BS), lambda i, _: (i, 0, 0)))
        specs.append(pl.BlockSpec((PER_STEP, pairs, height, BS), lambda i, _: (i, 0, 0, 0)))
        sums = pl.pallas_call(
            functools.partial(warp_kernel, span, before),
            grid_spec=pltpu.PrefetchScalarGridSpec(
                num_scalar_prefetch=1,
                grid=(slots // PER_STEP,),
                in_specs=specs,
                out_specs=[pl.BlockSpec((PB_DEV, height, 2 * BS), lambda i, _: (0, 0, 0))] * groups,
                scratch_shapes=[pltpu.VMEM((groups * PB_DEV + 1, height, 2 * BS), jnp.float32)],
            ),
            out_shape=[
                jax.ShapeDtypeStruct(
                    (PB_DEV, height, 2 * BS), jnp.float32 if index == 0 else jnp.bfloat16
                )
                for index in range(groups)
            ],
            compiler_params=params,
            name="warp",
        )(aims, *before, arrived[part], column_maps, row_maps[part])
        whole = sums[0]
        for step in range(1, groups):
            whole = whole + lax.ppermute(
                sums[step], "visit", [(i, (i + step) % groups) for i in range(groups)]
            ).astype(jnp.float32)
        results.append(whole[:, :, :BS] / jnp.maximum(whole[:, :, BS:], 1.0))
    return jnp.concatenate(results, axis=1)


def solution(mesh):
    return jax.shard_map(
        local,
        mesh=mesh,
        in_specs=(
            P("visit", "sky", None),
            P("visit", "sky", None),
            P("visit", "sky", None),
            P("visit", None, None),
            P("visit", "sky", None),
            P("visit", "sky", None, None),
            P("visit", "sky", None, None, None),
            P("visit", "sky", None, None, None),
        ),
        out_specs=P(("visit", "sky"), None, None),
        check_vma=False,
    )
```

time: 504 us -> 165 us (0.33)
  waiting for transfers between devices: 304 us -> 12.9 us
  Pallas kernels: 0 us -> 77.4 us
  local copies, waits for them, and re-layouts: 76.5 us -> 5.48 us
  other arithmetic: 50 us -> 2.64 us
  matrix products: 36.2 us -> 0.18 us
  blocking collectives: 0 us -> 35.9 us
  between operations: 13.7 us -> 0.24 us
  starting transfers between devices: 20.7 us -> 29.5 us
    all_to_all x2, waiting for transfers between devices: 213 us -> 0.01 us  [exchange(): return lax.all_to_all(array, 'sky', split_axis=0, concat_axis=0, tiled=True)]
    psum x1 -> x0, waiting for transfers between devices: 91.1 us -> none  [local(): summed = lax.psum(partial_value, 'visit')]
    pallas_call x0 -> x4, Pallas kernels: none -> 77.4 us  [the longest x2 37.6 us: local(): pl.pallas_call(functools.partial(warp_kernel, span, before), grid_spec=pl...]
    reshape x5 -> x3, local copies, waits for them, and re-layouts: 49.8 us -> 0.35 us  [the longest x1 0.12 us: local(): known[:, 2 * pairs:4 * pairs].reshape(slots * 2 * pairs, 1)]
    convert_element_type x7 -> x3, other arithmetic: 45.8 us -> 0.01 us  [the longest x1 0.01 us: local(): known = exchange(table).astype(jnp.float32)]
    dot_general x9 -> x1, matrix products: 36.2 us -> 0.18 us  [local(): jnp.dot(claimed, facts, preferred_element_type=jnp.float32)]
    all_to_all x0 -> x1, blocking collectives: none -> 35.9 us  [exchange(): return lax.all_to_all(array, 'sky', split_axis=0, concat_axis=0, tiled=True)]
    ppermute x2 -> x8, waiting for transfers between devices: 0.01 us -> 12.9 us  [the longest x6 12.9 us: local(): lax.ppermute(sums[step], 'visit', [(i, (i + step) % groups) for i in rang...]
  transfers between devices with their start and end apart: 5 -> 10, of which waited for: 2 -> 2; matrix products, arithmetic and copies ran while one was open for 19% -> 2% of each run, Pallas kernels for 0% -> 47%
where the time goes in v1:
time: 165 us; the launch traced here: 164 us
  Pallas kernels  77.4 us (47%)
  blocking collectives  35.9 us (22%)
  starting transfers between devices  29.5 us (18%)
  waiting for transfers between devices  12.9 us (8%)
  local copies, waits for them, and re-layouts  5.48 us (3%)
  other arithmetic  2.64 us (2%)
    pallas_call x2, Pallas kernels, local(): pl.pallas_call(functools.partial(warp_kernel, span, before), grid_spec=pl...  37.6 us
    all_to_all x1, blocking collectives, exchange(): return lax.all_to_all(array, 'sky', split_axis=0, concat_axis=0, tiled=True)  35.9 us
    pallas_call x1, Pallas kernels, local(): pl.pallas_call(functools.partial(map_kernel, shapes), grid=(slots // map_...  25.6 us
    all_to_all x2, starting transfers between devices, exchange(): return lax.all_to_all(array, 'sky', split_axis=0, concat_axis=0, tiled=True)  14.7 us
    pallas_call x1, Pallas kernels, local(): pl.pallas_call(functools.partial(filter_kernel, CUTS), out_shape=[jax.Sha...  14.1 us
    ppermute x6, waiting for transfers between devices, local(): lax.ppermute(sums[step], 'visit', [(i, (i + step) % groups) for i in rang...  12.9 us
    ppermute x6, starting transfers between devices, local(): lax.ppermute(sums[step], 'visit', [(i, (i + step) % groups) for i in rang...  10.4 us
  transfers between devices with their start and end apart: 10, of which 2 were waited for; matrix products, arithmetic and copies ran while one was open for 2% of the time, Pallas kernels for 47%

profile of v1, /device:TPU:0, one launch (start us, length us, event | category | flops | bytes accessed | tf_op | source)
XLA Modules:
  0.0 164.2 jit_solution(7579521564263779162)
XLA Ops:
  0.0 1.3 fusion.19
  1.3 1.3 collective-permute-start.1
  2.7 3.0 %collective-permute-start = (bf16[2,16,4096]{2,1,0:T(8,128)(2,1)S(1)}, bf16[2,16,4096]{2,1,0:T(8,128)(2,1)S(1)}, u32[]{:S(2)}, u32[]{:S(2)}) collective-permute-start(bf16[2,16,4096]{2,1,0:T(8,128)(2,1)S(1)} %pad_maximum_fusion.1), channel_id=1, source_target_pairs={{0,1},{1,2},{2,3},{3,4},{4,5},{5,6},{6,7},{7,8},{8,9},{9,10},{10,1... | collective-permute-start | bytes 786440 | tf_op jit(solution)/shard_map/ppermute | solution.py:199
  6.0 0.2 convolution_convert_fusion
  6.2 0.7 copy.17
  6.9 9.9 %all-to-all-start = ((bf16[32,2,21]{2,1,0:T(2,128)(2,1)}), bf16[32,2,21]{2,1,0:T(2,128)(2,1)S(1)}, u32[]{:S(2)}, u32[]{:S(2)}) async-start(bf16[32,2,21]{2,1,0:T(2,128)(2,1)} %bitcast.4), calls=%async_computation | async-start | bytes 32768 | tf_op jit(solution)/shard_map/all_to_all | solution.py:244
  16.9 14.1 %filter.1 = (bf16[64,2,64,128]{3,2,1,0:T(8,128)(2,1)S(1)}, bf16[64,2,64,128]{3,2,1,0:T(8,128)(2,1)}) custom-call(s32[32]{0:T(128)S(1)} %multiply_add_fusion.slot_ref, f32[2,21]{1,0:T(2,128)S(1)} %bitcast_convert_fusion.taps_ref, bf16[128,4096]{1,0:T(8,128)(2,1)S(1)} %bitcast.16, bf16[128,4096]{1,0:T(8,128)(2,1)S(1)} %bitcast.17, s32[128,4096]{1,0:T(8,128)} %bitcast.18, ...), custom_call_target="tpu_custom_call" | custom-call | tf_op jit(solution)/shard_map/filter/pallas_call | solution.py:218
  31.1 1.3 copy-done.1
  32.4 35.9 %all_to_all.19.refs_0_ = bf16[64,2,64,128]{3,2,1,0:T(8,128)(2,1)S(1)} all-to-all(bf16[64,2,64,128]{3,2,1,0:T(8,128)(2,1)} %copy-done.1), channel_id=1, replica_groups=mesh['visit'=4,'sky'=32] {'sky'}, dimensions={0} | all-to-all | bytes 4194304 | tf_op jit(solution)/shard_map/all_to_all | solution.py:244
  68.4 4.8 %all-to-all-start.2 = ((bf16[64,2,64,128]{3,2,1,0:T(8,128)(2,1)}), bf16[64,2,64,128]{3,2,1,0:T(8,128)(2,1)}, u32[]{:S(2)}, u32[]{:S(2)}) async-start(bf16[64,2,64,128]{3,2,1,0:T(8,128)(2,1)} %get-tuple-element.25), calls=%async_computation.2 | async-start | bytes 4194304 | tf_op jit(solution)/shard_map/all_to_all | solution.py:244
  73.9 25.6 %maps.1 = (bf16[64,128,512]{2,1,0:T(8,128)(2,1)}, bf16[64,4,48,128]{3,2,1,0:T(8,128)(2,1)S(1)}, bf16[64,4,80,128]{3,2,1,0:T(8,128)(2,1)}) custom-call(f32[512,1]{1,0:T(8,128)S(1)} %reshape.57.stretch_ref, f32[512,1]{1,0:T(8,128)S(1)} %reshape.58.offset_ref), custom_call_target="tpu_custom_call" | custom-call | tf_op jit(solution)/shard_map/maps/pallas_call | solution.py:250
  99.5 1.6 copy-done
  101.1 17.8 %warp.2 = (f32[8,48,256]{2,1,0:T(8,128)S(1)}, bf16[8,48,256]{2,1,0:T(8,128)(2,1)S(1)}, bf16[8,48,256]{2,1,0:T(8,128)(2,1)S(1)}, bf16[8,48,256]{2,1,0:T(8,128)(2,1)S(1)}) custom-call(s32[256]{0:T(256)S(1)} %reshape.49.aim_ref, bf16[64,2,64,128]{3,2,1,0:T(8,128)(2,1)S(1)} %all_to_all.19.refs_0_, bf16[64,128,512]{2,1,0:T(8,128)(2,1)} %get-tuple-element.19.refs_1_.refs_2_, ...), custom_call_target="tpu_custom_call" | custom-call | tf_op jit(solution)/shard_map/warp/pallas_call | solution.py:298
  118.9 2.0 %collective-permute-start.2 = (bf16[8,48,256]{2,1,0:T(8,128)(2,1)S(1)}, bf16[8,48,256]{2,1,0:T(8,128)(2,1)S(1)}, u32[]{:S(2)}, u32[]{:S(2)}) collective-permute-start(bf16[8,48,256]{2,1,0:T(8,128)(2,1)S(1)} %get-tuple-element.22), channel_id=1, source_target_pairs={{0,32},{32,64},{64,96},{96,0},{1,33},{33,65},{65,97},{97,1},{2,34}... | collective-permute-start | bytes 589832 | tf_op jit(solution)/shard_map/ppermute | solution.py:318
  120.9 3.6 %collective-permute-start.3 = (bf16[8,48,256]{2,1,0:T(8,128)(2,1)S(1)}, bf16[8,48,256]{2,1,0:T(8,128)(2,1)S(1)}, u32[]{:S(2)}, u32[]{:S(2)}) collective-permute-start(bf16[8,48,256]{2,1,0:T(8,128)(2,1)S(1)} %get-tuple-element.23), channel_id=1, source_target_pairs={{0,64},{32,96},{64,0},{96,32},{1,65},{33,97},{65,1},{97,33},{2,66}... | collective-permute-start | bytes 589832 | tf_op jit(solution)/shard_map/ppermute | solution.py:318
  124.5 1.0 collective-permute-start.4
  125.5 19.8 %warp.3 = (f32[8,80,256]{2,1,0:T(8,128)S(1)}, bf16[8,80,256]{2,1,0:T(8,128)(2,1)S(1)}, bf16[8,80,256]{2,1,0:T(8,128)(2,1)S(1)}, bf16[8,80,256]{2,1,0:T(8,128)(2,1)S(1)}) custom-call(s32[256]{0:T(256)S(1)} %reshape.49.aim_ref, bf16[64,2,64,128]{3,2,1,0:T(8,128)(2,1)S(1)} %all_to_all.19.refs_0_, bf16[64,2,64,128]{3,2,1,0:T(8,128)(2,1)} %all-to-all-done.2.refs_1_, ...), custom_call_target="tpu_custom_call" | custom-call | tf_op jit(solution)/shard_map/warp/pallas_call | solution.py:298
  145.4 1.1 collective-permute-start.5
  146.5 0.5 collective-permute-start.6
  146.9 2.3 %collective-permute-start.7 = (bf16[8,80,256]{2,1,0:T(8,128)(2,1)S(1)}, bf16[8,80,256]{2,1,0:T(8,128)(2,1)S(1)}, u32[]{:S(2)}, u32[]{:S(2)}) collective-permute-start(bf16[8,80,256]{2,1,0:T(8,128)(2,1)S(1)} %get-tuple-element.30), channel_id=1, source_target_pairs={{0,96},{32,0},{64,32},{96,64},{1,97},{33,1},{65,33},{97,65},{2,98}... | collective-permute-start | bytes 983048 | tf_op jit(solution)/shard_map/ppermute | solution.py:318
  149.2 1.0 convert_add_fusion.1
  150.3 12.2 %collective-permute-done.5 = bf16[8,80,256]{2,1,0:T(8,128)(2,1)S(1)} collective-permute-done((bf16[8,80,256]{2,1,0:T(8,128)(2,1)S(1)}, bf16[8,80,256]{2,1,0:T(8,128)(2,1)S(1)}, u32[]{:S(2)}, u32[]{:S(2)}) %collective-permute-start.5) | collective-permute-done | bytes 327712 | tf_op jit(solution)/shard_map/ppermute | solution.py:318
  162.5 0.6 collective-permute-done.7
  163.4 0.8 pad_maximum_fusion
  (41 shorter events, 1.3 us)
Async XLA Ops:
  0.0 16.9 %copy-start.2 = (bf16[1,128,4096]{2,1,0:T(8,128)(2,1)S(1)}, bf16[1,128,4096]{2,1,0:T(8,128)(2,1)}, u32[]{:S(2)}) copy-start(bf16[1,128,4096]{2,1,0:T(8,128)(2,1)} %param.8) | copy-start | bytes 3145732
  0.0 16.9 %copy-start.3 = (bf16[1,128,4096]{2,1,0:T(8,128)(2,1)S(1)}, bf16[1,128,4096]{2,1,0:T(8,128)(2,1)}, u32[]{:S(2)}) copy-start(bf16[1,128,4096]{2,1,0:T(8,128)(2,1)} %param.9) | copy-start | bytes 3145732
  0.0 5.7 %copy-start.7 = (s32[1,1,32]{2,1,0:T(1,128)S(1)}, s32[1,1,32]{2,1,0:T(1,128)}, u32[]{:S(2)}) copy-start(s32[1,1,32]{2,1,0:T(1,128)} %param.12) | copy-start | bytes 388
  0.0 5.9 %copy-start.4 = (s32[1,1,32,4]{2,3,1,0:T(4,128)S(1)}, s32[1,1,32,4]{2,3,1,0:T(4,128)}, u32[]{:S(2)}) copy-start(s32[1,1,32,4]{2,3,1,0:T(4,128)} %param.13) | copy-start | bytes 1540
  0.0 6.0 %copy-start.6 = (bf16[1,1,32,4,2]{2,4,3,1,0:T(2,128)(2,1)S(1)}, bf16[1,1,32,4,2]{2,4,3,1,0:T(2,128)(2,1)}, u32[]{:S(2)}) copy-start(bf16[1,1,32,4,2]{2,4,3,1,0:T(2,128)(2,1)} %param.14) | copy-start | bytes 1540
  0.0 6.0 %copy-start.5 = (bf16[1,1,32,4,2]{2,4,3,1,0:T(2,128)(2,1)S(1)}, bf16[1,1,32,4,2]{2,4,3,1,0:T(2,128)(2,1)}, u32[]{:S(2)}) copy-start(bf16[1,1,32,4,2]{2,4,3,1,0:T(2,128)(2,1)} %param.15) | copy-start | bytes 1540
  0.0 16.8 %copy-start.8 = (bf16[1,2,21]{2,1,0:T(2,128)(2,1)S(1)}, bf16[1,2,21]{2,1,0:T(2,128)(2,1)}, u32[]{:S(2)}) copy-start(bf16[1,2,21]{2,1,0:T(2,128)(2,1)} %param.11) | copy-start | bytes 256
  1.3 15.5 %collective-permute-start.1 = (bf16[2,16,4096]{2,1,0:T(8,128)(2,1)S(1)}, bf16[2,16,4096]{2,1,0:T(8,128)(2,1)S(1)}, u32[]{:S(2)}, u32[]{:S(2)}) collective-permute-start(bf16[2,16,4096]{2,1,0:T(8,128)(2,1)S(1)} %pad_maximum_fusion.2), channel_id=1, source_target_pairs={{1,0},{2,1},{3,2},{4,3},{5,4},{6,5},{7,6},{8,7},{9,8},{10,9},{11,1... | collective-permute-start | bytes 786440 | tf_op jit(solution)/shard_map/ppermute | solution.py:200
  2.7 14.2 %collective-permute-start = (bf16[2,16,4096]{2,1,0:T(8,128)(2,1)S(1)}, bf16[2,16,4096]{2,1,0:T(8,128)(2,1)S(1)}, u32[]{:S(2)}, u32[]{:S(2)}) collective-permute-start(bf16[2,16,4096]{2,1,0:T(8,128)(2,1)S(1)} %pad_maximum_fusion.1), channel_id=1, source_target_pairs={{0,1},{1,2},{2,3},{3,4},{4,5},{5,6},{6,7},{7,8},{8,9},{9,10},{10,1... | collective-permute-start | bytes 786440 | tf_op jit(solution)/shard_map/ppermute | solution.py:199
  6.9 25.5 %all-to-all-start = ((bf16[32,2,21]{2,1,0:T(2,128)(2,1)}), bf16[32,2,21]{2,1,0:T(2,128)(2,1)S(1)}, u32[]{:S(2)}, u32[]{:S(2)}) async-start(bf16[32,2,21]{2,1,0:T(2,128)(2,1)} %bitcast.4), calls=%async_computation | async-start | bytes 32768 | tf_op jit(solution)/shard_map/all_to_all | solution.py:244
  31.1 1.3 copy-start.1
  68.4 57.2 %all-to-all-start.2 = ((bf16[64,2,64,128]{3,2,1,0:T(8,128)(2,1)}), bf16[64,2,64,128]{3,2,1,0:T(8,128)(2,1)}, u32[]{:S(2)}, u32[]{:S(2)}) async-start(bf16[64,2,64,128]{3,2,1,0:T(8,128)(2,1)} %get-tuple-element.25), calls=%async_computation.2 | async-start | bytes 4194304 | tf_op jit(solution)/shard_map/all_to_all | solution.py:244
  99.5 1.6 copy-start
  118.9 28.0 %collective-permute-start.2 = (bf16[8,48,256]{2,1,0:T(8,128)(2,1)S(1)}, bf16[8,48,256]{2,1,0:T(8,128)(2,1)S(1)}, u32[]{:S(2)}, u32[]{:S(2)}) collective-permute-start(bf16[8,48,256]{2,1,0:T(8,128)(2,1)S(1)} %get-tuple-element.22), channel_id=1, source_target_pairs={{0,32},{32,64},{64,96},{96,0},{1,33},{33,65},{65,97},{97,1},{2,34}... | collective-permute-start | bytes 589832 | tf_op jit(solution)/shard_map/ppermute | solution.py:318
  120.9 28.3 %collective-permute-start.3 = (bf16[8,48,256]{2,1,0:T(8,128)(2,1)S(1)}, bf16[8,48,256]{2,1,0:T(8,128)(2,1)S(1)}, u32[]{:S(2)}, u32[]{:S(2)}) collective-permute-start(bf16[8,48,256]{2,1,0:T(8,128)(2,1)S(1)} %get-tuple-element.23), channel_id=1, source_target_pairs={{0,64},{32,96},{64,0},{96,32},{1,65},{33,97},{65,1},{97,33},{2,66}... | collective-permute-start | bytes 589832 | tf_op jit(solution)/shard_map/ppermute | solution.py:318
  124.5 24.7 %collective-permute-start.4 = (bf16[8,48,256]{2,1,0:T(8,128)(2,1)S(1)}, bf16[8,48,256]{2,1,0:T(8,128)(2,1)}, u32[]{:S(2)}, u32[]{:S(2)}) collective-permute-start(bf16[8,48,256]{2,1,0:T(8,128)(2,1)S(1)} %get-tuple-element.24), channel_id=1, source_target_pairs={{0,96},{32,0},{64,32},{96,64},{1,97},{33,1},{65,33},{97,65},{2,98}... | collective-permute-start | bytes 589832 | tf_op jit(solution)/shard_map/ppermute | solution.py:318
  145.4 17.2 %collective-permute-start.5 = (bf16[8,80,256]{2,1,0:T(8,128)(2,1)S(1)}, bf16[8,80,256]{2,1,0:T(8,128)(2,1)S(1)}, u32[]{:S(2)}, u32[]{:S(2)}) collective-permute-start(bf16[8,80,256]{2,1,0:T(8,128)(2,1)S(1)} %get-tuple-element.28), channel_id=1, source_target_pairs={{0,32},{32,64},{64,96},{96,0},{1,33},{33,65},{65,97},{97,1},{2,34}... | collective-permute-start | bytes 983048 | tf_op jit(solution)/shard_map/ppermute | solution.py:318
  146.5 16.1 %collective-permute-start.6 = (bf16[8,80,256]{2,1,0:T(8,128)(2,1)S(1)}, bf16[8,80,256]{2,1,0:T(8,128)(2,1)S(1)}, u32[]{:S(2)}, u32[]{:S(2)}) collective-permute-start(bf16[8,80,256]{2,1,0:T(8,128)(2,1)S(1)} %get-tuple-element.29), channel_id=1, source_target_pairs={{0,64},{32,96},{64,0},{96,32},{1,65},{33,97},{65,1},{97,33},{2,66}... | collective-permute-start | bytes 983048 | tf_op jit(solution)/shard_map/ppermute | solution.py:318
  146.9 16.2 %collective-permute-start.7 = (bf16[8,80,256]{2,1,0:T(8,128)(2,1)S(1)}, bf16[8,80,256]{2,1,0:T(8,128)(2,1)S(1)}, u32[]{:S(2)}, u32[]{:S(2)}) collective-permute-start(bf16[8,80,256]{2,1,0:T(8,128)(2,1)S(1)} %get-tuple-element.30), channel_id=1, source_target_pairs={{0,96},{32,0},{64,32},{96,64},{1,97},{33,1},{65,33},{97,65},{2,98}... | collective-permute-start | bytes 983048 | tf_op jit(solution)/shard_map/ppermute | solution.py:318

commit v2 on v0

v2 whole, which is shorter than its diff:
```python
import functools
import math

import jax
import jax.numpy as jnp
from jax import lax
from jax.experimental import pallas as pl
from jax.experimental.pallas import tpu as pltpu
from jax.sharding import PartitionSpec as P

BS = 128
HALO = 16
BAND = 16
CAP = 2
PB_DEV = 8
CUT = 80
EDGE = CUT - 16
FILTER_COLUMNS = 1024
MAP_SLOTS = 16
WARP_SLOTS = 16
VMEM = 60 * 1024 * 1024


def toeplitz(rows, columns, shift, tap):
    lag = lax.broadcasted_iota(jnp.int32, (rows, columns), 0) - lax.broadcasted_iota(jnp.int32, (rows, columns), 1) + shift
    matrix = jnp.zeros((rows, columns), jnp.float32)
    for index, value in enumerate(tap):
        matrix = jnp.where(lag == index, value, matrix)
    return matrix.astype(jnp.bfloat16)

def filter_kernel(first, last, slot_ref, taps_ref, *refs):
    images, mask_ref, halo_ref = (refs[0:3], refs[3:6]), refs[6], refs[7]
    out, framed, across_ref, down_ref = refs[8:]
    rows, columns = mask_ref.shape
    height = last - first
    tall = height + 2 * HALO
    wide = 2 * BS
    half = (taps_ref.shape[-1] - 1) // 2
    step, steps = pl.program_id(0), pl.num_programs(0)

    @pl.when(step == 0)
    def _():
        empty = jnp.zeros((BS, BS), jnp.bfloat16)
        values = taps_ref[0].astype(jnp.float32)
        for plane in range(2):
            taps = [
                [values[way : way + 1, tap : tap + 1] for tap in range(taps_ref.shape[-1])]
                for way in range(2)
            ]
            if plane == 1:
                taps = [[tap * tap for tap in way] for way in taps]
            left, middle, right = (toeplitz(BS, BS, half + by * BS, taps[0]) for by in (-1, 0, 1))
            pattern = ((left, empty), (middle, left), (right, middle), (empty, right))
            for row, blocks in enumerate(pattern):
                across_ref[plane, row * BS : (row + 1) * BS, :BS] = blocks[0]
                across_ref[plane, row * BS : (row + 1) * BS, BS:] = blocks[1]
            down_ref[plane] = toeplitz(height, tall, half + HALO, taps[1][::-1])

    start = pl.multiple_of(step * columns, columns)
    before = pl.multiple_of(jnp.maximum(start - BS, 0), BS)
    after = pl.multiple_of(jnp.minimum(start + columns, (steps - 1) * columns - BS + columns), BS)
    for plane, parts in enumerate(images):
        halo = [
            halo_ref[plane, :, pl.ds(before, BS)],
            halo_ref[plane, :, pl.ds(start, columns)],
            halo_ref[plane, :, pl.ds(after, BS)],
        ]
        if first == 0:
            strips = ((0, halo), (HALO, [part[: last + HALO, :] for part in parts]))
        else:
            strips = (
                (0, [part[first - HALO :, :] for part in parts]),
                (rows - first + HALO, halo),
            )
        for row, pieces in strips:
            column = 0
            for piece, kept in zip(pieces, (step > 0, None, step < steps - 1)):
                if kept is not None:
                    piece = jnp.where(kept, piece, jnp.zeros_like(piece))
                framed[
                    plane, row : row + piece.shape[0], column : column + piece.shape[1]
                ] = piece
                column += piece.shape[1]

    tiles = columns // wide
    matched = []
    for plane in range(2):
        stack = jnp.concatenate(
            [framed[plane, :, tile * wide : tile * wide + 4 * BS] for tile in range(tiles)], axis=0
        )
        passed = jnp.dot(stack, across_ref[plane], preferred_element_type=jnp.float32).astype(
            jnp.bfloat16
        )
        matched.append(
            [
                jnp.dot(
                    down_ref[plane],
                    passed[tile * tall : (tile + 1) * tall],
                    preferred_element_type=jnp.float32,
                )
                for tile in range(tiles)
            ]
        )
    for tile in range(tiles):
        usable = mask_ref[first:last, tile * wide : (tile + 1) * wide].astype(jnp.float32)
        weight = usable / matched[1][tile]
        weighted = (weight * matched[0][tile]).astype(jnp.bfloat16)
        weight = weight.astype(jnp.bfloat16)
        for block in range(2):
            slot = slot_ref[(step * tiles + tile) * 2 + block]
            lanes = slice(block * BS, (block + 1) * BS)
            out[slot, 0] = weighted[:, lanes]
            out[slot, 1] = weight[:, lanes]


def filtered(first, last, slots, slot, taps, exposure, variance, mask, halo):
    rows, columns = mask.shape
    height = last - first
    per_step = FILTER_COLUMNS // BS
    end = columns // BS - 1
    smem = pl.BlockSpec(memory_space=pltpu.SMEM)
    vmem = pl.BlockSpec(memory_space=pltpu.VMEM)
    image_specs = [
        pl.BlockSpec((rows, BS), lambda i: (0, jnp.maximum(i * per_step - 1, 0))),
        pl.BlockSpec((rows, FILTER_COLUMNS), lambda i: (0, i)),
        pl.BlockSpec((rows, BS), lambda i: (0, jnp.minimum((i + 1) * per_step, end))),
    ]
    return pl.pallas_call(
        functools.partial(filter_kernel, first, last),
        grid=(columns // FILTER_COLUMNS,),
        out_shape=jax.ShapeDtypeStruct((slots, 2, height, BS), jnp.bfloat16),
        in_specs=[smem, vmem] + image_specs * 2 + [image_specs[1], vmem],
        out_specs=pl.BlockSpec((slots, 2, height, BS), lambda i: (0, 0, 0, 0)),
        scratch_shapes=[
            pltpu.VMEM((2, height + 2 * HALO, FILTER_COLUMNS + 2 * BS), jnp.bfloat16),
            pltpu.VMEM((2, 4 * BS, 2 * BS), jnp.bfloat16),
            pltpu.VMEM((2, height, height + 2 * HALO), jnp.bfloat16),
        ],
        compiler_params=pltpu.CompilerParams(vmem_limit_bytes=VMEM),
        cost_estimate=pl.CostEstimate(
            flops=2 * 10**9, bytes_accessed=16 * 2**20, transcendentals=0
        ),
        name="filter",
    )(slot, taps, *[exposure] * 3, *[variance] * 3, mask, halo)


def map_kernel(pairs, split, table_ref, first_ref, second_ref, column_ref, spread_ref, place_ref):
    lanes = lax.broadcasted_iota(jnp.int32, (BS, BS), 1)
    rows = lax.broadcasted_iota(jnp.int32, (BS, BS), 0)
    group = lanes // BAND
    target = rows + lanes % BAND - BAND // 2
    facts = table_ref[...]
    pick = lax.broadcasted_iota(jnp.int32, (facts.shape[1], BS), 0)
    own = lax.broadcasted_iota(jnp.int32, (facts.shape[1], BS), 1) // BAND
    for index in range(2):
        chosen = (pick == own + index * 2 * pairs).astype(jnp.bfloat16)
        spread_ref[index] = jnp.dot(facts, chosen, preferred_element_type=jnp.float32)
    centre = (BS - 1) / 2.0
    place_ref[0] = rows.astype(jnp.float32) - centre
    inside = (target >= 0) & (target < BS)
    place_ref[1] = jnp.where(inside, target.astype(jnp.float32) - centre, 1e3)

    def build(slot):
        stretch = spread_ref[0, pl.ds(slot, 1), :]
        offset = spread_ref[1, pl.ds(slot, 1), :]
        x = (1.0 + stretch) * place_ref[0] + offset - place_ref[1]
        square = x * x * (math.pi / 3.0) ** 2
        sinc = jnp.full_like(x, 1.0 / math.factorial(21))
        for term in range(9, -1, -1):
            sinc = sinc * square + (-1.0) ** term / math.factorial(2 * term + 1)
        power = sinc * sinc
        value = power * (1.0 - (4.0 / 3.0) * power * square)
        value = jnp.where(jnp.abs(x) < 3.0, value, 0.0)
        for pair in range(pairs):
            for direction in range(2):
                index = pair * 2 + direction
                one = jnp.where(group == index, value, 0.0)
                shift = (-BAND // 2 - BAND * index) % BS
                turned = pltpu.roll(one, shift, 1, stride=1, stride_axis=0).astype(jnp.bfloat16)
                if direction == 0:
                    first_ref[slot, pair] = turned[:split]
                    second_ref[slot, pair] = turned[split:]
                else:
                    column_ref[slot, pair] = turned.T

    @pl.loop(0, column_ref.shape[0] // 2)
    def _(batch):
        build(batch * 2)
        build(batch * 2 + 1)


def make_maps(table, earlier, pairs, part, parts):
    slots = table.shape[0]
    heights = (EDGE, BS - EDGE, BS)
    steps = slots // parts // MAP_SLOTS

    def kernel(table_ref, *refs):
        map_kernel(pairs, EDGE, table_ref, *refs[-5:])

    return pl.pallas_call(
        kernel,
        grid=(steps,),
        out_shape=[jax.ShapeDtypeStruct((slots, pairs, height, BS), jnp.bfloat16) for height in heights],
        in_specs=[pl.BlockSpec((MAP_SLOTS, table.shape[1]), lambda i: (part * steps + i, 0))]
        + [pl.BlockSpec(memory_space=pl.ANY)] * (3 if earlier else 0),
        out_specs=[
            pl.BlockSpec((MAP_SLOTS, pairs, height, BS), lambda i: (part * steps + i, 0, 0, 0))
            for height in heights
        ],
        scratch_shapes=[
            pltpu.VMEM((2, MAP_SLOTS, BS), jnp.float32),
            pltpu.VMEM((2, BS, BS), jnp.float32),
        ],
        input_output_aliases={1: 0, 2: 1, 3: 2} if earlier else {},
        compiler_params=pltpu.CompilerParams(vmem_limit_bytes=VMEM),
        cost_estimate=pl.CostEstimate(
            flops=10**10, bytes_accessed=24 * 2**20, transcendentals=0
        ),
        name="maps",
    )(table, *(earlier or []))


def warp_kernel(count, aim_ref, *refs):
    blocks, row_ref, column_ref = refs[:count], refs[count], refs[count + 1]
    outs, total = refs[count + 2 : -1], refs[-1]
    step = pl.program_id(0)
    per_step, pairs, height, _ = row_ref.shape

    @pl.when(step == 0)
    def _():
        total[...] = jnp.zeros_like(total)

    for slot in range(per_step):
        source = jnp.concatenate(
            [jnp.concatenate([ref[slot, plane] for ref in blocks], axis=0) for plane in range(2)],
            axis=1,
        )
        stack = row_ref[slot].reshape(pairs * height, BS)[:, : source.shape[0]]
        half_warp = jnp.dot(stack, source, preferred_element_type=jnp.float32).astype(jnp.bfloat16)
        for pair in range(pairs):
            mine = half_warp[pair * height : (pair + 1) * height]
            both = jnp.concatenate([mine[:, :BS], mine[:, BS:]], axis=0)
            aim = aim_ref[(step * per_step + slot) * pairs + pair]
            total[aim] += jnp.dot(both, column_ref[slot, pair], preferred_element_type=jnp.float32)

    @pl.when(step == pl.num_programs(0) - 1)
    def _():
        for index, out in enumerate(outs):
            out[...] = total[index * PB_DEV : (index + 1) * PB_DEV].astype(out.dtype)


def warp(aims, blocks, row_maps, column_maps, groups):
    slots, pairs, height, _ = row_maps.shape

    def whole(array):
        return pl.BlockSpec((WARP_SLOTS,) + array.shape[1:], lambda i, _: (i, 0, 0, 0))

    operands = [*blocks, row_maps, column_maps]
    return pl.pallas_call(
        functools.partial(warp_kernel, len(blocks)),
        grid_spec=pltpu.PrefetchScalarGridSpec(
            num_scalar_prefetch=1,
            grid=(slots // WARP_SLOTS,),
            in_specs=[whole(array) for array in operands],
            out_specs=[pl.BlockSpec((PB_DEV, 2 * height, BS), lambda i, _: (0, 0, 0))] * groups,
            scratch_shapes=[pltpu.VMEM((groups * PB_DEV + 1, 2 * height, BS), jnp.float32)],
        ),
        out_shape=[
            jax.ShapeDtypeStruct(
                (PB_DEV, 2 * height, BS), jnp.float32 if index == 0 else jnp.bfloat16
            )
            for index in range(groups)
        ],
        compiler_params=pltpu.CompilerParams(vmem_limit_bytes=VMEM),
        cost_estimate=pl.CostEstimate(
            flops=6 * 10**9, bytes_accessed=32 * 2**20, transcendentals=0
        ),
        name="warp",
    )(aims, *operands)


def local(
    exposure, variance, pixel_mask, psf_kernel, block_owner, patch_index, pair_stretch, pair_offset
):
    _, rows, columns = exposure.shape
    block_count = columns // BS
    owners = lax.axis_size("sky")
    groups = lax.axis_size("visit")
    slots = owners * CAP
    pairs = patch_index.shape[-1]

    def exchange(array):
        return lax.all_to_all(array, "sky", split_axis=0, concat_axis=0, tiled=True)

    low = jnp.concatenate([exposure[:, rows - HALO :], variance[:, rows - HALO :]], axis=0)
    high = jnp.concatenate([exposure[:, :HALO], variance[:, :HALO]], axis=0)
    low, high, block_owner, patch_index, pair_stretch, pair_offset = lax.optimization_barrier(
        (low, high, block_owner, patch_index, pair_stretch, pair_offset)
    )
    top = lax.ppermute(low, "sky", [(i, i + 1) for i in range(owners - 1)])
    bottom = lax.ppermute(high, "sky", [(i + 1, i) for i in range(owners - 1)])

    facts = jnp.concatenate(
        [
            pair_stretch.reshape(-1),
            pair_offset.reshape(-1),
            patch_index.reshape(-1).astype(jnp.bfloat16),
            block_owner.reshape(-1).astype(jnp.bfloat16),
        ]
    )
    known = exchange(jnp.broadcast_to(facts[None], (owners, facts.shape[0])))

    owner = block_owner.reshape(block_count)
    order = jnp.arange(block_count)
    earlier = (owner[:, None] == owner[None, :]) & (order[None, :] < order[:, None])
    slot = owner * CAP + jnp.sum(earlier, axis=1).astype(jnp.int32)

    images = [array.reshape(rows, columns) for array in (exposure, variance, pixel_mask)]
    upper_planes = filtered(0, CUT, slots, slot, psf_kernel, *images, top)
    upper_planes, known, slot, bottom = lax.optimization_barrier(
        (upper_planes, known, slot, bottom)
    )
    first = exchange(upper_planes)

    lower_planes = filtered(CUT, rows, slots, slot, psf_kernel, *images, bottom)
    sizes = [2 * pairs * block_count, 2 * pairs * block_count, pairs * block_count, block_count]
    ends = [sum(sizes[: index + 1]) for index in range(len(sizes))]
    stretch, offset, patch, holder = (
        known[:, end - size : end].reshape(owners, block_count, -1).astype(jnp.float32)
        for end, size in zip(ends, sizes)
    )
    mine = holder[:, :, 0] == lax.axis_index("sky").astype(jnp.float32)
    rank = jnp.cumsum(mine.astype(jnp.int32), axis=1) - 1
    chosen = mine[:, None, :] & (rank[:, None, :] == jnp.arange(CAP)[None, :, None])
    chosen = chosen.astype(jnp.bfloat16)

    def picked(values):
        return jnp.einsum(
            "srb,sbf->srf",
            chosen,
            values.astype(jnp.bfloat16),
            preferred_element_type=jnp.float32,
        ).reshape(slots, -1)

    table = picked(jnp.concatenate([stretch, offset, patch, jnp.ones_like(holder)], axis=2))

    patch = table[:, 4 * pairs : 5 * pairs].astype(jnp.int32)
    distance = (patch // PB_DEV - lax.axis_index("visit")) % groups
    aims = jnp.where(
        table[:, 5 * pairs :] > 0.5, distance * PB_DEV + patch % PB_DEV, groups * PB_DEV
    )
    aims = aims.reshape(slots * pairs)
    maps = make_maps(table.astype(jnp.bfloat16), None, pairs, 0, 1)

    first, lower_planes, aims, *maps = lax.optimization_barrier((first, lower_planes, aims, *maps))
    first_maps, second_maps, column_maps = maps
    second = exchange(lower_planes)

    def coadd(sums):
        whole = sums[0]
        for step in range(1, groups):
            ring = [(i, (i + step) % groups) for i in range(groups)]
            whole = whole + lax.ppermute(sums[step], "visit", ring).astype(jnp.float32)
        height = whole.shape[1] // 2
        return whole[:, :height] / jnp.maximum(whole[:, height:], 1.0)

    upper = warp(aims, [first], first_maps, column_maps, groups)
    *upper, first = lax.optimization_barrier((*upper, first))
    lower = warp(aims, [first, second], second_maps, column_maps, groups)
    return jnp.concatenate([coadd(upper), coadd(lower)], axis=1)


def solution(mesh):
    return jax.shard_map(
        local,
        mesh=mesh,
        in_specs=(
            P("visit", "sky", None),
            P("visit", "sky", None),
            P("visit", "sky", None),
            P("visit", None, None),
            P("visit", "sky", None),
            P("visit", "sky", None, None),
            P("visit", "sky", None, None, None),
            P("visit", "sky", None, None, None),
        ),
        out_specs=P(("visit", "sky"), None, None),
        check_vma=False,
    )
```

time: 504 us -> 133 us (0.26)
  waiting for transfers between devices: 304 us -> 24.9 us
  local copies, waits for them, and re-layouts: 76.5 us -> 8.46 us
  Pallas kernels: 0 us -> 56.9 us
  other arithmetic: 50 us -> 5.31 us
  matrix products: 36.2 us -> 0.27 us
  starting transfers between devices: 20.7 us -> 35.9 us
  between operations: 13.7 us -> 0.21 us
    all_to_all x2 -> x3, waiting for transfers between devices: 213 us -> 15.7 us  [exchange(): return lax.all_to_all(array, 'sky', split_axis=0, concat_axis=0, tiled=True)]
    psum x1 -> x0, waiting for transfers between devices: 91.1 us -> none  [local(): summed = lax.psum(partial_value, 'visit')]
    pallas_call x0 -> x5, Pallas kernels: none -> 56.9 us  [the longest x2 21.3 us: warp(): pl.pallas_call(functools.partial(warp_kernel, len(blocks)), grid_spec=plt...]
    reshape x5 -> x3, local copies, waits for them, and re-layouts: 49.8 us -> 0.99 us  [the longest x1 0.7 us: local(): aims = aims.reshape(slots * pairs)]
    convert_element_type x7 -> x4, other arithmetic: 45.8 us -> 1.98 us  [the longest x1 0.68 us: local(): patch_index.reshape(-1).astype(jnp.bfloat16)]
    dot_general x9 -> x1, matrix products: 36.2 us -> 0.27 us  [picked(): jnp.einsum('srb,sbf->srf', chosen, values.astype(jnp.bfloat16), preferred...]
    ppermute x2 -> x8, starting transfers between devices: 3.66 us -> 16.5 us  [the longest x6 13 us: coadd(): whole = whole + lax.ppermute(sums[step], 'visit', ring).astype(jnp.float32)]
    gather x2 -> x0, local copies, waits for them, and re-layouts: 11.4 us -> none  [the longest x1 10.8 us: local(): warped[source_of]]
  transfers between devices with their start and end apart: 5 -> 11, of which waited for: 2 -> 5; matrix products, arithmetic and copies ran while one was open for 19% -> 3% of each run, Pallas kernels for 0% -> 43%
where the time goes in v2:
time: 133 us; the launch traced here: 132 us
  Pallas kernels  56.9 us (43%)
  starting transfers between devices  35.9 us (27%)
  waiting for transfers between devices  24.9 us (19%)
  local copies, waits for them, and re-layouts  8.46 us (6%)
  other arithmetic  5.31 us (4%)
    pallas_call x2, Pallas kernels, warp(): pl.pallas_call(functools.partial(warp_kernel, len(blocks)), grid_spec=plt...  21.3 us
    pallas_call x1, Pallas kernels, make_maps(): pl.pallas_call(kernel, grid=(steps,), out_shape=[jax.ShapeDtypeStruct((sl...  20.6 us
    all_to_all x3, starting transfers between devices, exchange(): return lax.all_to_all(array, 'sky', split_axis=0, concat_axis=0, tiled=True)  19.4 us
    all_to_all x3, waiting for transfers between devices, exchange(): return lax.all_to_all(array, 'sky', split_axis=0, concat_axis=0, tiled=True)  15.7 us
    pallas_call x2, Pallas kernels, filtered(): pl.pallas_call(functools.partial(filter_kernel, first, last), grid=(colum...  14.9 us
    ppermute x6, starting transfers between devices, coadd(): whole = whole + lax.ppermute(sums[step], 'visit', ring).astype(jnp.float32)  13 us
    ppermute x6, waiting for transfers between devices, coadd(): whole = whole + lax.ppermute(sums[step], 'visit', ring).astype(jnp.float32)  9.27 us
  transfers between devices with their start and end apart: 11, of which 5 were waited for; matrix products, arithmetic and copies ran while one was open for 3% of the time, Pallas kernels for 43%

profile of v2, /device:TPU:0, one launch (start us, length us, event | category | flops | bytes accessed | tf_op | source)
XLA Modules:
  0.0 132.0 jit_solution(11653977204269405848)
XLA Ops:
  0.0 1.0 fusion.25
  1.0 1.0 fusion.26
  6.1 0.9 reduce.2
  7.8 7.4 %all-to-all-start = ((bf16[32,2,336]{2,1,0:T(2,128)(2,1)}), bf16[32,2,336]{2,1,0:T(2,128)(2,1)S(1)}, u32[]{:S(2)}, u32[]{:S(2)}) async-start(bf16[32,2,336]{2,1,0:T(2,128)(2,1)} %reshape.68), calls=%async_computation | async-start | bytes 98304 | tf_op jit(solution)/shard_map/all_to_all | solution.py:293
  15.2 2.2 %collective-permute-start = (bf16[2,16,4096]{2,1,0:T(8,128)(2,1)S(1)}, bf16[2,16,4096]{2,1,0:T(8,128)(2,1)S(1)}, u32[]{:S(2)}, u32[]{:S(2)}) collective-permute-start(bf16[2,16,4096]{2,1,0:T(8,128)(2,1)S(1)} %get-tuple-element.38), channel_id=1, source_target_pairs={{0,1},{1,2},{2,3},{3,4},{4,5},{5,6},{6,7},{7,8},{8,9},{9,10},{10,1... | collective-permute-start | bytes 786440 | tf_op jit(solution)/shard_map/ppermute | solution.py:300
  17.4 1.3 collective-permute-start.1
  19.4 3.2 %all-to-all-done = bf16[32,2,336]{2,1,0:T(2,128)(2,1)S(1)} async-done(((bf16[32,2,336]{2,1,0:T(2,128)(2,1)}), bf16[32,2,336]{2,1,0:T(2,128)(2,1)S(1)}, u32[]{:S(2)}, u32[]{:S(2)}) %all-to-all-start) | async-done | bytes 43040 | tf_op jit(solution)/shard_map/all_to_all | solution.py:293
  23.7 7.9 %filter.2 = bf16[64,2,80,128]{3,2,1,0:T(8,128)(2,1)} custom-call(s32[32]{0:T(128)} %multiply_add_fusion.slot_ref, bf16[1,2,21]{2,1,0:T(2,128)(2,1)} %taps_ref.3, bf16[128,4096]{1,0:T(8,128)(2,1)} %bitcast.16, bf16[128,4096]{1,0:T(8,128)(2,1)} %bitcast.17, bf16[128,4096]{1,0:T(8,128)(2,1)} %bitcast.18, bf16[128,4096]{1,0:T(8,128)(2,1)} %bitcast.22, ...), custom_call_target="tpu_custom_call" | custom-call | flops 2000000000 | bytes 16777216 | tf_op jit(solution)/shard_map/filter/pallas_call | solution.py:128
  32.3 7.3 %all-to-all-start.1 = ((bf16[64,2,80,128]{3,2,1,0:T(8,128)(2,1)}), bf16[64,2,80,128]{3,2,1,0:T(8,128)(2,1)S(1)}, u32[]{:S(2)}, u32[]{:S(2)}) async-start(bf16[64,2,80,128]{3,2,1,0:T(8,128)(2,1)} %filter.2), calls=%async_computation.1 | async-start | bytes 5242880 | tf_op jit(solution)/shard_map/all_to_all | solution.py:293
  42.4 7.0 %filter.3 = bf16[64,2,48,128]{3,2,1,0:T(8,128)(2,1)} custom-call(s32[32]{0:T(128)} %multiply_add_fusion.slot_ref, bf16[1,2,21]{2,1,0:T(2,128)(2,1)} %taps_ref.3, bf16[128,4096]{1,0:T(8,128)(2,1)} %bitcast.19, bf16[128,4096]{1,0:T(8,128)(2,1)} %bitcast.20, bf16[128,4096]{1,0:T(8,128)(2,1)} %bitcast.21, bf16[128,4096]{1,0:T(8,128)(2,1)} %bitcast.25, ...), custom_call_target="tpu_custom_call" | custom-call | flops 2000000000 | bytes 16777216 | tf_op jit(solution)/shard_map/filter/pallas_call | solution.py:128
  49.4 20.6 %maps.1 = (bf16[64,4,64,128]{3,2,1,0:T(8,128)(2,1)}, bf16[64,4,64,128]{3,2,1,0:T(8,128)(2,1)}, bf16[64,4,128,128]{3,2,1,0:T(8,128)(2,1)}) custom-call(bf16[64,21]{1,0:T(8,128)(2,1)} %convert_element_type.71.table_ref), custom_call_target="tpu_custom_call" | custom-call | flops 10000000000 | bytes 25165824 | tf_op jit(solution)/shard_map/maps/pallas_call | solution.py:200
  70.0 5.6 %all-to-all-done.1.refs_0_ = bf16[64,2,80,128]{3,2,1,0:T(8,128)(2,1)S(1)} async-done(((bf16[64,2,80,128]{3,2,1,0:T(8,128)(2,1)}), bf16[64,2,80,128]{3,2,1,0:T(8,128)(2,1)S(1)}, u32[]{:S(2)}, u32[]{:S(2)}) %all-to-all-start.1) | async-done | bytes 2621472 | tf_op jit(solution)/shard_map/all_to_all | solution.py:293
  75.6 4.7 %all-to-all-start.2 = ((bf16[64,2,48,128]{3,2,1,0:T(8,128)(2,1)}), bf16[64,2,48,128]{3,2,1,0:T(8,128)(2,1)}, u32[]{:S(2)}, u32[]{:S(2)}) async-start(bf16[64,2,48,128]{3,2,1,0:T(8,128)(2,1)} %filter.3), calls=%async_computation.2 | async-start | bytes 3145728 | tf_op jit(solution)/shard_map/all_to_all | solution.py:293
  80.4 10.6 %warp.2 = (f32[8,128,128]{2,1,0:T(8,128)}, bf16[8,128,128]{2,1,0:T(8,128)(2,1)}, bf16[8,128,128]{2,1,0:T(8,128)(2,1)}, bf16[8,128,128]{2,1,0:T(8,128)(2,1)}) custom-call(s32[256]{0:T(256)} %reshape.65.aim_ref, bf16[64,2,80,128]{3,2,1,0:T(8,128)(2,1)} %copy-done, bf16[64,4,64,128]{3,2,1,0:T(8,128)(2,1)} %get-tuple-element.52.refs_1_, ...), custom_call_target="tpu_custom_call" | custom-call | flops 6000000000 | bytes 33554432 | tf_op jit(solution)/shard_map/warp/pallas_call | solution.py:259
  90.9 1.9 %collective-permute-start.2 = (bf16[8,128,128]{2,1,0:T(8,128)(2,1)}, bf16[8,128,128]{2,1,0:T(8,128)(2,1)S(1)}, u32[]{:S(2)}, u32[]{:S(2)}) collective-permute-start(bf16[8,128,128]{2,1,0:T(8,128)(2,1)} %get-tuple-element.59), channel_id=1, source_target_pairs={{0,32},{32,64},{64,96},{96,0},{1,33},{33,65},{65,97},{97,1},{2,34}... | collective-permute-start | bytes 786440 | tf_op jit(solution)/shard_map/ppermute | solution.py:363
  92.8 3.6 %collective-permute-start.3 = (bf16[8,128,128]{2,1,0:T(8,128)(2,1)}, bf16[8,128,128]{2,1,0:T(8,128)(2,1)S(1)}, u32[]{:S(2)}, u32[]{:S(2)}) collective-permute-start(bf16[8,128,128]{2,1,0:T(8,128)(2,1)} %get-tuple-element.60), channel_id=1, source_target_pairs={{0,64},{32,96},{64,0},{96,32},{1,65},{33,97},{65,1},{97,33},{2,66}... | collective-permute-start | bytes 786440 | tf_op jit(solution)/shard_map/ppermute | solution.py:363
  96.4 1.0 collective-permute-start.4
  97.4 6.8 %all-to-all-done.2.refs_1_ = bf16[64,2,48,128]{3,2,1,0:T(8,128)(2,1)} async-done(((bf16[64,2,48,128]{3,2,1,0:T(8,128)(2,1)}), bf16[64,2,48,128]{3,2,1,0:T(8,128)(2,1)}, u32[]{:S(2)}, u32[]{:S(2)}) %all-to-all-start.2) | async-done | bytes 1572896 | tf_op jit(solution)/shard_map/all_to_all | solution.py:293
  104.3 10.8 %warp.3 = (f32[8,128,128]{2,1,0:T(8,128)}, bf16[8,128,128]{2,1,0:T(8,128)(2,1)}, bf16[8,128,128]{2,1,0:T(8,128)(2,1)}, bf16[8,128,128]{2,1,0:T(8,128)(2,1)}) custom-call(s32[256]{0:T(256)} %reshape.65.aim_ref, bf16[64,2,80,128]{3,2,1,0:T(8,128)(2,1)} %copy-done, bf16[64,2,48,128]{3,2,1,0:T(8,128)(2,1)} %all-to-all-done.2.refs_1_, ...), custom_call_target="tpu_custom_call" | custom-call | flops 6000000000 | bytes 33554432 | tf_op jit(solution)/shard_map/warp/pallas_call | solution.py:259
  115.0 1.9 %collective-permute-start.5 = (bf16[8,128,128]{2,1,0:T(8,128)(2,1)}, bf16[8,128,128]{2,1,0:T(8,128)(2,1)S(1)}, u32[]{:S(2)}, u32[]{:S(2)}) collective-permute-start(bf16[8,128,128]{2,1,0:T(8,128)(2,1)} %get-tuple-element.66), channel_id=1, source_target_pairs={{0,32},{32,64},{64,96},{96,0},{1,33},{33,65},{65,97},{97,1},{2,34}... | collective-permute-start | bytes 786440 | tf_op jit(solution)/shard_map/ppermute | solution.py:363
  117.0 3.6 %collective-permute-start.6 = (bf16[8,128,128]{2,1,0:T(8,128)(2,1)}, bf16[8,128,128]{2,1,0:T(8,128)(2,1)S(1)}, u32[]{:S(2)}, u32[]{:S(2)}) collective-permute-start(bf16[8,128,128]{2,1,0:T(8,128)(2,1)} %get-tuple-element.67), channel_id=1, source_target_pairs={{0,64},{32,96},{64,0},{96,32},{1,65},{33,97},{65,1},{97,33},{2,66}... | collective-permute-start | bytes 786440 | tf_op jit(solution)/shard_map/ppermute | solution.py:363
  120.5 1.0 collective-permute-start.7
  121.7 3.9 %collective-permute-done.5 = bf16[8,128,128]{2,1,0:T(8,128)(2,1)S(1)} collective-permute-done((bf16[8,128,128]{2,1,0:T(8,128)(2,1)}, bf16[8,128,128]{2,1,0:T(8,128)(2,1)S(1)}, u32[]{:S(2)}, u32[]{:S(2)}) %collective-permute-start.5) | collective-permute-done | bytes 262176 | tf_op jit(solution)/shard_map/ppermute | solution.py:363
  125.6 5.4 %collective-permute-done.6 = bf16[8,128,128]{2,1,0:T(8,128)(2,1)S(1)} collective-permute-done((bf16[8,128,128]{2,1,0:T(8,128)(2,1)}, bf16[8,128,128]{2,1,0:T(8,128)(2,1)S(1)}, u32[]{:S(2)}, u32[]{:S(2)}) %collective-permute-start.6) | collective-permute-done | bytes 262176 | tf_op jit(solution)/shard_map/ppermute | solution.py:363
  (56 shorter events, 11.1 us)
Async XLA Ops:
  0.0 18.7 %copy-start.5 = (s32[1,1,32]{2,1,0:T(1,128)S(1)}, s32[1,1,32]{2,1,0:T(1,128)}, u32[]{:S(2)}) copy-start(s32[1,1,32]{2,1,0:T(1,128)} %param.12) | copy-start | bytes 388
  7.8 14.9 %all-to-all-start = ((bf16[32,2,336]{2,1,0:T(2,128)(2,1)}), bf16[32,2,336]{2,1,0:T(2,128)(2,1)S(1)}, u32[]{:S(2)}, u32[]{:S(2)}) async-start(bf16[32,2,336]{2,1,0:T(2,128)(2,1)} %reshape.68), calls=%async_computation | async-start | bytes 98304 | tf_op jit(solution)/shard_map/all_to_all | solution.py:293
  15.2 7.8 %collective-permute-start = (bf16[2,16,4096]{2,1,0:T(8,128)(2,1)S(1)}, bf16[2,16,4096]{2,1,0:T(8,128)(2,1)S(1)}, u32[]{:S(2)}, u32[]{:S(2)}) collective-permute-start(bf16[2,16,4096]{2,1,0:T(8,128)(2,1)S(1)} %get-tuple-element.38), channel_id=1, source_target_pairs={{0,1},{1,2},{2,3},{3,4},{4,5},{5,6},{6,7},{7,8},{8,9},{9,10},{10,1... | collective-permute-start | bytes 786440 | tf_op jit(solution)/shard_map/ppermute | solution.py:300
  17.4 14.2 %collective-permute-start.1 = (bf16[2,16,4096]{2,1,0:T(8,128)(2,1)S(1)}, bf16[2,16,4096]{2,1,0:T(8,128)(2,1)S(1)}, u32[]{:S(2)}, u32[]{:S(2)}) collective-permute-start(bf16[2,16,4096]{2,1,0:T(8,128)(2,1)S(1)} %get-tuple-element.42), channel_id=1, source_target_pairs={{1,0},{2,1},{3,2},{4,3},{5,4},{6,5},{7,6},{8,7},{9,8},{10,9},{11,1... | collective-permute-start | bytes 786440 | tf_op jit(solution)/shard_map/ppermute | solution.py:301
  23.0 0.7 copy-start.3
  31.6 0.7 copy-start.4
  32.3 43.3 %all-to-all-start.1 = ((bf16[64,2,80,128]{3,2,1,0:T(8,128)(2,1)}), bf16[64,2,80,128]{3,2,1,0:T(8,128)(2,1)S(1)}, u32[]{:S(2)}, u32[]{:S(2)}) async-start(bf16[64,2,80,128]{3,2,1,0:T(8,128)(2,1)} %filter.2), calls=%async_computation.1 | async-start | bytes 5242880 | tf_op jit(solution)/shard_map/all_to_all | solution.py:293
  75.6 4.7 %copy-start = (bf16[64,2,80,128]{3,2,1,0:T(8,128)(2,1)}, bf16[64,2,80,128]{3,2,1,0:T(8,128)(2,1)S(1)}, u32[]{:S(2)}) copy-start(bf16[64,2,80,128]{3,2,1,0:T(8,128)(2,1)S(1)} %all-to-all-done.1.refs_0_) | copy-start | bytes 7864324
  75.6 28.6 %all-to-all-start.2 = ((bf16[64,2,48,128]{3,2,1,0:T(8,128)(2,1)}), bf16[64,2,48,128]{3,2,1,0:T(8,128)(2,1)}, u32[]{:S(2)}, u32[]{:S(2)}) async-start(bf16[64,2,48,128]{3,2,1,0:T(8,128)(2,1)} %filter.3), calls=%async_computation.2 | async-start | bytes 3145728 | tf_op jit(solution)/shard_map/all_to_all | solution.py:293
  90.9 30.6 %copy-start.1 = (f32[8,128,128]{2,1,0:T(8,128)S(1)}, f32[8,128,128]{2,1,0:T(8,128)}, u32[]{:S(2)}) copy-start(f32[8,128,128]{2,1,0:T(8,128)} %get-tuple-element.58) | copy-start | bytes 1572868
  90.9 29.6 %collective-permute-start.2 = (bf16[8,128,128]{2,1,0:T(8,128)(2,1)}, bf16[8,128,128]{2,1,0:T(8,128)(2,1)S(1)}, u32[]{:S(2)}, u32[]{:S(2)}) collective-permute-start(bf16[8,128,128]{2,1,0:T(8,128)(2,1)} %get-tuple-element.59), channel_id=1, source_target_pairs={{0,32},{32,64},{64,96},{96,0},{1,33},{33,65},{65,97},{97,1},{2,34}... | collective-permute-start | bytes 786440 | tf_op jit(solution)/shard_map/ppermute | solution.py:363
  92.8 28.7 %collective-permute-start.3 = (bf16[8,128,128]{2,1,0:T(8,128)(2,1)}, bf16[8,128,128]{2,1,0:T(8,128)(2,1)S(1)}, u32[]{:S(2)}, u32[]{:S(2)}) collective-permute-start(bf16[8,128,128]{2,1,0:T(8,128)(2,1)} %get-tuple-element.60), channel_id=1, source_target_pairs={{0,64},{32,96},{64,0},{96,32},{1,65},{33,97},{65,1},{97,33},{2,66}... | collective-permute-start | bytes 786440 | tf_op jit(solution)/shard_map/ppermute | solution.py:363
  96.4 25.1 %collective-permute-start.4 = (bf16[8,128,128]{2,1,0:T(8,128)(2,1)}, bf16[8,128,128]{2,1,0:T(8,128)(2,1)S(1)}, u32[]{:S(2)}, u32[]{:S(2)}) collective-permute-start(bf16[8,128,128]{2,1,0:T(8,128)(2,1)} %get-tuple-element.61), channel_id=1, source_target_pairs={{0,96},{32,0},{64,32},{96,64},{1,97},{33,1},{65,33},{97,65},{2,98}... | collective-permute-start | bytes 786440 | tf_op jit(solution)/shard_map/ppermute | solution.py:363
  115.0 16.0 %copy-start.2 = (f32[8,128,128]{2,1,0:T(8,128)S(1)}, f32[8,128,128]{2,1,0:T(8,128)}, u32[]{:S(2)}) copy-start(f32[8,128,128]{2,1,0:T(8,128)} %get-tuple-element.65) | copy-start | bytes 1572868
  115.0 10.6 %collective-permute-start.5 = (bf16[8,128,128]{2,1,0:T(8,128)(2,1)}, bf16[8,128,128]{2,1,0:T(8,128)(2,1)S(1)}, u32[]{:S(2)}, u32[]{:S(2)}) collective-permute-start(bf16[8,128,128]{2,1,0:T(8,128)(2,1)} %get-tuple-element.66), channel_id=1, source_target_pairs={{0,32},{32,64},{64,96},{96,0},{1,33},{33,65},{65,97},{97,1},{2,34}... | collective-permute-start | bytes 786440 | tf_op jit(solution)/shard_map/ppermute | solution.py:363
  117.0 14.0 %collective-permute-start.6 = (bf16[8,128,128]{2,1,0:T(8,128)(2,1)}, bf16[8,128,128]{2,1,0:T(8,128)(2,1)S(1)}, u32[]{:S(2)}, u32[]{:S(2)}) collective-permute-start(bf16[8,128,128]{2,1,0:T(8,128)(2,1)} %get-tuple-element.67), channel_id=1, source_target_pairs={{0,64},{32,96},{64,0},{96,32},{1,65},{33,97},{65,1},{97,33},{2,66}... | collective-permute-start | bytes 786440 | tf_op jit(solution)/shard_map/ppermute | solution.py:363
  120.5 10.5 %collective-permute-start.7 = (bf16[8,128,128]{2,1,0:T(8,128)(2,1)}, bf16[8,128,128]{2,1,0:T(8,128)(2,1)S(1)}, u32[]{:S(2)}, u32[]{:S(2)}) collective-permute-start(bf16[8,128,128]{2,1,0:T(8,128)(2,1)} %get-tuple-element.68), channel_id=1, source_target_pairs={{0,96},{32,0},{64,32},{96,64},{1,97},{33,1},{65,33},{97,65},{2,98}... | collective-permute-start | bytes 786440 | tf_op jit(solution)/shard_map/ppermute | solution.py:363

commit v3 on v2

v3 whole, which is shorter than its diff:
```python
import functools
import math

import jax
import jax.numpy as jnp
from jax import lax
from jax.experimental import pallas as pl
from jax.experimental.pallas import tpu as pltpu
from jax.sharding import PartitionSpec as P

BS = 128
HALO = 16
BAND = 16
CAP = 2
PB_DEV = 8
CUT = 80
EDGE = CUT - 16
FACTS = 16
FILTER_COLUMNS = 1024
WARP_SLOTS = 16
FILTER_VMEM = 32 * 1024 * 1024
WARP_VMEM = 60 * 1024 * 1024


def toeplitz(rows, columns, shift, tap):
    lag = lax.broadcasted_iota(jnp.int32, (rows, columns), 0) - lax.broadcasted_iota(jnp.int32, (rows, columns), 1) + shift
    matrix = jnp.zeros((rows, columns), jnp.float32)
    for index, value in enumerate(tap):
        matrix = jnp.where(lag == index, value, matrix)
    return matrix.astype(jnp.bfloat16)

def filter_kernel(first, last, slot_ref, taps_ref, *refs):
    images, mask_ref, halo_ref = (refs[0:3], refs[3:6]), refs[6], refs[7]
    facts_ref, (out, framed, across_ref, down_ref) = refs[8:-4], refs[-4:]
    rows, columns = mask_ref.shape
    height = last - first
    tall = height + 2 * HALO
    wide = 2 * BS
    half = (taps_ref.shape[-1] - 1) // 2
    step, steps = pl.program_id(0), pl.num_programs(0)

    @pl.when(step == 0)
    def _():
        empty = jnp.zeros((BS, BS), jnp.bfloat16)
        values = taps_ref[0].astype(jnp.float32)
        for plane in range(2):
            taps = [
                [values[way : way + 1, tap : tap + 1] for tap in range(taps_ref.shape[-1])]
                for way in range(2)
            ]
            if plane == 1:
                taps = [[tap * tap for tap in way] for way in taps]
            left, middle, right = (toeplitz(BS, BS, half + by * BS, taps[0]) for by in (-1, 0, 1))
            pattern = ((left, empty), (middle, left), (right, middle), (empty, right))
            for row, blocks in enumerate(pattern):
                across_ref[plane, row * BS : (row + 1) * BS, :BS] = blocks[0]
                across_ref[plane, row * BS : (row + 1) * BS, BS:] = blocks[1]
            down_ref[plane] = toeplitz(height, tall, half + HALO, taps[1][::-1])

        for ref in facts_ref:
            out[:, 2 * height :, :] = jnp.zeros((out.shape[0], FACTS, BS), jnp.bfloat16)

    start = pl.multiple_of(step * columns, columns)
    before = pl.multiple_of(jnp.maximum(start - BS, 0), BS)
    after = pl.multiple_of(jnp.minimum(start + columns, (steps - 1) * columns - BS + columns), BS)
    for plane, parts in enumerate(images):
        halo = [
            halo_ref[plane, :, pl.ds(before, BS)],
            halo_ref[plane, :, pl.ds(start, columns)],
            halo_ref[plane, :, pl.ds(after, BS)],
        ]
        if first == 0:
            strips = ((0, halo), (HALO, [part[: last + HALO, :] for part in parts]))
        else:
            strips = (
                (0, [part[first - HALO :, :] for part in parts]),
                (rows - first + HALO, halo),
            )
        for row, pieces in strips:
            column = 0
            for piece, kept in zip(pieces, (step > 0, None, step < steps - 1)):
                if kept is not None:
                    piece = jnp.where(kept, piece, jnp.zeros_like(piece))
                framed[
                    plane, row : row + piece.shape[0], column : column + piece.shape[1]
                ] = piece
                column += piece.shape[1]

    tiles = columns // wide
    matched = []
    for plane in range(2):
        stack = jnp.concatenate(
            [framed[plane, :, tile * wide : tile * wide + 4 * BS] for tile in range(tiles)], axis=0
        )
        passed = jnp.dot(stack, across_ref[plane], preferred_element_type=jnp.float32).astype(
            jnp.bfloat16
        )
        matched.append(
            [
                jnp.dot(
                    down_ref[plane],
                    passed[tile * tall : (tile + 1) * tall],
                    preferred_element_type=jnp.float32,
                )
                for tile in range(tiles)
            ]
        )
    for tile in range(tiles):
        usable = mask_ref[first:last, tile * wide : (tile + 1) * wide].astype(jnp.float32)
        weight = usable / matched[1][tile]
        weighted = (weight * matched[0][tile]).astype(jnp.bfloat16)
        weight = weight.astype(jnp.bfloat16)
        for block in range(2):
            index = (step * tiles + tile) * 2 + block
            slot = slot_ref[index]
            lanes = slice(block * BS, (block + 1) * BS)
            out[slot, :height, :] = weighted[:, lanes]
            out[slot, height : 2 * height, :] = weight[:, lanes]
            for ref in facts_ref:
                row = jnp.broadcast_to(ref[pl.ds(index, 1), :], (FACTS, BS))
                out[slot, 2 * height :, :] = row.astype(jnp.bfloat16)


def filtered(first, last, slots, slot, taps, exposure, variance, mask, halo, *facts):
    rows, columns = mask.shape
    height = last - first
    tall = 2 * height + (FACTS if facts else 0)
    per_step = FILTER_COLUMNS // BS
    end = columns // BS - 1
    smem = pl.BlockSpec(memory_space=pltpu.SMEM)
    vmem = pl.BlockSpec(memory_space=pltpu.VMEM)
    image_specs = [
        pl.BlockSpec((rows, BS), lambda i: (0, jnp.maximum(i * per_step - 1, 0))),
        pl.BlockSpec((rows, FILTER_COLUMNS), lambda i: (0, i)),
        pl.BlockSpec((rows, BS), lambda i: (0, jnp.minimum((i + 1) * per_step, end))),
    ]
    return pl.pallas_call(
        functools.partial(filter_kernel, first, last),
        grid=(columns // FILTER_COLUMNS,),
        out_shape=jax.ShapeDtypeStruct((slots, tall, BS), jnp.bfloat16),
        in_specs=[smem, vmem] + image_specs * 2 + [image_specs[1], vmem] + [vmem] * len(facts),
        out_specs=pl.BlockSpec((slots, tall, BS), lambda i: (0, 0, 0)),
        scratch_shapes=[
            pltpu.VMEM((2, height + 2 * HALO, FILTER_COLUMNS + 2 * BS), jnp.bfloat16),
            pltpu.VMEM((2, 4 * BS, 2 * BS), jnp.bfloat16),
            pltpu.VMEM((2, height, height + 2 * HALO), jnp.bfloat16),
        ],
        compiler_params=pltpu.CompilerParams(vmem_limit_bytes=FILTER_VMEM),
        cost_estimate=pl.CostEstimate(
            flops=2 * 10**9, bytes_accessed=16 * 2**20, transcendentals=0
        ),
        name="filter",
    )(slot, taps, *[exposure] * 3, *[variance] * 3, mask, halo, *facts)


def series(square, count, odd):
    total = jnp.zeros_like(square)
    for term in range(count, -1, -1):
        total = total * square + (-1.0) ** term / math.factorial(2 * term + odd)
    return total


def accumulate(total, aims, rows, source, columns):
    height = rows.shape[0] // len(columns)
    half_warp = jnp.dot(rows, source, preferred_element_type=jnp.float32).astype(jnp.bfloat16)
    for pair, column in enumerate(columns):
        mine = half_warp[pair * height : (pair + 1) * height]
        both = jnp.concatenate([mine[:, :BS], mine[:, BS:]], axis=0)
        total[aims[pair]] += jnp.dot(both, column, preferred_element_type=jnp.float32)


def upper_kernel(
    pairs, unroll, aim_ref, table_ref, block_ref, second_ref, column_ref, *refs
):
    outs, (total, spread_ref, place_ref, near_ref, taps_ref) = refs[:-5], refs[-5:]
    step = pl.program_id(0)
    per_step = column_ref.shape[0]
    half = per_step // 2
    lanes = lax.broadcasted_iota(jnp.int32, (BS, BS), 1)
    rows = lax.broadcasted_iota(jnp.int32, (BS, BS), 0)
    group = lanes // BAND
    centre = (BS - 1) / 2.0

    @pl.when(step == 0)
    def _():
        total[...] = jnp.zeros_like(total)
        target = rows + lanes % BAND - BAND // 2
        inside = (target >= 0) & (target < BS)
        place_ref[0] = rows.astype(jnp.float32) - centre
        place_ref[1] = jnp.where(inside, target.astype(jnp.float32) - centre, 1e3)

    facts = table_ref[...]
    low, high = facts[:half].astype(jnp.bfloat16), facts[half:].astype(jnp.bfloat16)
    facts = facts.astype(jnp.bfloat16)

    def sent(values, chosen):
        return jnp.dot(values, chosen.astype(jnp.bfloat16), preferred_element_type=jnp.float32)

    for kind in range(2):
        field = 2 * pairs * kind
        spread_ref[kind] = sent(low, (rows == field + 2 * group) & (group < pairs)) + sent(
            high, (rows == field + 2 * (group - pairs)) & (group >= pairs)
        )
    pixels = lanes[:per_step].astype(jnp.float32) - centre
    for pair in range(pairs):
        stretch = sent(facts, rows == 2 * pair + 1)
        offset = sent(facts, rows == 2 * pairs + 2 * pair + 1)
        source = (1.0 + stretch) * pixels + centre + offset
        near = jnp.round(source)
        x = source - near
        near_ref[pair] = near
        whole, third = math.pi * x, (math.pi / 3.0) * x
        whole_sinc = series(whole * whole, 8, 1)
        third_sinc = series(third * third, 8, 1)
        third_cos = series(third * third, 8, 0)
        for k in range(-3, 4):
            if k == 0:
                value = whole_sinc * third_sinc
            else:
                angle = math.pi * k / 3.0
                slow = third_sinc * third * math.cos(angle) - third_cos * math.sin(angle)
                far = x - k
                value = ((-1.0) ** k * 3.0 / math.pi**2) * whole_sinc * whole * slow / (far * far)
                value = jnp.where(jnp.abs(far) < 3.0, value, 0.0)
            taps_ref[k + 3, pair] = value

    numbers = rows.astype(jnp.bfloat16)

    def build(m):
        stretch = spread_ref[0, pl.ds(m, 1), :]
        offset = spread_ref[1, pl.ds(m, 1), :]
        x = (1.0 + stretch) * place_ref[0] + offset - place_ref[1]
        square = x * x * (math.pi / 3.0) ** 2
        power = series(square, 10, 1)
        power = power * power
        value = power * (1.0 - (4.0 / 3.0) * power * square)
        value = jnp.where(jnp.abs(x) < 3.0, value, 0.0)
        for part in range(2):
            slot = m + part * half
            stack, columns = [], []
            for pair in range(pairs):
                index = part * pairs + pair
                one = jnp.where(group == index, value, 0.0)
                shift = (-BAND // 2 - BAND * index) % BS
                turned = pltpu.roll(one, shift, 1, stride=1, stride_axis=0).astype(jnp.bfloat16)
                second_ref[slot, pair] = turned[EDGE:]
                stack.append(turned[:EDGE, :CUT])
                lag = numbers - near_ref[pair, pl.ds(slot, 1), :].astype(jnp.bfloat16)
                column = jnp.zeros((BS, BS), jnp.bfloat16)
                for k in range(7):
                    tap = taps_ref[k, pair, pl.ds(slot, 1), :].astype(jnp.bfloat16)
                    column = jnp.where(lag == jnp.bfloat16(k - 3), tap, column)
                column_ref[slot, pair] = column
                columns.append(column)
            source = jnp.concatenate(
                [block_ref[slot, :CUT, :], block_ref[slot, CUT : 2 * CUT, :]], axis=1
            )
            aims = [aim_ref[(step * per_step + slot) * pairs + pair] for pair in range(pairs)]
            accumulate(total, aims, jnp.concatenate(stack, axis=0), source, columns)

    @pl.loop(0, half // unroll)
    def _(batch):
        for inner in range(unroll):
            build(batch * unroll + inner)

    @pl.when(step == pl.num_programs(0) - 1)
    def _():
        for index, out in enumerate(outs):
            out[...] = total[index * PB_DEV : (index + 1) * PB_DEV].astype(out.dtype)


def upper_warp(aims, table, first, pairs, groups, unroll=2):
    slots = first.shape[0]
    return pl.pallas_call(
        functools.partial(upper_kernel, pairs, unroll),
        grid_spec=pltpu.PrefetchScalarGridSpec(
            num_scalar_prefetch=1,
            grid=(slots // WARP_SLOTS,),
            in_specs=[
                pl.BlockSpec((WARP_SLOTS, BS), lambda i, _: (i, 0)),
                pl.BlockSpec((WARP_SLOTS,) + first.shape[1:], lambda i, _: (i, 0, 0)),
            ],
            out_specs=[
                pl.BlockSpec((WARP_SLOTS, pairs, BS - EDGE, BS), lambda i, _: (i, 0, 0, 0)),
                pl.BlockSpec((WARP_SLOTS, pairs, BS, BS), lambda i, _: (i, 0, 0, 0)),
            ]
            + [pl.BlockSpec((PB_DEV, 2 * EDGE, BS), lambda i, _: (0, 0, 0))] * groups,
            scratch_shapes=[
                pltpu.VMEM((groups * PB_DEV + 1, 2 * EDGE, BS), jnp.float32),
                pltpu.VMEM((2, WARP_SLOTS // 2, BS), jnp.float32),
                pltpu.VMEM((2, BS, BS), jnp.float32),
                pltpu.VMEM((pairs, WARP_SLOTS, BS), jnp.float32),
                pltpu.VMEM((7, pairs, WARP_SLOTS, BS), jnp.float32),
            ],
        ),
        out_shape=[
            jax.ShapeDtypeStruct((slots, pairs, BS - EDGE, BS), jnp.bfloat16),
            jax.ShapeDtypeStruct((slots, pairs, BS, BS), jnp.bfloat16),
        ]
        + [
            jax.ShapeDtypeStruct(
                (PB_DEV, 2 * EDGE, BS), jnp.float32 if index == 0 else jnp.bfloat16
            )
            for index in range(groups)
        ],
        compiler_params=pltpu.CompilerParams(vmem_limit_bytes=WARP_VMEM),
        cost_estimate=pl.CostEstimate(
            flops=10**10, bytes_accessed=32 * 2**20, transcendentals=0
        ),
        name="upper_warp",
    )(aims, table, first)


def lower_kernel(pairs, aim_ref, first_ref, second_ref, row_ref, column_ref, *refs):
    outs, total = refs[:-1], refs[-1]
    step = pl.program_id(0)
    per_step = column_ref.shape[0]

    @pl.when(step == 0)
    def _():
        total[...] = jnp.zeros_like(total)

    for slot in range(per_step):
        source = jnp.concatenate(
            [
                jnp.concatenate(
                    [
                        first_ref[slot, plane * CUT : (plane + 1) * CUT, :],
                        second_ref[slot, plane * (BS - CUT) : (plane + 1) * (BS - CUT), :],
                    ],
                    axis=0,
                )
                for plane in range(2)
            ],
            axis=1,
        )
        aims = [aim_ref[(step * per_step + slot) * pairs + pair] for pair in range(pairs)]
        rows = row_ref[slot].reshape(pairs * row_ref.shape[2], BS)
        columns = [column_ref[slot, pair] for pair in range(pairs)]
        accumulate(total, aims, rows, source, columns)

    @pl.when(step == pl.num_programs(0) - 1)
    def _():
        for index, out in enumerate(outs):
            out[...] = total[index * PB_DEV : (index + 1) * PB_DEV].astype(out.dtype)


def lower_warp(aims, first, second, row_maps, column_maps, groups):
    slots, pairs, height, _ = row_maps.shape

    def whole(array):
        return pl.BlockSpec(
            (WARP_SLOTS,) + array.shape[1:], lambda i, _: (i,) + (0,) * (array.ndim - 1)
        )

    operands = [first, second, row_maps, column_maps]
    return pl.pallas_call(
        functools.partial(lower_kernel, pairs),
        grid_spec=pltpu.PrefetchScalarGridSpec(
            num_scalar_prefetch=1,
            grid=(slots // WARP_SLOTS,),
            in_specs=[whole(array) for array in operands],
            out_specs=[pl.BlockSpec((PB_DEV, 2 * height, BS), lambda i, _: (0, 0, 0))] * groups,
            scratch_shapes=[pltpu.VMEM((groups * PB_DEV + 1, 2 * height, BS), jnp.float32)],
        ),
        out_shape=[
            jax.ShapeDtypeStruct(
                (PB_DEV, 2 * height, BS), jnp.float32 if index == 0 else jnp.bfloat16
            )
            for index in range(groups)
        ],
        compiler_params=pltpu.CompilerParams(vmem_limit_bytes=WARP_VMEM),
        cost_estimate=pl.CostEstimate(
            flops=6 * 10**9, bytes_accessed=32 * 2**20, transcendentals=0
        ),
        name="lower_warp",
    )(aims, *operands)


def local(
    exposure, variance, pixel_mask, psf_kernel, block_owner, patch_index, pair_stretch, pair_offset
):
    _, rows, columns = exposure.shape
    block_count = columns // BS
    owners = lax.axis_size("sky")
    groups = lax.axis_size("visit")
    slots = owners * CAP
    pairs = patch_index.shape[-1]

    def exchange(array):
        return lax.all_to_all(array, "sky", split_axis=0, concat_axis=0, tiled=True)

    low = jnp.concatenate([exposure[:, rows - HALO :], variance[:, rows - HALO :]], axis=0)
    high = jnp.concatenate([exposure[:, :HALO], variance[:, :HALO]], axis=0)
    top = lax.ppermute(low, "sky", [(i, i + 1) for i in range(owners - 1)])
    bottom = lax.ppermute(high, "sky", [(i + 1, i) for i in range(owners - 1)])

    owner = block_owner.reshape(block_count)
    order = jnp.arange(block_count)
    earlier = (owner[:, None] == owner[None, :]) & (order[None, :] < order[:, None])
    slot = owner * CAP + jnp.sum(earlier, axis=1).astype(jnp.int32)
    facts = jnp.concatenate(
        [
            pair_stretch.reshape(block_count, 2 * pairs).astype(jnp.float32),
            pair_offset.reshape(block_count, 2 * pairs).astype(jnp.float32),
            patch_index.reshape(block_count, pairs).astype(jnp.float32),
            jnp.ones((block_count, BS - 5 * pairs), jnp.float32),
        ],
        axis=1,
    )

    images = [array.reshape(rows, columns) for array in (exposure, variance, pixel_mask)]
    upper_planes = filtered(0, CUT, slots, slot, psf_kernel, *images, top, facts)
    upper_planes, slot, bottom = lax.optimization_barrier((upper_planes, slot, bottom))
    first = exchange(upper_planes)

    lower_planes = filtered(CUT, rows, slots, slot, psf_kernel, *images, bottom)
    first, lower_planes = lax.optimization_barrier((first, lower_planes))
    second = exchange(lower_planes)

    table = first[:, 2 * CUT, :].astype(jnp.float32)
    patch = table[:, 4 * pairs : 5 * pairs].astype(jnp.int32)
    distance = (patch // PB_DEV - lax.axis_index("visit")) % groups
    aims = jnp.where(
        table[:, 5 * pairs : 5 * pairs + 1] > 0.5,
        distance * PB_DEV + patch % PB_DEV,
        groups * PB_DEV,
    )
    aims = aims.reshape(slots * pairs)
    second_maps, column_maps, *upper = upper_warp(aims, table, first, pairs, groups)

    def coadd(sums):
        whole = sums[0]
        for step in range(1, groups):
            ring = [(i, (i + step) % groups) for i in range(groups)]
            whole = whole + lax.ppermute(sums[step], "visit", ring).astype(jnp.float32)
        height = whole.shape[1] // 2
        return whole[:, :height] / jnp.maximum(whole[:, height:], 1.0)

    lower = lower_warp(aims, first, second, second_maps, column_maps, groups)
    return jnp.concatenate([coadd(upper), coadd(lower)], axis=1)


def solution(mesh):
    return jax.shard_map(
        local,
        mesh=mesh,
        in_specs=(
            P("visit", "sky", None),
            P("visit", "sky", None),
            P("visit", "sky", None),
            P("visit", None, None),
            P("visit", "sky", None),
            P("visit", "sky", None, None),
            P("visit", "sky", None, None, None),
            P("visit", "sky", None, None, None),
        ),
        out_specs=P(("visit", "sky"), None, None),
        check_vma=False,
    )
```

time: 133 us -> 126 us (0.947)
  waiting for transfers between devices: 24.9 us -> 42.5 us
  Pallas kernels: 56.9 us -> 39.4 us
  starting transfers between devices: 35.9 us -> 27.5 us
  local copies, waits for them, and re-layouts: 8.46 us -> 11.3 us
    all_to_all x3 -> x2, waiting for transfers between devices: 15.7 us -> 31.3 us  [exchange(): return lax.all_to_all(array, 'sky', split_axis=0, concat_axis=0, tiled=True)]
    pallas_call x3 -> x2, Pallas kernels: 42 us -> 29.1 us  [the longest x1 18.1 us: upper_warp(): pl.pallas_call(functools.partial(upper_kernel, pairs, unroll), grid_spec=...]
    unnamed x14 -> x24, local copies, waits for them, and re-layouts: 2.28 us -> 7.68 us
    all_to_all x3 -> x2, starting transfers between devices: 19.4 us -> 14.6 us  [exchange(): return lax.all_to_all(array, 'sky', split_axis=0, concat_axis=0, tiled=True)]
    pallas_call x2, Pallas kernels: 14.9 us -> 10.4 us  [filtered(): pl.pallas_call(functools.partial(filter_kernel, first, last), grid=(colum...]
    ppermute x6, starting transfers between devices: 13 us -> 10.4 us  [coadd(): whole = whole + lax.ppermute(sums[step], 'visit', ring).astype(jnp.float32)]
    ppermute x6, waiting for transfers between devices: 9.27 us -> 11.2 us  [coadd(): whole = whole + lax.ppermute(sums[step], 'visit', ring).astype(jnp.float32)]
    optimization_barrier x2 -> x0, local copies, waits for them, and re-layouts: 1.62 us -> none  [local(): lax.optimization_barrier((low, high, block_owner, patch_index, pair_stret...]
  transfers between devices with their start and end apart: 11 -> 10, of which waited for: 5 -> 3; matrix products, arithmetic and copies ran while one was open for 3% -> 5% of each run, Pallas kernels for 43% -> 31%
where the time goes in v3:
time: 126 us
  waiting for transfers between devices  42.5 us (34%)
  Pallas kernels  39.4 us (31%)
  starting transfers between devices  27.5 us (22%)
  local copies, waits for them, and re-layouts  11.3 us (9%)
  other arithmetic  4.77 us (4%)
    all_to_all x2, waiting for transfers between devices, exchange(): return lax.all_to_all(array, 'sky', split_axis=0, concat_axis=0, tiled=True)  31.3 us
    pallas_call x1, Pallas kernels, upper_warp(): pl.pallas_call(functools.partial(upper_kernel, pairs, unroll), grid_spec=...  18.1 us
    all_to_all x2, starting transfers between devices, exchange(): return lax.all_to_all(array, 'sky', split_axis=0, concat_axis=0, tiled=True)  14.6 us
    ppermute x6, waiting for transfers between devices, coadd(): whole = whole + lax.ppermute(sums[step], 'visit', ring).astype(jnp.float32)  11.2 us
    pallas_call x1, Pallas kernels, lower_warp(): pl.pallas_call(functools.partial(lower_kernel, pairs), grid_spec=pltpu.Pr...  10.9 us
    ppermute x6, starting transfers between devices, coadd(): whole = whole + lax.ppermute(sums[step], 'visit', ring).astype(jnp.float32)  10.4 us
    pallas_call x2, Pallas kernels, filtered(): pl.pallas_call(functools.partial(filter_kernel, first, last), grid=(colum...  10.4 us
    unnamed x24, local copies, waits for them, and re-layouts  7.68 us
  transfers between devices with their start and end apart: 10, of which 3 were waited for; matrix products, arithmetic and copies ran while one was open for 5% of the time, Pallas kernels for 31%

profile of v3, /device:TPU:0, one launch (start us, length us, event | category | flops | bytes accessed | tf_op | source)
XLA Modules:
  0.0 125.8 jit_solution(17631135909002505720)
XLA Ops:
  0.0 1.3 %fusion.10 = (bf16[1,16,4096]{2,1,0:T(8,128)(2,1)S(1)}, bf16[1,16,4096]{2,1,0:T(8,128)(2,1)S(1)}, bf16[1,16,4096]{2,1,0:T(8,128)(2,1)S(1)}, bf16[1,16,4096]{2,1,0:T(8,128)(2,1)S(1)}) fusion(bf16[1,128,4096]{2,1,0:T(8,128)(2,1)} %param.8, bf16[1,128,4096]{2,1,0:T(8,128)(2,1)} %param.9), kind=kLoop, calls=%fused_computation.34 | loop fusion | bytes 1048576 | tf_op jit(solution)/shard_map/slice | solution.py:394
  1.3 1.3 %collective-permute-start = (bf16[2,16,4096]{2,1,0:T(8,128)(2,1)S(1)}, bf16[2,16,4096]{2,1,0:T(8,128)(2,1)S(1)}, u32[]{:S(2)}, u32[]{:S(2)}) collective-permute-start(bf16[2,16,4096]{2,1,0:T(8,128)(2,1)S(1)} %pad_maximum_fusion.1), channel_id=1, source_target_pairs={{0,1},{1,2},{2,3},{3,4},{4,5},{5,6},{6,7},{7,8},{8,9},{9,10},{10,1... | collective-permute-start | bytes 786440 | tf_op jit(solution)/shard_map/ppermute | solution.py:395
  2.7 1.3 %collective-permute-start.1 = (bf16[2,16,4096]{2,1,0:T(8,128)(2,1)S(1)}, bf16[2,16,4096]{2,1,0:T(8,128)(2,1)S(1)}, u32[]{:S(2)}, u32[]{:S(2)}) collective-permute-start(bf16[2,16,4096]{2,1,0:T(8,128)(2,1)S(1)} %pad_maximum_fusion.2), channel_id=1, source_target_pairs={{1,0},{2,1},{3,2},{4,3},{5,4},{6,5},{7,6},{8,7},{9,8},{10,9},{11,1... | collective-permute-start | bytes 786440 | tf_op jit(solution)/shard_map/ppermute | solution.py:396
  6.4 0.9 convert_reduce_fusion
  8.0 1.6 %copy-done.3 = s32[1,128,4096]{2,1,0:T(8,128)S(1)} copy-done((s32[1,128,4096]{2,1,0:T(8,128)S(1)}, s32[1,128,4096]{2,1,0:T(8,128)}, u32[]{:S(2)}) %copy-start.3) | copy-done | bytes 2097176
  10.3 5.6 %filter.2 = bf16[64,176,128]{2,1,0:T(8,128)(2,1)S(1)} custom-call(s32[32]{0:T(128)S(1)} %multiply_add_fusion.slot_ref, bf16[1,2,21]{2,1,0:T(2,128)(2,1)S(1)} %copy-done.6, bf16[128,4096]{1,0:T(8,128)(2,1)S(1)} %bitcast.12, bf16[128,4096]{1,0:T(8,128)(2,1)S(1)} %bitcast.13, bf16[128,4096]{1,0:T(8,128)(2,1)S(1)} %bitcast.14, bf16[128,4096]{1,0:T(8,128)(2,1)S(1)} %bitcast.18, ...), custom_call_target="tpu_custom_call" | custom-call | flops 2000000000 | bytes 16777216 | tf_op jit(solution)/shard_map/filter/pallas_call | solution.py:137
  15.8 1.6 %copy-done.2 = bf16[64,176,128]{2,1,0:T(8,128)(2,1)} copy-done((bf16[64,176,128]{2,1,0:T(8,128)(2,1)}, bf16[64,176,128]{2,1,0:T(8,128)(2,1)S(1)}, u32[]{:S(2)}) %copy-start.2) | copy-done | bytes 2883608
  17.4 10.6 %all-to-all-start = ((bf16[64,176,128]{2,1,0:T(8,128)(2,1)}), bf16[64,176,128]{2,1,0:T(8,128)(2,1)}, u32[]{:S(2)}, u32[]{:S(2)}) async-start(bf16[64,176,128]{2,1,0:T(8,128)(2,1)} %copy-done.2), calls=%async_computation | async-start | bytes 5767168 | tf_op jit(solution)/shard_map/all_to_all | solution.py:391
  28.0 1.6 %copy-done.4 = s32[1,128,4096]{2,1,0:T(8,128)S(1)} copy-done((s32[1,128,4096]{2,1,0:T(8,128)S(1)}, s32[1,128,4096]{2,1,0:T(8,128)}, u32[]{:S(2)}) %copy-start.4) | copy-done | bytes 2097176
  29.6 4.8 %filter.3 = bf16[64,96,128]{2,1,0:T(8,128)(2,1)S(1)} custom-call(s32[32]{0:T(128)S(1)} %multiply_add_fusion.slot_ref, bf16[1,2,21]{2,1,0:T(2,128)(2,1)S(1)} %copy-done.7, bf16[128,4096]{1,0:T(8,128)(2,1)S(1)} %bitcast.15, bf16[128,4096]{1,0:T(8,128)(2,1)S(1)} %bitcast.16, bf16[128,4096]{1,0:T(8,128)(2,1)S(1)} %bitcast.17, bf16[128,4096]{1,0:T(8,128)(2,1)S(1)} %bitcast.21, ...), custom_call_target="tpu_custom_call" | custom-call | flops 2000000000 | bytes 16777216 | tf_op jit(solution)/shard_map/filter/pallas_call | solution.py:137
  34.4 1.1 copy-done.5
  35.6 31.3 %all-to-all-done.block_ref.first_ref = bf16[64,176,128]{2,1,0:T(8,128)(2,1)} async-done(((bf16[64,176,128]{2,1,0:T(8,128)(2,1)}), bf16[64,176,128]{2,1,0:T(8,128)(2,1)}, u32[]{:S(2)}, u32[]{:S(2)}) %all-to-all-start) | async-done | bytes 2883616 | tf_op jit(solution)/shard_map/all_to_all | solution.py:391
  66.9 4.0 %all-to-all-start.1 = ((bf16[64,96,128]{2,1,0:T(8,128)(2,1)}), bf16[64,96,128]{2,1,0:T(8,128)(2,1)S(1)}, u32[]{:S(2)}, u32[]{:S(2)}) async-start(bf16[64,96,128]{2,1,0:T(8,128)(2,1)} %copy-done.5), calls=%async_computation.1 | async-start | bytes 3145728 | tf_op jit(solution)/shard_map/all_to_all | solution.py:391
  70.8 0.9 slice_convert_fusion.1
  72.8 18.1 %upper_warp.1 = (bf16[64,4,64,128]{3,2,1,0:T(8,128)(2,1)}, bf16[64,4,128,128]{3,2,1,0:T(8,128)(2,1)}, f32[8,128,128]{2,1,0:T(8,128)}, bf16[8,128,128]{2,1,0:T(8,...) custom-call(s32[256]{0:T(256)} %reshape.31.aim_ref, f32[64,128]{1,0:T(8,128)} %bitcast.28, ...), custom_call_target="tpu_custom_call" | custom-call | flops 10000000000 | bytes 33554432 | tf_op jit(solution)/shard_map/upper_warp/pallas_call | solution.py:274
  91.0 2.0 %collective-permute-start.2 = (bf16[8,128,128]{2,1,0:T(8,128)(2,1)}, bf16[8,128,128]{2,1,0:T(8,128)(2,1)S(1)}, u32[]{:S(2)}, u32[]{:S(2)}) collective-permute-start(bf16[8,128,128]{2,1,0:T(8,128)(2,1)} %get-tuple-element.25), channel_id=1, source_target_pairs={{0,32},{32,64},{64,96},{96,0},{1,33},{33,65},{65,97},{97,1},{2,34}... | collective-permute-start | bytes 786440 | tf_op jit(solution)/shard_map/ppermute | solution.py:436
  92.9 3.6 %collective-permute-start.3 = (bf16[8,128,128]{2,1,0:T(8,128)(2,1)}, bf16[8,128,128]{2,1,0:T(8,128)(2,1)S(1)}, u32[]{:S(2)}, u32[]{:S(2)}) collective-permute-start(bf16[8,128,128]{2,1,0:T(8,128)(2,1)} %get-tuple-element.26), channel_id=1, source_target_pairs={{0,64},{32,96},{64,0},{96,32},{1,65},{33,97},{65,1},{97,33},{2,66}... | collective-permute-start | bytes 786440 | tf_op jit(solution)/shard_map/ppermute | solution.py:436
  96.5 1.0 collective-permute-start.4
  97.5 1.1 copy-done.8
  98.7 10.9 %lower_warp.1 = (f32[8,128,128]{2,1,0:T(8,128)}, bf16[8,128,128]{2,1,0:T(8,128)(2,1)}, bf16[8,128,128]{2,1,0:T(8,128)(2,1)}, bf16[8,128,128]{2,1,0:T(8,128)(2,1)}) custom-call(s32[256]{0:T(256)} %reshape.31.aim_ref, bf16[64,176,128]{2,1,0:T(8,128)(2,1)} %all-to-all-done.block_ref.first_ref, bf16[64,96,128]{2,1,0:T(8,128)(2,1)} %copy-done.8, ...), custom_call_target="tpu_custom_call" | custom-call | flops 6000000000 | bytes 33554432 | tf_op jit(solution)/shard_map/lower_warp/pallas_call | solution.py:357
  109.6 1.0 collective-permute-start.5
  110.6 1.7 %collective-permute-start.6 = (bf16[8,128,128]{2,1,0:T(8,128)(2,1)}, bf16[8,128,128]{2,1,0:T(8,128)(2,1)S(1)}, u32[]{:S(2)}, u32[]{:S(2)}) collective-permute-start(bf16[8,128,128]{2,1,0:T(8,128)(2,1)} %get-tuple-element.33), channel_id=1, source_target_pairs={{0,64},{32,96},{64,0},{96,32},{1,65},{33,97},{65,1},{97,33},{2,66}... | collective-permute-start | bytes 786440 | tf_op jit(solution)/shard_map/ppermute | solution.py:436
  112.4 1.0 collective-permute-start.7
  113.6 10.6 %collective-permute-done.5 = bf16[8,128,128]{2,1,0:T(8,128)(2,1)S(1)} collective-permute-done((bf16[8,128,128]{2,1,0:T(8,128)(2,1)}, bf16[8,128,128]{2,1,0:T(8,128)(2,1)S(1)}, u32[]{:S(2)}, u32[]{:S(2)}) %collective-permute-start.5) | collective-permute-done | bytes 262176 | tf_op jit(solution)/shard_map/ppermute | solution.py:436
  (45 shorter events, 6.6 us)
Async XLA Ops:
  0.0 8.0 %copy-start = (bf16[1,128,4096]{2,1,0:T(8,128)(2,1)S(1)}, bf16[1,128,4096]{2,1,0:T(8,128)(2,1)}, u32[]{:S(2)}) copy-start(bf16[1,128,4096]{2,1,0:T(8,128)(2,1)} %param.8) | copy-start | bytes 3145732
  0.0 8.0 %copy-start.1 = (bf16[1,128,4096]{2,1,0:T(8,128)(2,1)S(1)}, bf16[1,128,4096]{2,1,0:T(8,128)(2,1)}, u32[]{:S(2)}) copy-start(bf16[1,128,4096]{2,1,0:T(8,128)(2,1)} %param.9) | copy-start | bytes 3145732
  1.3 6.7 %collective-permute-start = (bf16[2,16,4096]{2,1,0:T(8,128)(2,1)S(1)}, bf16[2,16,4096]{2,1,0:T(8,128)(2,1)S(1)}, u32[]{:S(2)}, u32[]{:S(2)}) collective-permute-start(bf16[2,16,4096]{2,1,0:T(8,128)(2,1)S(1)} %pad_maximum_fusion.1), channel_id=1, source_target_pairs={{0,1},{1,2},{2,3},{3,4},{4,5},{5,6},{6,7},{7,8},{8,9},{9,10},{10,1... | collective-permute-start | bytes 786440 | tf_op jit(solution)/shard_map/ppermute | solution.py:395
  2.7 14.7 %collective-permute-start.1 = (bf16[2,16,4096]{2,1,0:T(8,128)(2,1)S(1)}, bf16[2,16,4096]{2,1,0:T(8,128)(2,1)S(1)}, u32[]{:S(2)}, u32[]{:S(2)}) collective-permute-start(bf16[2,16,4096]{2,1,0:T(8,128)(2,1)S(1)} %pad_maximum_fusion.2), channel_id=1, source_target_pairs={{1,0},{2,1},{3,2},{4,3},{5,4},{6,5},{7,6},{8,7},{9,8},{10,9},{11,1... | collective-permute-start | bytes 786440 | tf_op jit(solution)/shard_map/ppermute | solution.py:396
  8.0 1.6 %copy-start.3 = (s32[1,128,4096]{2,1,0:T(8,128)S(1)}, s32[1,128,4096]{2,1,0:T(8,128)}, u32[]{:S(2)}) copy-start(s32[1,128,4096]{2,1,0:T(8,128)} %param.10) | copy-start | bytes 6291460
  9.6 0.7 copy-start.6
  15.8 1.6 %copy-start.2 = (bf16[64,176,128]{2,1,0:T(8,128)(2,1)}, bf16[64,176,128]{2,1,0:T(8,128)(2,1)S(1)}, u32[]{:S(2)}) copy-start(bf16[64,176,128]{2,1,0:T(8,128)(2,1)S(1)} %filter.2) | copy-start | bytes 8650756
  17.4 10.6 %copy-start.7 = (bf16[1,2,21]{2,1,0:T(2,128)(2,1)S(1)}, bf16[1,2,21]{2,1,0:T(2,128)(2,1)}, u32[]{:S(2)}) copy-start(bf16[1,2,21]{2,1,0:T(2,128)(2,1)} %taps_ref.3) | copy-start | bytes 256
  17.4 49.5 %all-to-all-start = ((bf16[64,176,128]{2,1,0:T(8,128)(2,1)}), bf16[64,176,128]{2,1,0:T(8,128)(2,1)}, u32[]{:S(2)}, u32[]{:S(2)}) async-start(bf16[64,176,128]{2,1,0:T(8,128)(2,1)} %copy-done.2), calls=%async_computation | async-start | bytes 5767168 | tf_op jit(solution)/shard_map/all_to_all | solution.py:391
  28.0 1.6 %copy-start.4 = (s32[1,128,4096]{2,1,0:T(8,128)S(1)}, s32[1,128,4096]{2,1,0:T(8,128)}, u32[]{:S(2)}) copy-start(s32[1,128,4096]{2,1,0:T(8,128)} %param.10) | copy-start | bytes 6291460
  34.4 1.1 copy-start.5
  66.9 30.7 %all-to-all-start.1 = ((bf16[64,96,128]{2,1,0:T(8,128)(2,1)}), bf16[64,96,128]{2,1,0:T(8,128)(2,1)S(1)}, u32[]{:S(2)}, u32[]{:S(2)}) async-start(bf16[64,96,128]{2,1,0:T(8,128)(2,1)} %copy-done.5), calls=%async_computation.1 | async-start | bytes 3145728 | tf_op jit(solution)/shard_map/all_to_all | solution.py:391
  71.8 1.0 copy-start.11
  91.0 21.4 %collective-permute-start.2 = (bf16[8,128,128]{2,1,0:T(8,128)(2,1)}, bf16[8,128,128]{2,1,0:T(8,128)(2,1)S(1)}, u32[]{:S(2)}, u32[]{:S(2)}) collective-permute-start(bf16[8,128,128]{2,1,0:T(8,128)(2,1)} %get-tuple-element.25), channel_id=1, source_target_pairs={{0,32},{32,64},{64,96},{96,0},{1,33},{33,65},{65,97},{97,1},{2,34}... | collective-permute-start | bytes 786440 | tf_op jit(solution)/shard_map/ppermute | solution.py:436
  92.9 20.5 %collective-permute-start.3 = (bf16[8,128,128]{2,1,0:T(8,128)(2,1)}, bf16[8,128,128]{2,1,0:T(8,128)(2,1)S(1)}, u32[]{:S(2)}, u32[]{:S(2)}) collective-permute-start(bf16[8,128,128]{2,1,0:T(8,128)(2,1)} %get-tuple-element.26), channel_id=1, source_target_pairs={{0,64},{32,96},{64,0},{96,32},{1,65},{33,97},{65,1},{97,33},{2,66}... | collective-permute-start | bytes 786440 | tf_op jit(solution)/shard_map/ppermute | solution.py:436
  96.5 16.9 %collective-permute-start.4 = (bf16[8,128,128]{2,1,0:T(8,128)(2,1)}, bf16[8,128,128]{2,1,0:T(8,128)(2,1)S(1)}, u32[]{:S(2)}, u32[]{:S(2)}) collective-permute-start(bf16[8,128,128]{2,1,0:T(8,128)(2,1)} %get-tuple-element.27), channel_id=1, source_target_pairs={{0,96},{32,0},{64,32},{96,64},{1,97},{33,1},{65,33},{97,65},{2,98}... | collective-permute-start | bytes 786440 | tf_op jit(solution)/shard_map/ppermute | solution.py:436
  97.5 1.1 copy-start.8
  98.7 14.7 %copy-start.9 = (f32[8,128,128]{2,1,0:T(8,128)S(1)}, f32[8,128,128]{2,1,0:T(8,128)}, u32[]{:S(2)}) copy-start(f32[8,128,128]{2,1,0:T(8,128)} %get-tuple-element.24) | copy-start | bytes 1572868
  109.6 15.2 %copy-start.10 = (f32[8,128,128]{2,1,0:T(8,128)S(1)}, f32[8,128,128]{2,1,0:T(8,128)}, u32[]{:S(2)}) copy-start(f32[8,128,128]{2,1,0:T(8,128)} %get-tuple-element.31) | copy-start | bytes 1572868
  109.6 14.6 %collective-permute-start.5 = (bf16[8,128,128]{2,1,0:T(8,128)(2,1)}, bf16[8,128,128]{2,1,0:T(8,128)(2,1)S(1)}, u32[]{:S(2)}, u32[]{:S(2)}) collective-permute-start(bf16[8,128,128]{2,1,0:T(8,128)(2,1)} %get-tuple-element.32), channel_id=1, source_target_pairs={{0,32},{32,64},{64,96},{96,0},{1,33},{33,65},{65,97},{97,1},{2,34}... | collective-permute-start | bytes 786440 | tf_op jit(solution)/shard_map/ppermute | solution.py:436
  110.6 13.6 %collective-permute-start.6 = (bf16[8,128,128]{2,1,0:T(8,128)(2,1)}, bf16[8,128,128]{2,1,0:T(8,128)(2,1)S(1)}, u32[]{:S(2)}, u32[]{:S(2)}) collective-permute-start(bf16[8,128,128]{2,1,0:T(8,128)(2,1)} %get-tuple-element.33), channel_id=1, source_target_pairs={{0,64},{32,96},{64,0},{96,32},{1,65},{33,97},{65,1},{97,33},{2,66}... | collective-permute-start | bytes 786440 | tf_op jit(solution)/shard_map/ppermute | solution.py:436
  112.4 12.4 %collective-permute-start.7 = (bf16[8,128,128]{2,1,0:T(8,128)(2,1)}, bf16[8,128,128]{2,1,0:T(8,128)(2,1)S(1)}, u32[]{:S(2)}, u32[]{:S(2)}) collective-permute-start(bf16[8,128,128]{2,1,0:T(8,128)(2,1)} %get-tuple-element.34), channel_id=1, source_target_pairs={{0,96},{32,0},{64,32},{96,64},{1,97},{33,1},{65,33},{97,65},{2,98}... | collective-permute-start | bytes 786440 | tf_op jit(solution)/shard_map/ppermute | solution.py:436

commit v4 on v3

v4 whole, which is shorter than its diff:
```python
import functools
import math

import jax
import jax.numpy as jnp
from jax import lax
from jax.experimental import pallas as pl
from jax.experimental.pallas import tpu as pltpu
from jax.sharding import PartitionSpec as P

BS = 128
HALO = 16
BAND = 16
CAP = 2
PB_DEV = 8
CUT = 80
EDGE = CUT - 16
REACH = EDGE - 16
FACTS = 16
FILTER_COLUMNS = 2048
UNROLL = 2
UPPER_PARTS = 4
FILTER_VMEM = 60 * 1024 * 1024
UPPER_VMEM = 60 * 1024 * 1024
LOWER_VMEM = 58 * 1024 * 1024
LOWER_PARTS = 4


def toeplitz(rows, columns, shift, tap):
    lag = lax.broadcasted_iota(jnp.int32, (rows, columns), 0) - lax.broadcasted_iota(jnp.int32, (rows, columns), 1) + shift
    matrix = jnp.zeros((rows, columns), jnp.float32)
    for index, value in enumerate(tap):
        matrix = jnp.where(lag == index, value, matrix)
    return matrix.astype(jnp.bfloat16)

def filter_kernel(span, chunk, side, owners, owner_ref, taps_ref, *refs):
    exposure_ref, variance_ref, mask_ref, halo_ref = refs[:4]
    pair_refs, out = refs[4:-14], refs[-14]
    framed, usable_ref, across_ref, down_ref, staged, empty_ref, facts_ref = refs[-13:-6]
    slot_ref, count_ref, here, near, done, cleared = refs[-6:]
    (first, last), (chunk_first, chunk_last) = span, chunk
    rows, columns = mask_ref.shape
    height, chunk_height = last - first, chunk_last - chunk_first
    tall = height + 2 * HALO
    wide = 2 * BS
    half = (taps_ref.shape[-1] - 1) // 2
    parts = here.shape[1]
    part_columns = columns // parts

    own_from, own_to = max(first - HALO, 0), min(last + HALO, rows)
    own_at, halo_at = (HALO, 0) if side == "top" else (0, own_to - own_from)

    def fetched(part):
        lanes = pl.ds(part * part_columns, part_columns)
        inner = pl.ds(BS + part * part_columns, part_columns)
        own, placed = pl.ds(own_from, own_to - own_from), pl.ds(own_at, own_to - own_from)
        kept = pl.ds(first, height)
        return [
            pltpu.make_async_copy(
                exposure_ref.at[own, lanes], framed.at[0, placed, inner], here.at[0, part]
            ),
            pltpu.make_async_copy(
                variance_ref.at[own, lanes], framed.at[1, placed, inner], here.at[1, part]
            ),
            pltpu.make_async_copy(
                mask_ref.at[kept, lanes], usable_ref.at[:, lanes], here.at[2, part]
            ),
        ]

    halos = [
        pltpu.make_async_copy(
            halo_ref.at[plane],
            framed.at[plane, pl.ds(halo_at, HALO), pl.ds(BS, columns)],
            near.at[plane],
        )
        for plane in range(2)
    ]
    for copy in halos:
        copy.start()
    for part in range(parts):
        for copy in fetched(part):
            copy.start()
    if pair_refs:
        empty_ref[...] = jnp.zeros(empty_ref.shape, jnp.bfloat16)
        clear = pltpu.make_async_copy(
            empty_ref, out.at[:, pl.ds(2 * chunk_height, FACTS), :], cleared.at[0]
        )
        clear.start()

    for owner in range(count_ref.shape[0]):
        count_ref[owner] = 0
    for block in range(slot_ref.shape[0]):
        owner = owner_ref[0, 0, block]
        rank = count_ref[owner]
        slot_ref[block] = owner * CAP + rank
        count_ref[owner] = rank + 1

    if pair_refs:
        stretch_ref, offset_ref, patch_ref = pair_refs
        pairs, blocks = patch_ref.shape
        facts_ref[...] = jnp.ones(facts_ref.shape, jnp.float32)
        for pair in range(pairs):
            for base, ref in ((0, stretch_ref), (2 * pairs, offset_ref)):
                facts_ref[base + 2 * pair : base + 2 * pair + 2, :blocks] = ref[pair].astype(
                    jnp.float32
                )
        facts_ref[4 * pairs : 5 * pairs, :blocks] = patch_ref[...].astype(jnp.float32)
        facts_ref[...] = facts_ref[...].T

    margin = jnp.zeros((tall, BS), jnp.bfloat16)
    empty = jnp.zeros((BS, BS), jnp.bfloat16)
    values = taps_ref[0].astype(jnp.float32)
    for plane in range(2):
        framed[plane, :, :BS] = margin
        framed[plane, :, BS + columns :] = margin
        taps = [
            [values[way : way + 1, tap : tap + 1] for tap in range(taps_ref.shape[-1])]
            for way in range(2)
        ]
        if plane == 1:
            taps = [[tap * tap for tap in way] for way in taps]
        left, middle, right = (toeplitz(BS, BS, half + by * BS, taps[0]) for by in (-1, 0, 1))
        pattern = ((left, empty), (middle, left), (right, middle), (empty, right))
        for row, blocks in enumerate(pattern):
            across_ref[plane, row * BS : (row + 1) * BS, :BS] = blocks[0]
            across_ref[plane, row * BS : (row + 1) * BS, BS:] = blocks[1]
        down_ref[plane] = toeplitz(height, tall, half + HALO, taps[1][::-1])

    for copy in halos:
        copy.wait()
    outermost = 0 if side == "top" else owners - 1
    inner = lax.axis_index("sky") != outermost
    for plane in range(2):
        halo = framed[plane, halo_at : halo_at + HALO, :]
        framed[plane, halo_at : halo_at + HALO, :] = jnp.where(inner, halo, jnp.zeros_like(halo))
    for copy in fetched(0):
        copy.wait()
    tiles = part_columns // wide
    sent = []
    for part in range(parts):
        if part + 1 < parts:
            for copy in fetched(part + 1):
                copy.wait()
        base = part * part_columns
        matched = []
        for plane in range(2):
            stack = jnp.concatenate(
                [
                    framed[plane, :, base + tile * wide : base + tile * wide + 4 * BS]
                    for tile in range(tiles)
                ],
                axis=0,
            )
            passed = jnp.dot(
                stack, across_ref[plane], preferred_element_type=jnp.float32
            ).astype(jnp.bfloat16)
            matched.append(
                [
                    jnp.dot(
                        down_ref[plane],
                        passed[tile * tall : (tile + 1) * tall],
                        preferred_element_type=jnp.float32,
                    )
                    for tile in range(tiles)
                ]
            )
        for tile in range(tiles):
            lanes = slice(base + tile * wide, base + (tile + 1) * wide)
            weight = usable_ref[:, lanes].astype(jnp.float32) / matched[1][tile]
            weighted = (weight * matched[0][tile]).astype(jnp.bfloat16)
            weight = weight.astype(jnp.bfloat16)
            for block in range(2):
                index = (part * tiles + tile) * 2 + block
                lanes = slice(block * BS, (block + 1) * BS)
                staged[index, :height, :] = weighted[:, lanes]
                staged[index, height : 2 * height, :] = weight[:, lanes]
                if pair_refs:
                    row = jnp.broadcast_to(facts_ref[index : index + 1, :], (FACTS, BS))
                    staged[index, 2 * height :, :] = row.astype(jnp.bfloat16)
        if pair_refs and part == 0:
            clear.wait()
        at = first - chunk_first
        pieces = [(0, height, at), (height, height, chunk_height + at)]
        if pair_refs:
            pieces[1] = (height, height + FACTS, chunk_height + at)
        for index in range(part * tiles * 2, (part + 1) * tiles * 2):
            for piece, (begin, count, to) in enumerate(pieces):
                copy = pltpu.make_async_copy(
                    staged.at[index, pl.ds(begin, count), :],
                    out.at[slot_ref[index], pl.ds(to, count), :],
                    done.at[index, piece],
                )
                copy.start()
                sent.append(copy)
    for copy in sent:
        copy.wait()


def filtered(span, chunk, owners, owner, taps, images, side, halo, facts=()):
    rows, columns = images[2].shape
    height = span[1] - span[0]
    tall = 2 * (chunk[1] - chunk[0]) + (0 if chunk[0] else FACTS)
    slots = owners * CAP
    blocks = columns // BS
    parts = columns // FILTER_COLUMNS
    smem = pl.BlockSpec(memory_space=pltpu.SMEM)
    hbm = pl.BlockSpec(memory_space=pltpu.HBM)

    def whole(array):
        return pl.BlockSpec(array.shape, lambda i: (0,) * array.ndim)

    operands = [owner, taps, *images, halo, *facts]
    specs = [smem, whole(taps), hbm, hbm, hbm, pl.BlockSpec(memory_space=pl.ANY)]
    specs += [whole(fact) for fact in facts]
    return pl.pallas_call(
        functools.partial(filter_kernel, span, chunk, side, owners),
        grid=(1,),
        out_shape=jax.ShapeDtypeStruct((slots, tall, BS), jnp.bfloat16),
        in_specs=specs,
        out_specs=hbm,
        scratch_shapes=[
            pltpu.VMEM((2, height + 2 * HALO, columns + 2 * BS), jnp.bfloat16),
            pltpu.VMEM((height, columns), jnp.int32),
            pltpu.VMEM((2, 4 * BS, 2 * BS), jnp.bfloat16),
            pltpu.VMEM((2, height, height + 2 * HALO), jnp.bfloat16),
            pltpu.VMEM((blocks, 2 * height + FACTS, BS), jnp.bfloat16),
            pltpu.VMEM((slots, FACTS, BS), jnp.bfloat16),
            pltpu.VMEM((BS, BS), jnp.float32),
            pltpu.SMEM((blocks,), jnp.int32),
            pltpu.SMEM((owners,), jnp.int32),
            pltpu.SemaphoreType.DMA((3, parts)),
            pltpu.SemaphoreType.DMA((2,)),
            pltpu.SemaphoreType.DMA((blocks, 2)),
            pltpu.SemaphoreType.DMA((1,)),
        ],
        compiler_params=pltpu.CompilerParams(vmem_limit_bytes=FILTER_VMEM),
        cost_estimate=pl.CostEstimate(
            flops=2 * 10**9, bytes_accessed=16 * 2**20, transcendentals=0
        ),
        name="filter",
    )(*operands)


def series(square, count, odd):
    total = jnp.zeros_like(square)
    for term in range(count, -1, -1):
        total = total * square + (-1.0) ** term / math.factorial(2 * term + odd)
    return total


def accumulate(total, aims, rows, source, columns):
    height = rows.shape[0] // len(columns)
    half_warp = jnp.dot(rows, source, preferred_element_type=jnp.float32).astype(jnp.bfloat16)
    for pair, column in enumerate(columns):
        mine = half_warp[pair * height : (pair + 1) * height]
        both = jnp.concatenate([mine[:, :BS], mine[:, BS:]], axis=0)
        total[aims[pair]] += jnp.dot(both, column, preferred_element_type=jnp.float32)


def upper_kernel(pairs, aim_ref, table_ref, first_ref, second_out, column_out, *refs):
    outs, (block_ref, second_ref, column_ref, arrived, left) = refs[:-10], refs[-10:-5]
    total, spread_ref, place_ref, near_ref, taps_ref = refs[-5:]
    parts = arrived.shape[1]
    half = table_ref.shape[0] // 2
    per_part = half // parts
    lanes = lax.broadcasted_iota(jnp.int32, (BS, BS), 1)
    rows = lax.broadcasted_iota(jnp.int32, (BS, BS), 0)
    group = lanes // BAND
    centre = (BS - 1) / 2.0

    def fetched(part):
        return [
            pltpu.make_async_copy(
                first_ref.at[pl.ds(base + part * per_part, per_part), pl.ds(0, 2 * CUT), :],
                block_ref.at[pl.ds(base + part * per_part, per_part)],
                arrived.at[index, part],
            )
            for index, base in enumerate((0, half))
        ]

    def returned(part):
        return [
            pltpu.make_async_copy(
                kept.at[pl.ds(base + part * per_part, per_part)],
                out.at[pl.ds(base + part * per_part, per_part)],
                left.at[2 * kind + index, part],
            )
            for index, base in enumerate((0, half))
            for kind, (kept, out) in enumerate(((second_ref, second_out), (column_ref, column_out)))
        ]

    for part in range(parts):
        for copy in fetched(part):
            copy.start()
    total[...] = jnp.zeros_like(total)
    target = rows + lanes % BAND - BAND // 2
    inside = (target >= 0) & (target < BS)
    place_ref[0] = rows.astype(jnp.float32) - centre
    place_ref[1] = jnp.where(inside, target.astype(jnp.float32) - centre, 1e3)

    facts = table_ref[...].astype(jnp.bfloat16)

    def sent(values, chosen):
        return jnp.dot(values, chosen.astype(jnp.bfloat16), preferred_element_type=jnp.float32)

    for kind in range(2):
        field = 2 * pairs * kind
        spread_ref[kind] = sent(
            facts[:half], (rows == field + 2 * group) & (group < pairs)
        ) + sent(facts[half:], (rows == field + 2 * (group - pairs)) & (group >= pairs))
    pixels = lanes[: 2 * half].astype(jnp.float32) - centre
    for pair in range(pairs):
        stretch = sent(facts, rows == 2 * pair + 1)
        offset = sent(facts, rows == 2 * pairs + 2 * pair + 1)
        source = (1.0 + stretch) * pixels + centre + offset
        near = jnp.round(source)
        x = source - near
        near_ref[pair] = near
        whole, third = math.pi * x, (math.pi / 3.0) * x
        whole_sinc = series(whole * whole, 8, 1)
        third_sinc = series(third * third, 8, 1)
        third_cos = series(third * third, 8, 0)
        for k in range(-3, 4):
            if k == 0:
                value = whole_sinc * third_sinc
            else:
                angle = math.pi * k / 3.0
                slow = third_sinc * third * math.cos(angle) - third_cos * math.sin(angle)
                far = x - k
                value = ((-1.0) ** k * 3.0 / math.pi**2) * whole_sinc * whole * slow / (far * far)
                value = jnp.where(jnp.abs(far) < 3.0, value, 0.0)
            taps_ref[k + 3, pair] = value

    numbers = rows.astype(jnp.bfloat16)

    def build(m):
        stretch = spread_ref[0, pl.ds(m, 1), :]
        offset = spread_ref[1, pl.ds(m, 1), :]
        x = (1.0 + stretch) * place_ref[0] + offset - place_ref[1]
        square = x * x * (math.pi / 3.0) ** 2
        power = series(square, 10, 1)
        power = power * power
        value = power * (1.0 - (4.0 / 3.0) * power * square)
        value = jnp.where(jnp.abs(x) < 3.0, value, 0.0)
        for which in range(2):
            slot = m + which * half
            stack, columns = [], []
            for pair in range(pairs):
                index = which * pairs + pair
                one = jnp.where(group == index, value, 0.0)
                shift = -BAND // 2 - BAND * index
                upper = pltpu.roll(one[:EDGE], shift % BS, 1, stride=1, stride_axis=0)
                lower = pltpu.roll(
                    one[EDGE:], (shift + EDGE - REACH) % BS, 1, stride=1, stride_axis=0
                )
                second_ref[slot, pair] = lower.astype(jnp.bfloat16)
                stack.append(upper.astype(jnp.bfloat16)[:, :CUT])
                lag = numbers - near_ref[pair, pl.ds(slot, 1), :].astype(jnp.bfloat16)
                column = jnp.zeros((BS, BS), jnp.bfloat16)
                for k in range(7):
                    tap = taps_ref[k, pair, pl.ds(slot, 1), :].astype(jnp.bfloat16)
                    column = jnp.where(lag == jnp.bfloat16(k - 3), tap, column)
                column_ref[slot, pair] = column
                columns.append(column)
            source = jnp.concatenate(
                [block_ref[slot, :CUT, :], block_ref[slot, CUT : 2 * CUT, :]], axis=1
            )
            aims = [aim_ref[slot * pairs + pair] for pair in range(pairs)]
            accumulate(total, aims, jnp.concatenate(stack, axis=0), source, columns)

    @pl.loop(0, parts)
    def _(part):
        for copy in fetched(part):
            copy.wait()

        @pl.loop(0, per_part // UNROLL)
        def _(batch):
            for inner in range(UNROLL):
                build(part * per_part + batch * UNROLL + inner)

        for copy in returned(part):
            copy.start()

    for index, out in enumerate(outs):
        out[...] = total[index * PB_DEV : (index + 1) * PB_DEV].astype(out.dtype)
    for part in range(parts):
        for copy in returned(part):
            copy.wait()


def upper_warp(aims, table, first, pairs, groups):
    slots = first.shape[0]
    second = jax.ShapeDtypeStruct((slots, pairs, BS - EDGE, BS), jnp.bfloat16)
    column = jax.ShapeDtypeStruct((slots, pairs, BS, BS), jnp.bfloat16)
    hbm = pl.BlockSpec(memory_space=pltpu.HBM)
    return pl.pallas_call(
        functools.partial(upper_kernel, pairs),
        grid=(1,),
        in_specs=[
            pl.BlockSpec(memory_space=pltpu.SMEM),
            pl.BlockSpec(table.shape, lambda i: (0, 0)),
            pl.BlockSpec(memory_space=pl.ANY),
        ],
        out_specs=[hbm, hbm]
        + [pl.BlockSpec((PB_DEV, 2 * EDGE, BS), lambda i: (0, 0, 0))] * groups,
        scratch_shapes=[
            pltpu.VMEM((slots, 2 * CUT, BS), jnp.bfloat16),
            pltpu.VMEM(second.shape, second.dtype),
            pltpu.VMEM(column.shape, column.dtype),
            pltpu.SemaphoreType.DMA((2, UPPER_PARTS)),
            pltpu.SemaphoreType.DMA((4, UPPER_PARTS)),
            pltpu.VMEM((groups * PB_DEV + 1, 2 * EDGE, BS), jnp.float32),
            pltpu.VMEM((2, slots // 2, BS), jnp.float32),
            pltpu.VMEM((2, BS, BS), jnp.float32),
            pltpu.VMEM((pairs, slots, BS), jnp.float32),
            pltpu.VMEM((7, pairs, slots, BS), jnp.float32),
        ],
        out_shape=[second, column]
        + [
            jax.ShapeDtypeStruct(
                (PB_DEV, 2 * EDGE, BS), jnp.float32 if index == 0 else jnp.bfloat16
            )
            for index in range(groups)
        ],
        compiler_params=pltpu.CompilerParams(vmem_limit_bytes=UPPER_VMEM),
        cost_estimate=pl.CostEstimate(
            flops=10**10, bytes_accessed=32 * 2**20, transcendentals=0
        ),
        name="upper_warp",
    )(aims, table, first)


def lower_kernel(pairs, aim_ref, *refs):
    (first, second, row, column), outs = refs[:4], refs[4:-6]
    first_ref, second_ref, row_ref, column_ref, total, arrived = refs[-6:]
    parts = arrived.shape[1]
    per_part = first_ref.shape[0] // parts
    near, far = CUT - REACH, BS - CUT

    def copies(part):
        slots = pl.ds(part * per_part, per_part)
        pieces = [
            (
                first.at[slots, pl.ds(plane * CUT + REACH, near), :],
                first_ref.at[slots, pl.ds(plane * near, near), :],
            )
            for plane in range(2)
        ]
        pieces += [
            (second.at[slots], second_ref.at[slots]),
            (row.at[slots], row_ref.at[slots]),
            (column.at[slots], column_ref.at[slots]),
        ]
        return [
            pltpu.make_async_copy(source, kept, arrived.at[index, part])
            for index, (source, kept) in enumerate(pieces)
        ]

    for part in range(parts):
        for copy in copies(part):
            copy.start()
    total[...] = jnp.zeros_like(total)

    @pl.loop(0, parts)
    def _(part):
        for copy in copies(part):
            copy.wait()
        for inner in range(per_part):
            slot = part * per_part + inner
            source = jnp.concatenate(
                [
                    jnp.concatenate(
                        [
                            first_ref[slot, plane * near : (plane + 1) * near, :],
                            second_ref[slot, plane * far : (plane + 1) * far, :],
                        ],
                        axis=0,
                    )
                    for plane in range(2)
                ],
                axis=1,
            )
            aims = [aim_ref[slot * pairs + pair] for pair in range(pairs)]
            rows = row_ref[slot].reshape(pairs * row_ref.shape[2], BS)[:, : near + far]
            columns = [column_ref[slot, pair] for pair in range(pairs)]
            accumulate(total, aims, rows, source, columns)

    for index, out in enumerate(outs):
        out[...] = total[index * PB_DEV : (index + 1) * PB_DEV].astype(out.dtype)


def lower_warp(aims, first, second, row_maps, column_maps, groups):
    slots, pairs, height, _ = row_maps.shape
    operands = [first, second, row_maps, column_maps]
    return pl.pallas_call(
        functools.partial(lower_kernel, pairs),
        in_specs=[pl.BlockSpec(memory_space=pltpu.SMEM)]
        + [pl.BlockSpec(memory_space=pl.ANY)] * len(operands),
        out_specs=[pl.BlockSpec(memory_space=pltpu.VMEM)] * groups,
        scratch_shapes=[
            pltpu.VMEM((slots, 2 * (CUT - REACH), BS), first.dtype),
            pltpu.VMEM(second.shape, second.dtype),
            pltpu.VMEM(row_maps.shape, row_maps.dtype),
            pltpu.VMEM(column_maps.shape, column_maps.dtype),
            pltpu.VMEM((groups * PB_DEV + 1, 2 * height, BS), jnp.float32),
            pltpu.SemaphoreType.DMA((5, LOWER_PARTS)),
        ],
        out_shape=[
            jax.ShapeDtypeStruct(
                (PB_DEV, 2 * height, BS), jnp.float32 if index == 0 else jnp.bfloat16
            )
            for index in range(groups)
        ],
        compiler_params=pltpu.CompilerParams(vmem_limit_bytes=LOWER_VMEM),
        cost_estimate=pl.CostEstimate(
            flops=6 * 10**9, bytes_accessed=32 * 2**20, transcendentals=0
        ),
        name="lower_warp",
    )(aims, *operands)


def local(
    exposure, variance, pixel_mask, psf_kernel, block_owner, patch_index, pair_stretch, pair_offset
):
    _, rows, columns = exposure.shape
    block_count = columns // BS
    owners = lax.axis_size("sky")
    groups = lax.axis_size("visit")
    slots = owners * CAP
    pairs = patch_index.shape[-1]

    def exchange(array):
        return lax.all_to_all(array, "sky", split_axis=0, concat_axis=0, tiled=True)

    low = jnp.concatenate([exposure[:, rows - HALO :], variance[:, rows - HALO :]], axis=0)
    high = jnp.concatenate([exposure[:, :HALO], variance[:, :HALO]], axis=0)
    top = lax.ppermute(low, "sky", [(i, (i + 1) % owners) for i in range(owners)])
    bottom = lax.ppermute(high, "sky", [((i + 1) % owners, i) for i in range(owners)])

    facts = [
        pair_stretch.transpose(0, 1, 3, 4, 2).reshape(pairs, 2, block_count),
        pair_offset.transpose(0, 1, 3, 4, 2).reshape(pairs, 2, block_count),
        patch_index.transpose(0, 1, 3, 2).reshape(pairs, block_count),
    ]

    images = [array.reshape(rows, columns) for array in (exposure, variance, pixel_mask)]
    common = (owners, block_owner, psf_kernel, images)
    upper_planes = filtered((0, CUT), (0, CUT), *common, "top", top, facts)
    upper_planes, bottom = lax.optimization_barrier((upper_planes, bottom))
    first = exchange(upper_planes)

    lower_planes = filtered((CUT, rows), (CUT, rows), *common, "bottom", bottom)
    first, lower_planes = lax.optimization_barrier((first, lower_planes))
    second = exchange(lower_planes)

    table = first[:, 2 * CUT, :].astype(jnp.float32)
    patch = table[:, 4 * pairs : 5 * pairs].astype(jnp.int32)
    distance = (patch // PB_DEV - lax.axis_index("visit")) % groups
    aims = jnp.where(
        table[:, 5 * pairs : 5 * pairs + 1] > 0.5,
        distance * PB_DEV + patch % PB_DEV,
        groups * PB_DEV,
    )
    aims = aims.reshape(slots * pairs)
    second_maps, column_maps, *upper = upper_warp(aims, table, first, pairs, groups)

    def coadd(sums):
        whole = sums[0]
        for step in (2, 1, 3):
            ring = [(i, (i + step) % groups) for i in range(groups)]
            whole = whole + lax.ppermute(sums[step], "visit", ring).astype(jnp.float32)
        height = whole.shape[1] // 2
        return whole[:, :height] / jnp.maximum(whole[:, height:], 1.0)

    lower = lower_warp(aims, first, second, second_maps, column_maps, groups)
    return jnp.concatenate([coadd(upper), coadd(lower)], axis=1)


def solution(mesh):
    return jax.shard_map(
        local,
        mesh=mesh,
        in_specs=(
            P("visit", "sky", None),
            P("visit", "sky", None),
            P("visit", "sky", None),
            P("visit", None, None),
            P("visit", "sky", None),
            P("visit", "sky", None, None),
            P("visit", "sky", None, None, None),
            P("visit", "sky", None, None, None),
        ),
        out_specs=P(("visit", "sky"), None, None),
        check_vma=False,
    )
```

time: 126 us -> 120 us (0.952); the launches traced: 126 us -> 118 us
  local copies, waits for them, and re-layouts: 11.3 us -> 3.18 us
  other arithmetic: 4.77 us -> 1.52 us
  waiting for transfers between devices: 42.5 us -> 45.7 us
  Pallas kernels: 39.4 us -> 40.7 us
    unnamed x24 -> x12, local copies, waits for them, and re-layouts: 7.68 us -> 1.42 us
    all_to_all x2, starting transfers between devices: 14.6 us -> 8.81 us  [exchange(): return lax.all_to_all(array, 'sky', split_axis=0, concat_axis=0, tiled=True)]
    ppermute x2, waiting for transfers between devices: 0.01 us -> 3.96 us  [the longest x1 3.95 us: local(): lax.ppermute(low, 'sky', [(i, (i + 1) % owners) for i in range(owners)])]
    ppermute x2, starting transfers between devices: 2.6 us -> 5.19 us  [the longest x1 5.12 us: local(): lax.ppermute(high, 'sky', [((i + 1) % owners, i) for i in range(owners)])]
    ppermute x6, starting transfers between devices: 10.4 us -> 12.9 us  [coadd(): whole = whole + lax.ppermute(sums[step], 'visit', ring).astype(jnp.float32)]
    ppermute x6, waiting for transfers between devices: 11.2 us -> 8.98 us  [coadd(): whole = whole + lax.ppermute(sums[step], 'visit', ring).astype(jnp.float32)]
    convert_element_type x3 -> x0, local copies, waits for them, and re-layouts: 1.6 us -> none  [the longest x1 0.76 us: local(): pair_offset.reshape(block_count, 2 * pairs).astype(jnp.float32)]
    all_to_all x2, waiting for transfers between devices: 31.3 us -> 32.7 us  [exchange(): return lax.all_to_all(array, 'sky', split_axis=0, concat_axis=0, tiled=True)]
  transfers between devices with their start and end apart: 10 -> 10, of which waited for: 3 -> 4; matrix products, arithmetic and copies ran while one was open for 5% -> 1% of each run, Pallas kernels for 31% -> 34%
where the time goes in v4:
time: 120 us; the launch traced here: 118 us
  waiting for transfers between devices  45.7 us (38%)
  Pallas kernels  40.7 us (34%)
  starting transfers between devices  26.9 us (22%)
  local copies, waits for them, and re-layouts  3.18 us (3%)
  other arithmetic  1.52 us (1%)
    all_to_all x2, waiting for transfers between devices, exchange(): return lax.all_to_all(array, 'sky', split_axis=0, concat_axis=0, tiled=True)  32.7 us
    pallas_call x1, Pallas kernels, upper_warp(): pl.pallas_call(functools.partial(upper_kernel, pairs), grid=(1,), in_spec...  17.2 us
    pallas_call x2, Pallas kernels, filtered(): pl.pallas_call(functools.partial(filter_kernel, span, chunk, side, owners...  13.8 us
    ppermute x6, starting transfers between devices, coadd(): whole = whole + lax.ppermute(sums[step], 'visit', ring).astype(jnp.float32)  12.9 us
    pallas_call x1, Pallas kernels, lower_warp(): pl.pallas_call(functools.partial(lower_kernel, pairs), in_specs=[pl.Block...  9.68 us
    ppermute x6, waiting for transfers between devices, coadd(): whole = whole + lax.ppermute(sums[step], 'visit', ring).astype(jnp.float32)  8.98 us
    all_to_all x2, starting transfers between devices, exchange(): return lax.all_to_all(array, 'sky', split_axis=0, concat_axis=0, tiled=True)  8.81 us
    ppermute x1, starting transfers between devices, local(): lax.ppermute(high, 'sky', [((i + 1) % owners, i) for i in range(owners)])  5.12 us
  transfers between devices with their start and end apart: 10, of which 4 were waited for; matrix products, arithmetic and copies ran while one was open for 1% of the time, Pallas kernels for 34%

profile of v4, /device:TPU:0, one launch (start us, length us, event | category | flops | bytes accessed | tf_op | source)
XLA Modules:
  0.0 118.2 jit_solution(11038884861421301878)
XLA Ops:
  0.0 1.1 fusion.9
  1.3 5.1 %collective-permute-start.1 = (bf16[2,16,4096]{2,1,0:T(8,128)(2,1)S(1)}, bf16[2,16,4096]{2,1,0:T(8,128)(2,1)S(1)}, u32[]{:S(2)}, u32[]{:S(2)}) collective-permute-start(bf16[2,16,4096]{2,1,0:T(8,128)(2,1)S(1)} %pad_maximum_fusion.2), channel_id=1, source_target_pairs={{1,0},{2,1},{3,2},{4,3},{5,4},{6,5},{7,6},{8,7},{9,8},{10,9},{11,1... | collective-permute-start | bytes 786440 | tf_op jit(solution)/shard_map/ppermute | solution.py:538
  6.4 4.0 %collective-permute-done.refs_3_ = bf16[2,16,4096]{2,1,0:T(8,128)(2,1)S(1)} collective-permute-done((bf16[2,16,4096]{2,1,0:T(8,128)(2,1)S(1)}, bf16[2,16,4096]{2,1,0:T(8,128)(2,1)S(1)}, u32[]{:S(2)}, u32[]{:S(2)}) %collective-permute-start) | collective-permute-done | bytes 262176 | tf_op jit(solution)/shard_map/ppermute | solution.py:537
  10.4 0.7 copy-done.5
  11.1 7.7 %filter.2 = bf16[64,176,128]{2,1,0:T(8,128)(2,1)} custom-call(s32[1,1,32]{2,1,0:T(1,128)} %owner_ref.3, bf16[1,2,21]{2,1,0:T(2,128)(2,1)} %taps_ref.3, bf16[128,4096]{1,0:T(8,128)(2,1)} %bitcast.16, bf16[128,4096]{1,0:T(8,128)(2,1)} %bitcast.18, s32[128,4096]{1,0:T(8,128)} %bitcast.20, bf16[2,16,4096]{2,1,0:T(8,128)(2,1)} %copy-done.5, ...), custom_call_target="tpu_custom_call" | custom-call | flops 2000000000 | bytes 16777216 | tf_op jit(solution)/shard_map/filter/pallas_call | solution.py:215
  18.8 0.7 copy-done.4
  19.5 4.1 %all-to-all-start = ((bf16[64,176,128]{2,1,0:T(8,128)(2,1)}), bf16[64,176,128]{2,1,0:T(8,128)(2,1)S(1)}, u32[]{:S(2)}, u32[]{:S(2)}) async-start(bf16[64,176,128]{2,1,0:T(8,128)(2,1)} %filter.2), calls=%async_computation | async-start | bytes 5767168 | tf_op jit(solution)/shard_map/all_to_all | solution.py:533
  23.6 6.1 %filter.3 = bf16[64,96,128]{2,1,0:T(8,128)(2,1)} custom-call(s32[1,1,32]{2,1,0:T(1,128)} %owner_ref.3, bf16[1,2,21]{2,1,0:T(2,128)(2,1)} %taps_ref.3, bf16[128,4096]{1,0:T(8,128)(2,1)} %bitcast.17, bf16[128,4096]{1,0:T(8,128)(2,1)} %bitcast.19, s32[128,4096]{1,0:T(8,128)} %bitcast.21, bf16[2,16,4096]{2,1,0:T(8,128)(2,1)} %copy-done.4), custom_call_target="tpu_custom_call" | custom-call | flops 2000000000 | bytes 16777216 | tf_op jit(solution)/shard_map/filter/pallas_call | solution.py:215
  29.7 32.7 %all-to-all-done.first_ref.refs_0_ = bf16[64,176,128]{2,1,0:T(8,128)(2,1)S(1)} async-done(((bf16[64,176,128]{2,1,0:T(8,128)(2,1)}), bf16[64,176,128]{2,1,0:T(8,128)(2,1)S(1)}, u32[]{:S(2)}, u32[]{:S(2)}) %all-to-all-start) | async-done | bytes 2883616 | tf_op jit(solution)/shard_map/all_to_all | solution.py:533
  62.5 4.7 %all-to-all-start.1 = ((bf16[64,96,128]{2,1,0:T(8,128)(2,1)}), bf16[64,96,128]{2,1,0:T(8,128)(2,1)}, u32[]{:S(2)}, u32[]{:S(2)}) async-start(bf16[64,96,128]{2,1,0:T(8,128)(2,1)} %filter.3), calls=%async_computation.1 | async-start | bytes 3145728 | tf_op jit(solution)/shard_map/all_to_all | solution.py:533
  67.2 0.2 fusion.8
  67.4 0.1 fusion.6
  67.5 0.6 reshape.29.aim_ref
  68.2 17.2 %upper_warp.1 = (bf16[64,4,64,128]{3,2,1,0:T(8,128)(2,1)}, bf16[64,4,128,128]{3,2,1,0:T(8,128)(2,1)}, f32[8,128,128]{2,1,0:T(8,128)}, bf16[8,128,128]{2,1,0:T(8,...) custom-call(s32[256]{0:T(256)} %reshape.29.aim_ref, f32[64,128]{1,0:T(8,128)} %bitcast.15, ...), custom_call_target="tpu_custom_call" | custom-call | flops 10000000000 | bytes 33554432 | tf_op jit(solution)/shard_map/upper_warp/pallas_call | solution.py:396
  85.4 4.0 %collective-permute-start.2 = (bf16[8,128,128]{2,1,0:T(8,128)(2,1)}, bf16[8,128,128]{2,1,0:T(8,128)(2,1)S(1)}, u32[]{:S(2)}, u32[]{:S(2)}) collective-permute-start(bf16[8,128,128]{2,1,0:T(8,128)(2,1)} %get-tuple-element.23), channel_id=1, source_target_pairs={{0,64},{32,96},{64,0},{96,32},{1,65},{33,97},{65,1},{97,33},{2,66}... | collective-permute-start | bytes 786440 | tf_op jit(solution)/shard_map/ppermute | solution.py:571
  89.4 1.0 collective-permute-start.3
  90.4 2.2 %collective-permute-start.4 = (bf16[8,128,128]{2,1,0:T(8,128)(2,1)}, bf16[8,128,128]{2,1,0:T(8,128)(2,1)S(1)}, u32[]{:S(2)}, u32[]{:S(2)}) collective-permute-start(bf16[8,128,128]{2,1,0:T(8,128)(2,1)} %get-tuple-element.25), channel_id=1, source_target_pairs={{0,96},{32,0},{64,32},{96,64},{1,97},{33,1},{65,33},{97,65},{2,98}... | collective-permute-start | bytes 786440 | tf_op jit(solution)/shard_map/ppermute | solution.py:571
  92.6 9.7 %lower_warp.1 = (f32[8,128,128]{2,1,0:T(8,128)}, bf16[8,128,128]{2,1,0:T(8,128)(2,1)}, bf16[8,128,128]{2,1,0:T(8,128)(2,1)}, bf16[8,128,128]{2,1,0:T(8,128)(2,1)}) custom-call(s32[256]{0:T(256)} %reshape.29.aim_ref, bf16[64,176,128]{2,1,0:T(8,128)(2,1)} %copy-done, bf16[64,96,128]{2,1,0:T(8,128)(2,1)} %all-to-all-done.1.refs_1_, ...), custom_call_target="tpu_custom_call" | custom-call | flops 6000000000 | bytes 33554432 | tf_op jit(solution)/shard_map/lower_warp/pallas_call | solution.py:495
  102.3 2.5 %collective-permute-start.5 = (bf16[8,128,128]{2,1,0:T(8,128)(2,1)}, bf16[8,128,128]{2,1,0:T(8,128)(2,1)S(1)}, u32[]{:S(2)}, u32[]{:S(2)}) collective-permute-start(bf16[8,128,128]{2,1,0:T(8,128)(2,1)} %get-tuple-element.30), channel_id=1, source_target_pairs={{0,64},{32,96},{64,0},{96,32},{1,65},{33,97},{65,1},{97,33},{2,66}... | collective-permute-start | bytes 786440 | tf_op jit(solution)/shard_map/ppermute | solution.py:571
  104.8 1.0 collective-permute-start.6
  105.8 2.2 %collective-permute-start.7 = (bf16[8,128,128]{2,1,0:T(8,128)(2,1)}, bf16[8,128,128]{2,1,0:T(8,128)(2,1)S(1)}, u32[]{:S(2)}, u32[]{:S(2)}) collective-permute-start(bf16[8,128,128]{2,1,0:T(8,128)(2,1)} %get-tuple-element.32), channel_id=1, source_target_pairs={{0,96},{32,0},{64,32},{96,64},{1,97},{33,1},{65,33},{97,65},{2,98}... | collective-permute-start | bytes 786440 | tf_op jit(solution)/shard_map/ppermute | solution.py:571
  108.2 5.2 %collective-permute-done.5 = bf16[8,128,128]{2,1,0:T(8,128)(2,1)S(1)} collective-permute-done((bf16[8,128,128]{2,1,0:T(8,128)(2,1)}, bf16[8,128,128]{2,1,0:T(8,128)(2,1)S(1)}, u32[]{:S(2)}, u32[]{:S(2)}) %collective-permute-start.5) | collective-permute-done | bytes 262176 | tf_op jit(solution)/shard_map/ppermute | solution.py:571
  113.4 3.8 %collective-permute-done.6 = bf16[8,128,128]{2,1,0:T(8,128)(2,1)S(1)} collective-permute-done((bf16[8,128,128]{2,1,0:T(8,128)(2,1)}, bf16[8,128,128]{2,1,0:T(8,128)(2,1)S(1)}, u32[]{:S(2)}, u32[]{:S(2)}) %collective-permute-start.6) | collective-permute-done | bytes 262176 | tf_op jit(solution)/shard_map/ppermute | solution.py:571
  117.4 0.8 pad_maximum_fusion
  (24 shorter events, 0.5 us)
Async XLA Ops:
  1.2 9.2 %collective-permute-start = (bf16[2,16,4096]{2,1,0:T(8,128)(2,1)S(1)}, bf16[2,16,4096]{2,1,0:T(8,128)(2,1)S(1)}, u32[]{:S(2)}, u32[]{:S(2)}) collective-permute-start(bf16[2,16,4096]{2,1,0:T(8,128)(2,1)S(1)} %pad_maximum_fusion.1), channel_id=1, source_target_pairs={{0,1},{1,2},{2,3},{3,4},{4,5},{5,6},{6,7},{7,8},{8,9},{9,10},{10,1... | collective-permute-start | bytes 786440 | tf_op jit(solution)/shard_map/ppermute | solution.py:537
  1.3 17.5 %collective-permute-start.1 = (bf16[2,16,4096]{2,1,0:T(8,128)(2,1)S(1)}, bf16[2,16,4096]{2,1,0:T(8,128)(2,1)S(1)}, u32[]{:S(2)}, u32[]{:S(2)}) collective-permute-start(bf16[2,16,4096]{2,1,0:T(8,128)(2,1)S(1)} %pad_maximum_fusion.2), channel_id=1, source_target_pairs={{1,0},{2,1},{3,2},{4,3},{5,4},{6,5},{7,6},{8,7},{9,8},{10,9},{11,1... | collective-permute-start | bytes 786440 | tf_op jit(solution)/shard_map/ppermute | solution.py:538
  10.4 0.7 copy-start.5
  18.8 0.7 copy-start.4
  19.5 43.0 %all-to-all-start = ((bf16[64,176,128]{2,1,0:T(8,128)(2,1)}), bf16[64,176,128]{2,1,0:T(8,128)(2,1)S(1)}, u32[]{:S(2)}, u32[]{:S(2)}) async-start(bf16[64,176,128]{2,1,0:T(8,128)(2,1)} %filter.2), calls=%async_computation | async-start | bytes 5767168 | tf_op jit(solution)/shard_map/all_to_all | solution.py:533
  62.5 5.7 %copy-start = (bf16[64,176,128]{2,1,0:T(8,128)(2,1)}, bf16[64,176,128]{2,1,0:T(8,128)(2,1)S(1)}, u32[]{:S(2)}) copy-start(bf16[64,176,128]{2,1,0:T(8,128)(2,1)S(1)} %all-to-all-done.first_ref.refs_0_) | copy-start | bytes 8650756
  62.5 30.1 %all-to-all-start.1 = ((bf16[64,96,128]{2,1,0:T(8,128)(2,1)}), bf16[64,96,128]{2,1,0:T(8,128)(2,1)}, u32[]{:S(2)}, u32[]{:S(2)}) async-start(bf16[64,96,128]{2,1,0:T(8,128)(2,1)} %filter.3), calls=%async_computation.1 | async-start | bytes 3145728 | tf_op jit(solution)/shard_map/all_to_all | solution.py:533
  67.2 1.0 copy-start.3
  85.4 20.4 %collective-permute-start.2 = (bf16[8,128,128]{2,1,0:T(8,128)(2,1)}, bf16[8,128,128]{2,1,0:T(8,128)(2,1)S(1)}, u32[]{:S(2)}, u32[]{:S(2)}) collective-permute-start(bf16[8,128,128]{2,1,0:T(8,128)(2,1)} %get-tuple-element.23), channel_id=1, source_target_pairs={{0,64},{32,96},{64,0},{96,32},{1,65},{33,97},{65,1},{97,33},{2,66}... | collective-permute-start | bytes 786440 | tf_op jit(solution)/shard_map/ppermute | solution.py:571
  89.4 18.7 %collective-permute-start.3 = (bf16[8,128,128]{2,1,0:T(8,128)(2,1)}, bf16[8,128,128]{2,1,0:T(8,128)(2,1)S(1)}, u32[]{:S(2)}, u32[]{:S(2)}) collective-permute-start(bf16[8,128,128]{2,1,0:T(8,128)(2,1)} %get-tuple-element.24), channel_id=1, source_target_pairs={{0,32},{32,64},{64,96},{96,0},{1,33},{33,65},{65,97},{97,1},{2,34}... | collective-permute-start | bytes 786440 | tf_op jit(solution)/shard_map/ppermute | solution.py:571
  90.4 17.6 %collective-permute-start.4 = (bf16[8,128,128]{2,1,0:T(8,128)(2,1)}, bf16[8,128,128]{2,1,0:T(8,128)(2,1)S(1)}, u32[]{:S(2)}, u32[]{:S(2)}) collective-permute-start(bf16[8,128,128]{2,1,0:T(8,128)(2,1)} %get-tuple-element.25), channel_id=1, source_target_pairs={{0,96},{32,0},{64,32},{96,64},{1,97},{33,1},{65,33},{97,65},{2,98}... | collective-permute-start | bytes 786440 | tf_op jit(solution)/shard_map/ppermute | solution.py:571
  92.6 15.4 %copy-start.1 = (f32[8,128,128]{2,1,0:T(8,128)S(1)}, f32[8,128,128]{2,1,0:T(8,128)}, u32[]{:S(2)}) copy-start(f32[8,128,128]{2,1,0:T(8,128)} %get-tuple-element.22) | copy-start | bytes 1572868
  102.3 14.9 %copy-start.2 = (f32[8,128,128]{2,1,0:T(8,128)S(1)}, f32[8,128,128]{2,1,0:T(8,128)}, u32[]{:S(2)}) copy-start(f32[8,128,128]{2,1,0:T(8,128)} %get-tuple-element.29) | copy-start | bytes 1572868
  102.3 11.1 %collective-permute-start.5 = (bf16[8,128,128]{2,1,0:T(8,128)(2,1)}, bf16[8,128,128]{2,1,0:T(8,128)(2,1)S(1)}, u32[]{:S(2)}, u32[]{:S(2)}) collective-permute-start(bf16[8,128,128]{2,1,0:T(8,128)(2,1)} %get-tuple-element.30), channel_id=1, source_target_pairs={{0,64},{32,96},{64,0},{96,32},{1,65},{33,97},{65,1},{97,33},{2,66}... | collective-permute-start | bytes 786440 | tf_op jit(solution)/shard_map/ppermute | solution.py:571
  104.8 12.4 %collective-permute-start.6 = (bf16[8,128,128]{2,1,0:T(8,128)(2,1)}, bf16[8,128,128]{2,1,0:T(8,128)(2,1)S(1)}, u32[]{:S(2)}, u32[]{:S(2)}) collective-permute-start(bf16[8,128,128]{2,1,0:T(8,128)(2,1)} %get-tuple-element.31), channel_id=1, source_target_pairs={{0,32},{32,64},{64,96},{96,0},{1,33},{33,65},{65,97},{97,1},{2,34}... | collective-permute-start | bytes 786440 | tf_op jit(solution)/shard_map/ppermute | solution.py:571
  105.8 11.4 %collective-permute-start.7 = (bf16[8,128,128]{2,1,0:T(8,128)(2,1)}, bf16[8,128,128]{2,1,0:T(8,128)(2,1)S(1)}, u32[]{:S(2)}, u32[]{:S(2)}) collective-permute-start(bf16[8,128,128]{2,1,0:T(8,128)(2,1)} %get-tuple-element.32), channel_id=1, source_target_pairs={{0,96},{32,0},{64,32},{96,64},{1,97},{33,1},{65,33},{97,65},{2,98}... | collective-permute-start | bytes 786440 | tf_op jit(solution)/shard_map/ppermute | solution.py:571

commit v5 on v4

--- a/solution.py
+++ b/solution.py
@@ -13,9 +13,11 @@
 BAND = 16
 CAP = 2
 PB_DEV = 8
-CUT = 80
-EDGE = CUT - 16
-REACH = EDGE - 16
+FROM, TO = 16, 96
+CUT = TO - FROM
+BEGIN, END = FROM + 8, TO - 8
+EDGE = END - BEGIN
+REACH = 16
 FACTS = 16
 FILTER_COLUMNS = 2048
 UNROLL = 2
@@ -33,46 +35,55 @@
         matrix = jnp.where(lag == index, value, matrix)
     return matrix.astype(jnp.bfloat16)
 
-def filter_kernel(span, chunk, side, owners, owner_ref, taps_ref, *refs):
-    exposure_ref, variance_ref, mask_ref, halo_ref = refs[:4]
-    pair_refs, out = refs[4:-14], refs[-14]
+def segments(spans, rows):
+    result, at, frame = [], 0, 0
+    for first, last in spans:
+        own_from, own_to = max(first - HALO, 0), min(last + HALO, rows)
+        own_at = frame + own_from - (first - HALO)
+        result.append((first, last, at, frame, own_from, own_to, own_at))
+        at += last - first
+        frame += last - first + 2 * HALO
+    return result, at, frame
+
+
+def filter_kernel(spans, owners, halo_count, owner_ref, taps_ref, *refs):
+    exposure_ref, variance_ref, mask_ref = refs[:3]
+    halo_refs = refs[3 : 3 + halo_count]
+    pair_refs, out = refs[3 + halo_count : -14], refs[-14]
     framed, usable_ref, across_ref, down_ref, staged, empty_ref, facts_ref = refs[-13:-6]
     slot_ref, count_ref, here, near, done, cleared = refs[-6:]
-    (first, last), (chunk_first, chunk_last) = span, chunk
     rows, columns = mask_ref.shape
-    height, chunk_height = last - first, chunk_last - chunk_first
-    tall = height + 2 * HALO
+    parted, height, tall = segments(spans, rows)
     wide = 2 * BS
     half = (taps_ref.shape[-1] - 1) // 2
     parts = here.shape[1]
     part_columns = columns // parts
 
-    own_from, own_to = max(first - HALO, 0), min(last + HALO, rows)
-    own_at, halo_at = (HALO, 0) if side == "top" else (0, own_to - own_from)
-
     def fetched(part):
         lanes = pl.ds(part * part_columns, part_columns)
         inner = pl.ds(BS + part * part_columns, part_columns)
-        own, placed = pl.ds(own_from, own_to - own_from), pl.ds(own_at, own_to - own_from)
-        kept = pl.ds(first, height)
+        pieces = []
+        for first, last, at, _, own_from, own_to, own_at in parted:
+            own, placed = pl.ds(own_from, own_to - own_from), pl.ds(own_at, own_to - own_from)
+            kept, put = pl.ds(first, last - first), pl.ds(at, last - first)
+            pieces += [
+                (exposure_ref.at[own, lanes], framed.at[0, placed, inner]),
+                (variance_ref.at[own, lanes], framed.at[1, placed, inner]),
+                (mask_ref.at[kept, lanes], usable_ref.at[put, lanes]),
+            ]
         return [
-            pltpu.make_async_copy(
-                exposure_ref.at[own, lanes], framed.at[0, placed, inner], here.at[0, part]
-            ),
-            pltpu.make_async_copy(
-                variance_ref.at[own, lanes], framed.at[1, placed, inner], here.at[1, part]
-            ),
-            pltpu.make_async_copy(
-                mask_ref.at[kept, lanes], usable_ref.at[:, lanes], here.at[2, part]
-            ),
+            pltpu.make_async_copy(source, target, here.at[index, part])
+            for index, (source, target) in enumerate(pieces)
         ]
 
+    halo_places = (0, tall - HALO)
     halos = [
         pltpu.make_async_copy(
             halo_ref.at[plane],
-            framed.at[plane, pl.ds(halo_at, HALO), pl.ds(BS, columns)],
-            near.at[plane],
+            framed.at[plane, pl.ds(place, HALO), pl.ds(BS, columns)],
+            near.at[index, plane],
         )
+        for index, (halo_ref, place) in enumerate(zip(halo_refs, halo_places))
         for plane in range(2)
     ]
     for copy in halos:
@@ -83,7 +94,7 @@
     if pair_refs:
         empty_ref[...] = jnp.zeros(empty_ref.shape, jnp.bfloat16)
         clear = pltpu.make_async_copy(
-            empty_ref, out.at[:, pl.ds(2 * chunk_height, FACTS), :], cleared.at[0]
+            empty_ref, out.at[:, pl.ds(2 * height, FACTS), :], cleared.at[0]
         )
         clear.start()
 
@@ -124,15 +135,19 @@
         for row, blocks in enumerate(pattern):
             across_ref[plane, row * BS : (row + 1) * BS, :BS] = blocks[0]
             across_ref[plane, row * BS : (row + 1) * BS, BS:] = blocks[1]
-        down_ref[plane] = toeplitz(height, tall, half + HALO, taps[1][::-1])
+        place = lax.broadcasted_iota(jnp.int32, (height, tall), 0)
+        shift = jnp.full((height, tall), half + HALO, jnp.int32)
+        for _, _, at, frame, *_ in parted[1:]:
+            shift = jnp.where(place >= at, half + HALO + frame - at, shift)
+        down_ref[plane] = toeplitz(height, tall, shift, taps[1][::-1])
 
     for copy in halos:
         copy.wait()
-    outermost = 0 if side == "top" else owners - 1
-    inner = lax.axis_index("sky") != outermost
-    for plane in range(2):
-        halo = framed[plane, halo_at : halo_at + HALO, :]
-        framed[plane, halo_at : halo_at + HALO, :] = jnp.where(inner, halo, jnp.zeros_like(halo))
+    for place, outermost in list(zip(halo_places, (0, owners - 1)))[:halo_count]:
+        inner = lax.axis_index("sky") != outermost
+        for plane in range(2):
+            halo = framed[plane, place : place + HALO, :]
+            framed[plane, place : place + HALO, :] = jnp.where(inner, halo, jnp.zeros_like(halo))
     for copy in fetched(0):
         copy.wait()
     tiles = part_columns // wide
@@ -179,27 +194,20 @@
                     staged[index, 2 * height :, :] = row.astype(jnp.bfloat16)
         if pair_refs and part == 0:
             clear.wait()
-        at = first - chunk_first
-        pieces = [(0, height, at), (height, height, chunk_height + at)]
-        if pair_refs:
-            pieces[1] = (height, height + FACTS, chunk_height + at)
         for index in range(part * tiles * 2, (part + 1) * tiles * 2):
-            for piece, (begin, count, to) in enumerate(pieces):
-                copy = pltpu.make_async_copy(
-                    staged.at[index, pl.ds(begin, count), :],
-                    out.at[slot_ref[index], pl.ds(to, count), :],
-                    done.at[index, piece],
-                )
-                copy.start()
-                sent.append(copy)
+            copy = pltpu.make_async_copy(
+                staged.at[index], out.at[slot_ref[index]], done.at[index]
+            )
+            copy.start()
+            sent.append(copy)
     for copy in sent:
         copy.wait()
 
 
-def filtered(span, chunk, owners, owner, taps, images, side, halo, facts=()):
+def filtered(spans, owners, owner, taps, images, halos=(), facts=()):
     rows, columns = images[2].shape
-    height = span[1] - span[0]
-    tall = 2 * (chunk[1] - chunk[0]) + (0 if chunk[0] else FACTS)
+    _, height, frame = segments(spans, rows)
+    tall = 2 * height + (FACTS if facts else 0)
     slots = owners * CAP
     blocks = columns // BS
     parts = columns // FILTER_COLUMNS
@@ -209,28 +217,28 @@
     def whole(array):
         return pl.BlockSpec(array.shape, lambda i: (0,) * array.ndim)
 
-    operands = [owner, taps, *images, halo, *facts]
-    specs = [smem, whole(taps), hbm, hbm, hbm, pl.BlockSpec(memory_space=pl.ANY)]
+    operands = [owner, taps, *images, *halos, *facts]
+    specs = [smem, whole(taps), hbm, hbm, hbm] + [pl.BlockSpec(memory_space=pl.ANY)] * len(halos)
     specs += [whole(fact) for fact in facts]
     return pl.pallas_call(
-        functools.partial(filter_kernel, span, chunk, side, owners),
+        functools.partial(filter_kernel, spans, owners, len(halos)),
         grid=(1,),
         out_shape=jax.ShapeDtypeStruct((slots, tall, BS), jnp.bfloat16),
         in_specs=specs,
         out_specs=hbm,
         scratch_shapes=[
-            pltpu.VMEM((2, height + 2 * HALO, columns + 2 * BS), jnp.bfloat16),
+            pltpu.VMEM((2, frame, columns + 2 * BS), jnp.bfloat16),
             pltpu.VMEM((height, columns), jnp.int32),
             pltpu.VMEM((2, 4 * BS, 2 * BS), jnp.bfloat16),
-            pltpu.VMEM((2, height, height + 2 * HALO), jnp.bfloat16),
-            pltpu.VMEM((blocks, 2 * height + FACTS, BS), jnp.bfloat16),
+            pltpu.VMEM((2, height, frame), jnp.bfloat16),
+            pltpu.VMEM((blocks, tall, BS), jnp.bfloat16),
             pltpu.VMEM((slots, FACTS, BS), jnp.bfloat16),
             pltpu.VMEM((BS, BS), jnp.float32),
             pltpu.SMEM((blocks,), jnp.int32),
             pltpu.SMEM((owners,), jnp.int32),
-            pltpu.SemaphoreType.DMA((3, parts)),
-            pltpu.SemaphoreType.DMA((2,)),
-            pltpu.SemaphoreType.DMA((blocks, 2)),
+            pltpu.SemaphoreType.DMA((3 * len(spans), parts)),
+            pltpu.SemaphoreType.DMA((2, 2)),
+            pltpu.SemaphoreType.DMA((blocks,)),
             pltpu.SemaphoreType.DMA((1,)),
         ],
         compiler_params=pltpu.CompilerParams(vmem_limit_bytes=FILTER_VMEM),
@@ -349,12 +357,20 @@
                 index = which * pairs + pair
                 one = jnp.where(group == index, value, 0.0)
                 shift = -BAND // 2 - BAND * index
-                upper = pltpu.roll(one[:EDGE], shift % BS, 1, stride=1, stride_axis=0)
-                lower = pltpu.roll(
-                    one[EDGE:], (shift + EDGE - REACH) % BS, 1, stride=1, stride_axis=0
+                inner, above, below = (
+                    pltpu.roll(
+                        one[begin:end], (shift + begin - lane) % BS, 1, stride=1, stride_axis=0
+                    )
+                    for begin, end, lane in (
+                        (BEGIN, END, FROM),
+                        (0, BEGIN, 0),
+                        (END, BS, TO - FROM - 2 * REACH),
+                    )
                 )
-                second_ref[slot, pair] = lower.astype(jnp.bfloat16)
-                stack.append(upper.astype(jnp.bfloat16)[:, :CUT])
+                second_ref[slot, pair] = jnp.concatenate([above, below], axis=0).astype(
+                    jnp.bfloat16
+                )
+                stack.append(inner.astype(jnp.bfloat16)[:, :CUT])
                 lag = numbers - near_ref[pair, pl.ds(slot, 1), :].astype(jnp.bfloat16)
                 column = jnp.zeros((BS, BS), jnp.bfloat16)
                 for k in range(7):
@@ -435,16 +451,20 @@
     first_ref, second_ref, row_ref, column_ref, total, arrived = refs[-6:]
     parts = arrived.shape[1]
     per_part = first_ref.shape[0] // parts
-    near, far = CUT - REACH, BS - CUT
+    far = BS - CUT
 
     def copies(part):
         slots = pl.ds(part * per_part, per_part)
         pieces = [
             (
-                first.at[slots, pl.ds(plane * CUT + REACH, near), :],
-                first_ref.at[slots, pl.ds(plane * near, near), :],
-            )
-            for plane in range(2)
+                first.at[slots, pl.ds(begin, count), :],
+                first_ref.at[slots, pl.ds(place, count), :],
+            )
+            for begin, count, place in (
+                (0, REACH, 0),
+                (CUT - REACH, 2 * REACH, REACH),
+                (2 * CUT - REACH, REACH, 3 * REACH),
+            )
         ]
         pieces += [
             (second.at[slots], second_ref.at[slots]),
@@ -471,8 +491,9 @@
                 [
                     jnp.concatenate(
                         [
-                            first_ref[slot, plane * near : (plane + 1) * near, :],
-                            second_ref[slot, plane * far : (plane + 1) * far, :],
+                            second_ref[slot, plane * far : plane * far + FROM, :],
+                            first_ref[slot, plane * 2 * REACH : (plane + 1) * 2 * REACH, :],
+                            second_ref[slot, plane * far + FROM : (plane + 1) * far, :],
                         ],
                         axis=0,
                     )
@@ -481,7 +502,7 @@
                 axis=1,
             )
             aims = [aim_ref[slot * pairs + pair] for pair in range(pairs)]
-            rows = row_ref[slot].reshape(pairs * row_ref.shape[2], BS)[:, : near + far]
+            rows = row_ref[slot].reshape(pairs * row_ref.shape[2], BS)[:, : 2 * REACH + far]
             columns = [column_ref[slot, pair] for pair in range(pairs)]
             accumulate(total, aims, rows, source, columns)
 
@@ -498,12 +519,12 @@
         + [pl.BlockSpec(memory_space=pl.ANY)] * len(operands),
         out_specs=[pl.BlockSpec(memory_space=pltpu.VMEM)] * groups,
         scratch_shapes=[
-            pltpu.VMEM((slots, 2 * (CUT - REACH), BS), first.dtype),
+            pltpu.VMEM((slots, 4 * REACH, BS), first.dtype),
             pltpu.VMEM(second.shape, second.dtype),
             pltpu.VMEM(row_maps.shape, row_maps.dtype),
             pltpu.VMEM(column_maps.shape, column_maps.dtype),
             pltpu.VMEM((groups * PB_DEV + 1, 2 * height, BS), jnp.float32),
-            pltpu.SemaphoreType.DMA((5, LOWER_PARTS)),
+            pltpu.SemaphoreType.DMA((6, LOWER_PARTS)),
         ],
         out_shape=[
             jax.ShapeDtypeStruct(
@@ -545,17 +566,17 @@
 
     images = [array.reshape(rows, columns) for array in (exposure, variance, pixel_mask)]
     common = (owners, block_owner, psf_kernel, images)
-    upper_planes = filtered((0, CUT), (0, CUT), *common, "top", top, facts)
-    upper_planes, bottom = lax.optimization_barrier((upper_planes, bottom))
-    first = exchange(upper_planes)
-
-    lower_planes = filtered((CUT, rows), (CUT, rows), *common, "bottom", bottom)
-    first, lower_planes = lax.optimization_barrier((first, lower_planes))
-    second = exchange(lower_planes)
+    inner_planes = filtered([(FROM, TO)], *common, facts=facts)
+    inner_planes, top, bottom = lax.optimization_barrier((inner_planes, top, bottom))
+    first = exchange(inner_planes)
+
+    outer_planes = filtered([(0, FROM), (TO, rows)], *common, halos=(top, bottom))
+    first, outer_planes = lax.optimization_barrier((first, outer_planes))
+    second = exchange(outer_planes)
 
     table = first[:, 2 * CUT, :].astype(jnp.float32)
     patch = table[:, 4 * pairs : 5 * pairs].astype(jnp.int32)
-    distance = (patch // PB_DEV - lax.axis_index("visit")) % groups
+    distance = (patch // PB_DEV) ^ lax.axis_index("visit")
     aims = jnp.where(
         table[:, 5 * pairs : 5 * pairs + 1] > 0.5,
         distance * PB_DEV + patch % PB_DEV,
@@ -567,13 +588,14 @@
     def coadd(sums):
         whole = sums[0]
         for step in (2, 1, 3):
-            ring = [(i, (i + step) % groups) for i in range(groups)]
+            ring = [(i, i ^ step) for i in range(groups)]
             whole = whole + lax.ppermute(sums[step], "visit", ring).astype(jnp.float32)
         height = whole.shape[1] // 2
         return whole[:, :height] / jnp.maximum(whole[:, height:], 1.0)
 
     lower = lower_warp(aims, first, second, second_maps, column_maps, groups)
-    return jnp.concatenate([coadd(upper), coadd(lower)], axis=1)
+    inner, outer = coadd(upper), coadd(lower)
+    return jnp.concatenate([outer[:, :BEGIN], inner, outer[:, BEGIN:]], axis=1)
 
 
 def solution(mesh):

time: 120 us -> 113 us (0.942); the launches traced: 118 us -> 113 us
  starting transfers between devices: 26.9 us -> 24.1 us
  waiting for transfers between devices: 45.7 us -> 43.2 us
    ppermute x1, waiting for transfers between devices: 3.95 us -> 0.01 us  [local(): lax.ppermute(low, 'sky', [(i, (i + 1) % owners) for i in range(owners)])]
    ppermute x6, starting transfers between devices: 12.9 us -> 10.1 us  [coadd(): whole = whole + lax.ppermute(sums[step], 'visit', ring).astype(jnp.float32)]
    ppermute x6, waiting for transfers between devices: 8.98 us -> 10.3 us  [coadd(): whole = whole + lax.ppermute(sums[step], 'visit', ring).astype(jnp.float32)]
  transfers between devices with their start and end apart: 10 -> 10, of which waited for: 4 -> 4; matrix products, arithmetic and copies ran while one was open for 1% -> 1% of each run, Pallas kernels for 34% -> 36%
where the time goes in v5:
time: 113 us
  waiting for transfers between devices  43.2 us (38%)
  Pallas kernels  40.9 us (36%)
  starting transfers between devices  24.1 us (21%)
  local copies, waits for them, and re-layouts  2.57 us (2%)
  other arithmetic  1.51 us (1%)
    all_to_all x2, waiting for transfers between devices, exchange(): return lax.all_to_all(array, 'sky', split_axis=0, concat_axis=0, tiled=True)  32.9 us
    pallas_call x1, Pallas kernels, upper_warp(): pl.pallas_call(functools.partial(upper_kernel, pairs), grid=(1,), in_spec...  17.2 us
    pallas_call x2, Pallas kernels, filtered(): pl.pallas_call(functools.partial(filter_kernel, spans, owners, len(halos)...  14 us
    ppermute x6, waiting for transfers between devices, coadd(): whole = whole + lax.ppermute(sums[step], 'visit', ring).astype(jnp.float32)  10.3 us
    ppermute x6, starting transfers between devices, coadd(): whole = whole + lax.ppermute(sums[step], 'visit', ring).astype(jnp.float32)  10.1 us
    pallas_call x1, Pallas kernels, lower_warp(): pl.pallas_call(functools.partial(lower_kernel, pairs), in_specs=[pl.Block...  9.72 us
    all_to_all x2, starting transfers between devices, exchange(): return lax.all_to_all(array, 'sky', split_axis=0, concat_axis=0, tiled=True)  8.81 us
    ppermute x1, starting transfers between devices, local(): lax.ppermute(high, 'sky', [((i + 1) % owners, i) for i in range(owners)])  5.12 us
  transfers between devices with their start and end apart: 10, of which 4 were waited for; matrix products, arithmetic and copies ran while one was open for 1% of the time, Pallas kernels for 36%

profile of v5, /device:TPU:0, one launch (start us, length us, event | category | flops | bytes accessed | tf_op | source)
XLA Modules:
  0.0 112.5 jit_solution(6467646619709483826)
XLA Ops:
  0.0 1.1 %fusion.11 = (bf16[1,16,4096]{2,1,0:T(8,128)(2,1)S(1)}, bf16[1,16,4096]{2,1,0:T(8,128)(2,1)S(1)}, bf16[1,16,4096]{2,1,0:T(8,128)(2,1)S(1)}, bf16[1,16,4096]{2,1,0:T(8,128)(2,1)S(1)}) fusion(bf16[1,128,4096]{2,1,0:T(8,128)(2,1)} %param.8, bf16[1,128,4096]{2,1,0:T(8,128)(2,1)} %param.9), kind=kLoop, calls=%fused_computation.27 | loop fusion | bytes 1048576 | tf_op jit(solution)/shard_map/slice | solution.py:557
  1.3 5.1 %collective-permute-start.1 = (bf16[2,16,4096]{2,1,0:T(8,128)(2,1)S(1)}, bf16[2,16,4096]{2,1,0:T(8,128)(2,1)S(1)}, u32[]{:S(2)}, u32[]{:S(2)}) collective-permute-start(bf16[2,16,4096]{2,1,0:T(8,128)(2,1)S(1)} %pad_maximum_fusion.2), channel_id=1, source_target_pairs={{1,0},{2,1},{3,2},{4,3},{5,4},{6,5},{7,6},{8,7},{9,8},{10,9},{11,1... | collective-permute-start | bytes 786440 | tf_op jit(solution)/shard_map/ppermute | solution.py:559
  6.4 7.4 %filter.2 = bf16[64,176,128]{2,1,0:T(8,128)(2,1)} custom-call(s32[1,1,32]{2,1,0:T(1,128)} %owner_ref.3, bf16[1,2,21]{2,1,0:T(2,128)(2,1)} %taps_ref.3, bf16[128,4096]{1,0:T(8,128)(2,1)} %bitcast.16, bf16[128,4096]{1,0:T(8,128)(2,1)} %bitcast.18, s32[128,4096]{1,0:T(8,128)} %bitcast.20, bf16[4,2,32]{2,1,0:T(2,128)(2,1)} %bitcast.22, ...), custom_call_target="tpu_custom_call" | custom-call | flops 2000000000 | bytes 16777216 | tf_op jit(solution)/shard_map/filter/pallas_call | solution.py:223
  13.8 0.7 copy-done.4
  14.5 0.1 copy-done.5
  14.6 4.1 %all-to-all-start = ((bf16[64,176,128]{2,1,0:T(8,128)(2,1)}), bf16[64,176,128]{2,1,0:T(8,128)(2,1)S(1)}, u32[]{:S(2)}, u32[]{:S(2)}) async-start(bf16[64,176,128]{2,1,0:T(8,128)(2,1)} %filter.2), calls=%async_computation | async-start | bytes 5767168 | tf_op jit(solution)/shard_map/all_to_all | solution.py:554
  18.7 6.6 %filter.3 = bf16[64,96,128]{2,1,0:T(8,128)(2,1)} custom-call(s32[1,1,32]{2,1,0:T(1,128)} %owner_ref.3, bf16[1,2,21]{2,1,0:T(2,128)(2,1)} %taps_ref.3, bf16[128,4096]{1,0:T(8,128)(2,1)} %bitcast.17, bf16[128,4096]{1,0:T(8,128)(2,1)} %bitcast.19, s32[128,4096]{1,0:T(8,128)} %bitcast.21, bf16[2,16,4096]{2,1,0:T(8,128)(2,1)} %copy-done.4, ...), custom_call_target="tpu_custom_call" | custom-call | flops 2000000000 | bytes 16777216 | tf_op jit(solution)/shard_map/filter/pallas_call | solution.py:223
  25.3 32.3 %all-to-all-done.first_ref.refs_0_ = bf16[64,176,128]{2,1,0:T(8,128)(2,1)S(1)} async-done(((bf16[64,176,128]{2,1,0:T(8,128)(2,1)}), bf16[64,176,128]{2,1,0:T(8,128)(2,1)S(1)}, u32[]{:S(2)}, u32[]{:S(2)}) %all-to-all-start) | async-done | bytes 2883616 | tf_op jit(solution)/shard_map/all_to_all | solution.py:554
  57.6 4.7 %all-to-all-start.1 = ((bf16[64,96,128]{2,1,0:T(8,128)(2,1)}), bf16[64,96,128]{2,1,0:T(8,128)(2,1)}, u32[]{:S(2)}, u32[]{:S(2)}) async-start(bf16[64,96,128]{2,1,0:T(8,128)(2,1)} %filter.3), calls=%async_computation.1 | async-start | bytes 3145728 | tf_op jit(solution)/shard_map/all_to_all | solution.py:554
  62.3 0.2 fusion.10
  62.5 0.1 fusion.5
  62.6 0.6 reshape.29.aim_ref
  63.3 17.2 %upper_warp.1 = (bf16[64,4,64,128]{3,2,1,0:T(8,128)(2,1)}, bf16[64,4,128,128]{3,2,1,0:T(8,128)(2,1)}, f32[8,128,128]{2,1,0:T(8,128)}, bf16[8,128,128]{2,1,0:T(8,...) custom-call(s32[256]{0:T(256)} %reshape.29.aim_ref, f32[64,128]{1,0:T(8,128)} %bitcast.15, ...), custom_call_target="tpu_custom_call" | custom-call | flops 10000000000 | bytes 33554432 | tf_op jit(solution)/shard_map/upper_warp/pallas_call | solution.py:412
  80.5 4.0 %collective-permute-start.5 = (bf16[8,128,128]{2,1,0:T(8,128)(2,1)}, bf16[8,128,128]{2,1,0:T(8,128)(2,1)S(1)}, u32[]{:S(2)}, u32[]{:S(2)}) collective-permute-start(bf16[8,128,128]{2,1,0:T(8,128)(2,1)} %get-tuple-element.32), channel_id=1, source_target_pairs={{0,64},{32,96},{64,0},{96,32},{1,65},{33,97},{65,1},{97,33},{2,66}... | collective-permute-start | bytes 786440 | tf_op jit(solution)/shard_map/ppermute | solution.py:592
  84.5 1.0 collective-permute-start.6
  85.5 0.7 all-to-all-done.1.refs_1_
  86.2 9.7 %lower_warp.1 = (f32[8,128,128]{2,1,0:T(8,128)}, bf16[8,128,128]{2,1,0:T(8,128)(2,1)}, bf16[8,128,128]{2,1,0:T(8,128)(2,1)}, bf16[8,128,128]{2,1,0:T(8,128)(2,1)}) custom-call(s32[256]{0:T(256)} %reshape.29.aim_ref, bf16[64,176,128]{2,1,0:T(8,128)(2,1)} %copy-done, bf16[64,96,128]{2,1,0:T(8,128)(2,1)} %all-to-all-done.1.refs_1_, ...), custom_call_target="tpu_custom_call" | custom-call | flops 6000000000 | bytes 33554432 | tf_op jit(solution)/shard_map/lower_warp/pallas_call | solution.py:516
  95.9 4.0 %collective-permute-start.2 = (bf16[8,128,128]{2,1,0:T(8,128)(2,1)}, bf16[8,128,128]{2,1,0:T(8,128)(2,1)S(1)}, u32[]{:S(2)}, u32[]{:S(2)}) collective-permute-start(bf16[8,128,128]{2,1,0:T(8,128)(2,1)} %get-tuple-element.28), channel_id=1, source_target_pairs={{0,64},{32,96},{64,0},{96,32},{1,65},{33,97},{65,1},{97,33},{2,66}... | collective-permute-start | bytes 786440 | tf_op jit(solution)/shard_map/ppermute | solution.py:592
  99.9 1.0 collective-permute-start.3
  101.0 0.1 convert_add_fusion
  101.2 6.2 %collective-permute-done.2 = bf16[8,128,128]{2,1,0:T(8,128)(2,1)S(1)} collective-permute-done((bf16[8,128,128]{2,1,0:T(8,128)(2,1)}, bf16[8,128,128]{2,1,0:T(8,128)(2,1)S(1)}, u32[]{:S(2)}, u32[]{:S(2)}) %collective-permute-start.2) | collective-permute-done | bytes 262176 | tf_op jit(solution)/shard_map/ppermute | solution.py:592
  107.4 4.1 %collective-permute-done.3 = bf16[8,128,128]{2,1,0:T(8,128)(2,1)S(1)} collective-permute-done((bf16[8,128,128]{2,1,0:T(8,128)(2,1)}, bf16[8,128,128]{2,1,0:T(8,128)(2,1)S(1)}, u32[]{:S(2)}, u32[]{:S(2)}) %collective-permute-start.3) | collective-permute-done | bytes 262176 | tf_op jit(solution)/shard_map/ppermute | solution.py:592
  111.5 0.1 convert_add_fusion.1
  111.7 0.8 pad_maximum_fusion
  (26 shorter events, 0.3 us)
Async XLA Ops:
  1.2 12.6 %collective-permute-start = (bf16[2,16,4096]{2,1,0:T(8,128)(2,1)S(1)}, bf16[2,16,4096]{2,1,0:T(8,128)(2,1)S(1)}, u32[]{:S(2)}, u32[]{:S(2)}) collective-permute-start(bf16[2,16,4096]{2,1,0:T(8,128)(2,1)S(1)} %pad_maximum_fusion.1), channel_id=1, source_target_pairs={{0,1},{1,2},{2,3},{3,4},{4,5},{5,6},{6,7},{7,8},{8,9},{9,10},{10,1... | collective-permute-start | bytes 786440 | tf_op jit(solution)/shard_map/ppermute | solution.py:558
  1.3 12.5 %collective-permute-start.1 = (bf16[2,16,4096]{2,1,0:T(8,128)(2,1)S(1)}, bf16[2,16,4096]{2,1,0:T(8,128)(2,1)S(1)}, u32[]{:S(2)}, u32[]{:S(2)}) collective-permute-start(bf16[2,16,4096]{2,1,0:T(8,128)(2,1)S(1)} %pad_maximum_fusion.2), channel_id=1, source_target_pairs={{1,0},{2,1},{3,2},{4,3},{5,4},{6,5},{7,6},{8,7},{9,8},{10,9},{11,1... | collective-permute-start | bytes 786440 | tf_op jit(solution)/shard_map/ppermute | solution.py:559
  13.8 0.7 copy-start.4
  13.8 0.8 copy-start.5
  14.6 43.0 %all-to-all-start = ((bf16[64,176,128]{2,1,0:T(8,128)(2,1)}), bf16[64,176,128]{2,1,0:T(8,128)(2,1)S(1)}, u32[]{:S(2)}, u32[]{:S(2)}) async-start(bf16[64,176,128]{2,1,0:T(8,128)(2,1)} %filter.2), calls=%async_computation | async-start | bytes 5767168 | tf_op jit(solution)/shard_map/all_to_all | solution.py:554
  57.6 5.7 %copy-start = (bf16[64,176,128]{2,1,0:T(8,128)(2,1)}, bf16[64,176,128]{2,1,0:T(8,128)(2,1)S(1)}, u32[]{:S(2)}) copy-start(bf16[64,176,128]{2,1,0:T(8,128)(2,1)S(1)} %all-to-all-done.first_ref.refs_0_) | copy-start | bytes 8650756
  57.6 28.6 %all-to-all-start.1 = ((bf16[64,96,128]{2,1,0:T(8,128)(2,1)}), bf16[64,96,128]{2,1,0:T(8,128)(2,1)}, u32[]{:S(2)}, u32[]{:S(2)}) async-start(bf16[64,96,128]{2,1,0:T(8,128)(2,1)} %filter.3), calls=%async_computation.1 | async-start | bytes 3145728 | tf_op jit(solution)/shard_map/all_to_all | solution.py:554
  62.3 1.0 copy-start.3
  80.5 20.5 %collective-permute-start.5 = (bf16[8,128,128]{2,1,0:T(8,128)(2,1)}, bf16[8,128,128]{2,1,0:T(8,128)(2,1)S(1)}, u32[]{:S(2)}, u32[]{:S(2)}) collective-permute-start(bf16[8,128,128]{2,1,0:T(8,128)(2,1)} %get-tuple-element.32), channel_id=1, source_target_pairs={{0,64},{32,96},{64,0},{96,32},{1,65},{33,97},{65,1},{97,33},{2,66}... | collective-permute-start | bytes 786440 | tf_op jit(solution)/shard_map/ppermute | solution.py:592
  84.5 16.5 %collective-permute-start.6 = (bf16[8,128,128]{2,1,0:T(8,128)(2,1)}, bf16[8,128,128]{2,1,0:T(8,128)(2,1)S(1)}, u32[]{:S(2)}, u32[]{:S(2)}) collective-permute-start(bf16[8,128,128]{2,1,0:T(8,128)(2,1)} %get-tuple-element.33), channel_id=1, source_target_pairs={{0,32},{32,0},{64,96},{96,64},{1,33},{33,1},{65,97},{97,65},{2,34}... | collective-permute-start | bytes 786440 | tf_op jit(solution)/shard_map/ppermute | solution.py:592
  85.5 15.5 %collective-permute-start.7 = (bf16[8,128,128]{2,1,0:T(8,128)(2,1)}, bf16[8,128,128]{2,1,0:T(8,128)(2,1)S(1)}, u32[]{:S(2)}, u32[]{:S(2)}) collective-permute-start(bf16[8,128,128]{2,1,0:T(8,128)(2,1)} %get-tuple-element.34), channel_id=1, source_target_pairs={{0,96},{32,64},{64,32},{96,0},{1,97},{33,65},{65,33},{97,1},{2,98}... | collective-permute-start | bytes 786440 | tf_op jit(solution)/shard_map/ppermute | solution.py:592
  86.2 14.8 %copy-start.1 = (f32[8,128,128]{2,1,0:T(8,128)S(1)}, f32[8,128,128]{2,1,0:T(8,128)}, u32[]{:S(2)}) copy-start(f32[8,128,128]{2,1,0:T(8,128)} %get-tuple-element.31) | copy-start | bytes 1572868
  95.9 15.5 %copy-start.2 = (f32[8,128,128]{2,1,0:T(8,128)S(1)}, f32[8,128,128]{2,1,0:T(8,128)}, u32[]{:S(2)}) copy-start(f32[8,128,128]{2,1,0:T(8,128)} %get-tuple-element.27) | copy-start | bytes 1572868
  95.9 11.4 %collective-permute-start.2 = (bf16[8,128,128]{2,1,0:T(8,128)(2,1)}, bf16[8,128,128]{2,1,0:T(8,128)(2,1)S(1)}, u32[]{:S(2)}, u32[]{:S(2)}) collective-permute-start(bf16[8,128,128]{2,1,0:T(8,128)(2,1)} %get-tuple-element.28), channel_id=1, source_target_pairs={{0,64},{32,96},{64,0},{96,32},{1,65},{33,97},{65,1},{97,33},{2,66}... | collective-permute-start | bytes 786440 | tf_op jit(solution)/shard_map/ppermute | solution.py:592
  99.9 11.5 %collective-permute-start.3 = (bf16[8,128,128]{2,1,0:T(8,128)(2,1)}, bf16[8,128,128]{2,1,0:T(8,128)(2,1)S(1)}, u32[]{:S(2)}, u32[]{:S(2)}) collective-permute-start(bf16[8,128,128]{2,1,0:T(8,128)(2,1)} %get-tuple-element.29), channel_id=1, source_target_pairs={{0,32},{32,0},{64,96},{96,64},{1,33},{33,1},{65,97},{97,65},{2,34}... | collective-permute-start | bytes 786440 | tf_op jit(solution)/shard_map/ppermute | solution.py:592
  101.0 10.5 %collective-permute-start.4 = (bf16[8,128,128]{2,1,0:T(8,128)(2,1)}, bf16[8,128,128]{2,1,0:T(8,128)(2,1)S(1)}, u32[]{:S(2)}, u32[]{:S(2)}) collective-permute-start(bf16[8,128,128]{2,1,0:T(8,128)(2,1)} %get-tuple-element.30), channel_id=1, source_target_pairs={{0,96},{32,64},{64,32},{96,0},{1,97},{33,65},{65,33},{97,1},{2,98}... | collective-permute-start | bytes 786440 | tf_op jit(solution)/shard_map/ppermute | solution.py:592

commit v6 on v5

--- a/solution.py
+++ b/solution.py
@@ -18,9 +18,8 @@
 BEGIN, END = FROM + 8, TO - 8
 EDGE = END - BEGIN
 REACH = 16
-FACTS = 16
+FACTS = 8
 FILTER_COLUMNS = 2048
-UNROLL = 2
 UPPER_PARTS = 4
 FILTER_VMEM = 60 * 1024 * 1024
 UPPER_VMEM = 60 * 1024 * 1024
@@ -49,8 +48,8 @@
 def filter_kernel(spans, owners, halo_count, owner_ref, taps_ref, *refs):
     exposure_ref, variance_ref, mask_ref = refs[:3]
     halo_refs = refs[3 : 3 + halo_count]
-    pair_refs, out = refs[3 + halo_count : -14], refs[-14]
-    framed, usable_ref, across_ref, down_ref, staged, empty_ref, facts_ref = refs[-13:-6]
+    pair_refs, out = refs[3 + halo_count : -15], refs[-15]
+    framed, usable_ref, across_ref, down_ref, staged, facts_ref, known_ref, told_ref = refs[-14:-6]
     slot_ref, count_ref, here, near, done, cleared = refs[-6:]
     rows, columns = mask_ref.shape
     parted, height, tall = segments(spans, rows)
@@ -91,12 +90,6 @@
     for part in range(parts):
         for copy in fetched(part):
             copy.start()
-    if pair_refs:
-        empty_ref[...] = jnp.zeros(empty_ref.shape, jnp.bfloat16)
-        clear = pltpu.make_async_copy(
-            empty_ref, out.at[:, pl.ds(2 * height, FACTS), :], cleared.at[0]
-        )
-        clear.start()
 
     for owner in range(count_ref.shape[0]):
         count_ref[owner] = 0
@@ -106,6 +99,7 @@
         slot_ref[block] = owner * CAP + rank
         count_ref[owner] = rank + 1
 
+    sent = []
     if pair_refs:
         stretch_ref, offset_ref, patch_ref = pair_refs
         pairs, blocks = patch_ref.shape
@@ -117,6 +111,19 @@
                 )
         facts_ref[4 * pairs : 5 * pairs, :blocks] = patch_ref[...].astype(jnp.float32)
         facts_ref[...] = facts_ref[...].T
+        known_ref[...] = jnp.zeros(known_ref.shape, jnp.float32)
+        for block in range(blocks):
+            slot = slot_ref[block]
+            begin = pl.multiple_of((slot % CAP) * FACTS, FACTS)
+            known_ref[slot // CAP, pl.ds(begin, FACTS), :] = jnp.broadcast_to(
+                facts_ref[block : block + 1, :], (FACTS, BS)
+            )
+        told_ref[...] = known_ref[...].astype(jnp.bfloat16)
+        tell = pltpu.make_async_copy(
+            told_ref, out.at[:, pl.ds(2 * CAP * height, CAP * FACTS), :], cleared.at[0]
+        )
+        tell.start()
+        sent.append(tell)
 
     margin = jnp.zeros((tall, BS), jnp.bfloat16)
     empty = jnp.zeros((BS, BS), jnp.bfloat16)
@@ -151,7 +158,6 @@
     for copy in fetched(0):
         copy.wait()
     tiles = part_columns // wide
-    sent = []
     for part in range(parts):
         if part + 1 < parts:
             for copy in fetched(part + 1):
@@ -189,14 +195,15 @@
                 lanes = slice(block * BS, (block + 1) * BS)
                 staged[index, :height, :] = weighted[:, lanes]
                 staged[index, height : 2 * height, :] = weight[:, lanes]
-                if pair_refs:
-                    row = jnp.broadcast_to(facts_ref[index : index + 1, :], (FACTS, BS))
-                    staged[index, 2 * height :, :] = row.astype(jnp.bfloat16)
-        if pair_refs and part == 0:
-            clear.wait()
         for index in range(part * tiles * 2, (part + 1) * tiles * 2):
             copy = pltpu.make_async_copy(
-                staged.at[index], out.at[slot_ref[index]], done.at[index]
+                staged.at[index],
+                out.at[
+                    slot_ref[index] // CAP,
+                    pl.ds(pl.multiple_of((slot_ref[index] % CAP) * 2 * height, HALO), 2 * height),
+                    :,
+                ],
+                done.at[index],
             )
             copy.start()
             sent.append(copy)
@@ -207,8 +214,7 @@
 def filtered(spans, owners, owner, taps, images, halos=(), facts=()):
     rows, columns = images[2].shape
     _, height, frame = segments(spans, rows)
-    tall = 2 * height + (FACTS if facts else 0)
-    slots = owners * CAP
+    tall = CAP * (2 * height + (FACTS if facts else 0))
     blocks = columns // BS
     parts = columns // FILTER_COLUMNS
     smem = pl.BlockSpec(memory_space=pltpu.SMEM)
@@ -223,7 +229,7 @@
     return pl.pallas_call(
         functools.partial(filter_kernel, spans, owners, len(halos)),
         grid=(1,),
-        out_shape=jax.ShapeDtypeStruct((slots, tall, BS), jnp.bfloat16),
+        out_shape=jax.ShapeDtypeStruct((owners, tall, BS), jnp.bfloat16),
         in_specs=specs,
         out_specs=hbm,
         scratch_shapes=[
@@ -231,9 +237,10 @@
             pltpu.VMEM((height, columns), jnp.int32),
             pltpu.VMEM((2, 4 * BS, 2 * BS), jnp.bfloat16),
             pltpu.VMEM((2, height, frame), jnp.bfloat16),
-            pltpu.VMEM((blocks, tall, BS), jnp.bfloat16),
-            pltpu.VMEM((slots, FACTS, BS), jnp.bfloat16),
+            pltpu.VMEM((blocks, 2 * height, BS), jnp.bfloat16),
             pltpu.VMEM((BS, BS), jnp.float32),
+            pltpu.VMEM((owners, CAP * FACTS, BS), jnp.float32),
+            pltpu.VMEM((owners, CAP * FACTS, BS), jnp.bfloat16),
             pltpu.SMEM((blocks,), jnp.int32),
             pltpu.SMEM((owners,), jnp.int32),
             pltpu.SemaphoreType.DMA((3 * len(spans), parts)),
@@ -279,8 +286,12 @@
     def fetched(part):
         return [
             pltpu.make_async_copy(
-                first_ref.at[pl.ds(base + part * per_part, per_part), pl.ds(0, 2 * CUT), :],
-                block_ref.at[pl.ds(base + part * per_part, per_part)],
+                first_ref.at[
+                    pl.ds((base + part * per_part) // CAP, per_part // CAP),
+                    pl.ds(0, 2 * CAP * CUT),
+                    :,
+                ],
+                block_ref.at[pl.ds((base + part * per_part) // CAP, per_part // CAP)],
                 arrived.at[index, part],
             )
             for index, base in enumerate((0, half))
@@ -341,7 +352,8 @@
 
     numbers = rows.astype(jnp.bfloat16)
 
-    def build(m):
+    def build(owner, rank):
+        m = owner * CAP + rank
         stretch = spread_ref[0, pl.ds(m, 1), :]
         offset = spread_ref[1, pl.ds(m, 1), :]
         x = (1.0 + stretch) * place_ref[0] + offset - place_ref[1]
@@ -378,8 +390,13 @@
                     column = jnp.where(lag == jnp.bfloat16(k - 3), tap, column)
                 column_ref[slot, pair] = column
                 columns.append(column)
+            holder, base = owner + which * (half // CAP), rank * 2 * CUT
             source = jnp.concatenate(
-                [block_ref[slot, :CUT, :], block_ref[slot, CUT : 2 * CUT, :]], axis=1
+                [
+                    block_ref[holder, base : base + CUT, :],
+                    block_ref[holder, base + CUT : base + 2 * CUT, :],
+                ],
+                axis=1,
             )
             aims = [aim_ref[slot * pairs + pair] for pair in range(pairs)]
             accumulate(total, aims, jnp.concatenate(stack, axis=0), source, columns)
@@ -389,10 +406,10 @@
         for copy in fetched(part):
             copy.wait()
 
-        @pl.loop(0, per_part // UNROLL)
-        def _(batch):
-            for inner in range(UNROLL):
-                build(part * per_part + batch * UNROLL + inner)
+        @pl.loop(0, per_part // CAP)
+        def _(owner):
+            for rank in range(CAP):
+                build(part * (per_part // CAP) + owner, rank)
 
         for copy in returned(part):
             copy.start()
@@ -405,7 +422,7 @@
 
 
 def upper_warp(aims, table, first, pairs, groups):
-    slots = first.shape[0]
+    slots = first.shape[0] * CAP
     second = jax.ShapeDtypeStruct((slots, pairs, BS - EDGE, BS), jnp.bfloat16)
     column = jax.ShapeDtypeStruct((slots, pairs, BS, BS), jnp.bfloat16)
     hbm = pl.BlockSpec(memory_space=pltpu.HBM)
@@ -420,7 +437,7 @@
         out_specs=[hbm, hbm]
         + [pl.BlockSpec((PB_DEV, 2 * EDGE, BS), lambda i: (0, 0, 0))] * groups,
         scratch_shapes=[
-            pltpu.VMEM((slots, 2 * CUT, BS), jnp.bfloat16),
+            pltpu.VMEM((slots // CAP, 2 * CAP * CUT, BS), jnp.bfloat16),
             pltpu.VMEM(second.shape, second.dtype),
             pltpu.VMEM(column.shape, column.dtype),
             pltpu.SemaphoreType.DMA((2, UPPER_PARTS)),
@@ -450,16 +467,18 @@
     (first, second, row, column), outs = refs[:4], refs[4:-6]
     first_ref, second_ref, row_ref, column_ref, total, arrived = refs[-6:]
     parts = arrived.shape[1]
-    per_part = first_ref.shape[0] // parts
+    per_part = row_ref.shape[0] // parts
     far = BS - CUT
 
     def copies(part):
         slots = pl.ds(part * per_part, per_part)
+        holders = pl.ds(part * per_part // CAP, per_part // CAP)
         pieces = [
             (
-                first.at[slots, pl.ds(begin, count), :],
-                first_ref.at[slots, pl.ds(place, count), :],
-            )
+                first.at[holders, pl.ds(rank * 2 * CUT + begin, count), :],
+                first_ref.at[holders, pl.ds(rank * 4 * REACH + place, count), :],
+            )
+            for rank in range(CAP)
             for begin, count, place in (
                 (0, REACH, 0),
                 (CUT - REACH, 2 * REACH, REACH),
@@ -467,7 +486,7 @@
             )
         ]
         pieces += [
-            (second.at[slots], second_ref.at[slots]),
+            (second.at[holders], second_ref.at[holders]),
             (row.at[slots], row_ref.at[slots]),
             (column.at[slots], column_ref.at[slots]),
         ]
@@ -487,17 +506,22 @@
             copy.wait()
         for inner in range(per_part):
             slot = part * per_part + inner
+            holder = part * (per_part // CAP) + inner // CAP
+            near_at, far_at = (inner % CAP) * 4 * REACH, (inner % CAP) * 2 * far
             source = jnp.concatenate(
                 [
                     jnp.concatenate(
                         [
-                            second_ref[slot, plane * far : plane * far + FROM, :],
-                            first_ref[slot, plane * 2 * REACH : (plane + 1) * 2 * REACH, :],
-                            second_ref[slot, plane * far + FROM : (plane + 1) * far, :],
+                            second_ref[holder, begin : begin + FROM, :],
+                            first_ref[holder, near : near + 2 * REACH, :],
+                            second_ref[holder, begin + FROM : begin + far, :],
                         ],
                         axis=0,
                     )
-                    for plane in range(2)
+                    for near, begin in (
+                        (near_at, far_at),
+                        (near_at + 2 * REACH, far_at + far),
+                    )
                 ],
                 axis=1,
             )
@@ -519,12 +543,12 @@
         + [pl.BlockSpec(memory_space=pl.ANY)] * len(operands),
         out_specs=[pl.BlockSpec(memory_space=pltpu.VMEM)] * groups,
         scratch_shapes=[
-            pltpu.VMEM((slots, 4 * REACH, BS), first.dtype),
+            pltpu.VMEM((slots // CAP, 4 * CAP * REACH, BS), first.dtype),
             pltpu.VMEM(second.shape, second.dtype),
             pltpu.VMEM(row_maps.shape, row_maps.dtype),
             pltpu.VMEM(column_maps.shape, column_maps.dtype),
             pltpu.VMEM((groups * PB_DEV + 1, 2 * height, BS), jnp.float32),
-            pltpu.SemaphoreType.DMA((6, LOWER_PARTS)),
+            pltpu.SemaphoreType.DMA((3 * CAP + 3, LOWER_PARTS)),
         ],
         out_shape=[
             jax.ShapeDtypeStruct(
@@ -574,7 +598,7 @@
     first, outer_planes = lax.optimization_barrier((first, outer_planes))
     second = exchange(outer_planes)
 
-    table = first[:, 2 * CUT, :].astype(jnp.float32)
+    table = first[:, 2 * CAP * CUT :: FACTS, :].astype(jnp.float32).reshape(slots, BS)
     patch = table[:, 4 * pairs : 5 * pairs].astype(jnp.int32)
     distance = (patch // PB_DEV) ^ lax.axis_index("visit")
     aims = jnp.where(

time: 113 us -> 111 us (0.982)
  waiting for transfers between devices: 43.2 us -> 41.6 us
    all_to_all x2, waiting for transfers between devices: 32.9 us -> 31.3 us  [exchange(): return lax.all_to_all(array, 'sky', split_axis=0, concat_axis=0, tiled=True)]
  transfers between devices with their start and end apart: 10 -> 10, of which waited for: 4 -> 4; matrix products, arithmetic and copies ran while one was open for 1% -> 1% of each run, Pallas kernels for 36% -> 37%
where the time goes in v6:
time: 111 us
  waiting for transfers between devices  41.6 us (37%)
  Pallas kernels  40.7 us (37%)
  starting transfers between devices  24.1 us (22%)
  local copies, waits for them, and re-layouts  2.8 us (3%)
  other arithmetic  1.5 us (1%)
    all_to_all x2, waiting for transfers between devices, exchange(): return lax.all_to_all(array, 'sky', split_axis=0, concat_axis=0, tiled=True)  31.3 us
    pallas_call x1, Pallas kernels, upper_warp(): pl.pallas_call(functools.partial(upper_kernel, pairs), grid=(1,), in_spec...  17.2 us
    pallas_call x2, Pallas kernels, filtered(): pl.pallas_call(functools.partial(filter_kernel, spans, owners, len(halos)...  13.7 us
    ppermute x6, waiting for transfers between devices, coadd(): whole = whole + lax.ppermute(sums[step], 'visit', ring).astype(jnp.float32)  10.3 us
    ppermute x6, starting transfers between devices, coadd(): whole = whole + lax.ppermute(sums[step], 'visit', ring).astype(jnp.float32)  10.1 us
    pallas_call x1, Pallas kernels, lower_warp(): pl.pallas_call(functools.partial(lower_kernel, pairs), in_specs=[pl.Block...  9.83 us
    all_to_all x2, starting transfers between devices, exchange(): return lax.all_to_all(array, 'sky', split_axis=0, concat_axis=0, tiled=True)  8.77 us
    ppermute x1, starting transfers between devices, local(): lax.ppermute(high, 'sky', [((i + 1) % owners, i) for i in range(owners)])  5.12 us
  transfers between devices with their start and end apart: 10, of which 4 were waited for; matrix products, arithmetic and copies ran while one was open for 1% of the time, Pallas kernels for 37%

profile of v6, /device:TPU:0, one launch (start us, length us, event | category | flops | bytes accessed | tf_op | source)
XLA Modules:
  0.0 110.9 jit_solution(7126837506814674291)
XLA Ops:
  0.0 1.1 %fusion.11 = (bf16[1,16,4096]{2,1,0:T(8,128)(2,1)S(1)}, bf16[1,16,4096]{2,1,0:T(8,128)(2,1)S(1)}, bf16[1,16,4096]{2,1,0:T(8,128)(2,1)S(1)}, bf16[1,16,4096]{2,1,0:T(8,128)(2,1)S(1)}) fusion(bf16[1,128,4096]{2,1,0:T(8,128)(2,1)} %param.8, bf16[1,128,4096]{2,1,0:T(8,128)(2,1)} %param.9), kind=kLoop, calls=%fused_computation.26 | loop fusion | bytes 1048576 | tf_op jit(solution)/shard_map/slice | solution.py:581
  1.3 5.1 %collective-permute-start.1 = (bf16[2,16,4096]{2,1,0:T(8,128)(2,1)S(1)}, bf16[2,16,4096]{2,1,0:T(8,128)(2,1)S(1)}, u32[]{:S(2)}, u32[]{:S(2)}) collective-permute-start(bf16[2,16,4096]{2,1,0:T(8,128)(2,1)S(1)} %pad_maximum_fusion.2), channel_id=1, source_target_pairs={{1,0},{2,1},{3,2},{4,3},{5,4},{6,5},{7,6},{8,7},{9,8},{10,9},{11,1... | collective-permute-start | bytes 786440 | tf_op jit(solution)/shard_map/ppermute | solution.py:583
  6.4 7.1 %filter.2 = bf16[32,336,128]{2,1,0:T(8,128)(2,1)} custom-call(s32[1,1,32]{2,1,0:T(1,128)} %owner_ref.3, bf16[1,2,21]{2,1,0:T(2,128)(2,1)} %taps_ref.3, bf16[128,4096]{1,0:T(8,128)(2,1)} %bitcast.15, bf16[128,4096]{1,0:T(8,128)(2,1)} %bitcast.17, s32[128,4096]{1,0:T(8,128)} %bitcast.19, bf16[4,2,32]{2,1,0:T(2,128)(2,1)} %bitcast.21, ...), custom_call_target="tpu_custom_call" | custom-call | flops 2000000000 | bytes 16777216 | tf_op jit(solution)/shard_map/filter/pallas_call | solution.py:229
  13.5 0.7 copy-done.4
  14.3 4.1 %all-to-all-start = ((bf16[32,336,128]{2,1,0:T(8,128)(2,1)}), bf16[32,336,128]{2,1,0:T(8,128)(2,1)S(1)}, u32[]{:S(2)}, u32[]{:S(2)}) async-start(bf16[32,336,128]{2,1,0:T(8,128)(2,1)} %filter.2), calls=%async_computation | async-start | bytes 5505024 | tf_op jit(solution)/shard_map/all_to_all | solution.py:578
  18.3 6.6 %filter.3 = bf16[32,192,128]{2,1,0:T(8,128)(2,1)} custom-call(s32[1,1,32]{2,1,0:T(1,128)} %owner_ref.3, bf16[1,2,21]{2,1,0:T(2,128)(2,1)} %taps_ref.3, bf16[128,4096]{1,0:T(8,128)(2,1)} %bitcast.16, bf16[128,4096]{1,0:T(8,128)(2,1)} %bitcast.18, s32[128,4096]{1,0:T(8,128)} %bitcast.20, bf16[2,16,4096]{2,1,0:T(8,128)(2,1)} %copy-done.4, ...), custom_call_target="tpu_custom_call" | custom-call | flops 2000000000 | bytes 16777216 | tf_op jit(solution)/shard_map/filter/pallas_call | solution.py:229
  25.0 30.9 %all-to-all-done.first_ref.refs_0_ = bf16[32,336,128]{2,1,0:T(8,128)(2,1)S(1)} async-done(((bf16[32,336,128]{2,1,0:T(8,128)(2,1)}), bf16[32,336,128]{2,1,0:T(8,128)(2,1)S(1)}, u32[]{:S(2)}, u32[]{:S(2)}) %all-to-all-start) | async-done | bytes 2752544 | tf_op jit(solution)/shard_map/all_to_all | solution.py:578
  55.8 4.7 %all-to-all-start.1 = ((bf16[32,192,128]{2,1,0:T(8,128)(2,1)}), bf16[32,192,128]{2,1,0:T(8,128)(2,1)}, u32[]{:S(2)}, u32[]{:S(2)}) async-start(bf16[32,192,128]{2,1,0:T(8,128)(2,1)} %filter.3), calls=%async_computation.1 | async-start | bytes 3145728 | tf_op jit(solution)/shard_map/all_to_all | solution.py:578
  60.6 0.2 slice.43
  60.8 0.2 fusion.10
  60.9 0.1 fusion.5
  61.1 0.7 reshape.34.aim_ref
  61.8 17.2 %upper_warp.1 = (bf16[64,4,64,128]{3,2,1,0:T(8,128)(2,1)}, bf16[64,4,128,128]{3,2,1,0:T(8,128)(2,1)}, f32[8,128,128]{2,1,0:T(8,128)}, bf16[8,128,128]{2,1,0:T(8,...) custom-call(s32[256]{0:T(256)} %reshape.34.aim_ref, f32[64,128]{1,0:T(8,128)} %copy-done.3, ...), custom_call_target="tpu_custom_call" | custom-call | flops 10000000000 | bytes 33554432 | tf_op jit(solution)/shard_map/upper_warp/pallas_call | solution.py:429
  79.0 4.0 %collective-permute-start.5 = (bf16[8,128,128]{2,1,0:T(8,128)(2,1)}, bf16[8,128,128]{2,1,0:T(8,128)(2,1)S(1)}, u32[]{:S(2)}, u32[]{:S(2)}) collective-permute-start(bf16[8,128,128]{2,1,0:T(8,128)(2,1)} %get-tuple-element.32), channel_id=1, source_target_pairs={{0,64},{32,96},{64,0},{96,32},{1,65},{33,97},{65,1},{97,33},{2,66}... | collective-permute-start | bytes 786440 | tf_op jit(solution)/shard_map/ppermute | solution.py:616
  83.0 1.0 collective-permute-start.6
  84.1 0.4 all-to-all-done.1.refs_1_
  84.5 9.8 %lower_warp.1 = (f32[8,128,128]{2,1,0:T(8,128)}, bf16[8,128,128]{2,1,0:T(8,128)(2,1)}, bf16[8,128,128]{2,1,0:T(8,128)(2,1)}, bf16[8,128,128]{2,1,0:T(8,128)(2,1)}) custom-call(s32[256]{0:T(256)} %reshape.34.aim_ref, bf16[32,336,128]{2,1,0:T(8,128)(2,1)} %copy-done, bf16[32,192,128]{2,1,0:T(8,128)(2,1)} %all-to-all-done.1.refs_1_, ...), custom_call_target="tpu_custom_call" | custom-call | flops 6000000000 | bytes 33554432 | tf_op jit(solution)/shard_map/lower_warp/pallas_call | solution.py:540
  94.3 4.0 %collective-permute-start.2 = (bf16[8,128,128]{2,1,0:T(8,128)(2,1)}, bf16[8,128,128]{2,1,0:T(8,128)(2,1)S(1)}, u32[]{:S(2)}, u32[]{:S(2)}) collective-permute-start(bf16[8,128,128]{2,1,0:T(8,128)(2,1)} %get-tuple-element.28), channel_id=1, source_target_pairs={{0,64},{32,96},{64,0},{96,32},{1,65},{33,97},{65,1},{97,33},{2,66}... | collective-permute-start | bytes 786440 | tf_op jit(solution)/shard_map/ppermute | solution.py:616
  98.4 1.0 collective-permute-start.3
  99.4 0.1 convert_add_fusion
  99.6 6.2 %collective-permute-done.2 = bf16[8,128,128]{2,1,0:T(8,128)(2,1)S(1)} collective-permute-done((bf16[8,128,128]{2,1,0:T(8,128)(2,1)}, bf16[8,128,128]{2,1,0:T(8,128)(2,1)S(1)}, u32[]{:S(2)}, u32[]{:S(2)}) %collective-permute-start.2) | collective-permute-done | bytes 262176 | tf_op jit(solution)/shard_map/ppermute | solution.py:616
  105.8 4.1 %collective-permute-done.3 = bf16[8,128,128]{2,1,0:T(8,128)(2,1)S(1)} collective-permute-done((bf16[8,128,128]{2,1,0:T(8,128)(2,1)}, bf16[8,128,128]{2,1,0:T(8,128)(2,1)S(1)}, u32[]{:S(2)}, u32[]{:S(2)}) %collective-permute-start.3) | collective-permute-done | bytes 262176 | tf_op jit(solution)/shard_map/ppermute | solution.py:616
  109.9 0.1 convert_add_fusion.1
  110.1 0.8 pad_maximum_fusion
  (27 shorter events, 0.4 us)
Async XLA Ops:
  1.2 12.3 %collective-permute-start = (bf16[2,16,4096]{2,1,0:T(8,128)(2,1)S(1)}, bf16[2,16,4096]{2,1,0:T(8,128)(2,1)S(1)}, u32[]{:S(2)}, u32[]{:S(2)}) collective-permute-start(bf16[2,16,4096]{2,1,0:T(8,128)(2,1)S(1)} %pad_maximum_fusion.1), channel_id=1, source_target_pairs={{0,1},{1,2},{2,3},{3,4},{4,5},{5,6},{6,7},{7,8},{8,9},{9,10},{10,1... | collective-permute-start | bytes 786440 | tf_op jit(solution)/shard_map/ppermute | solution.py:582
  1.3 12.2 %collective-permute-start.1 = (bf16[2,16,4096]{2,1,0:T(8,128)(2,1)S(1)}, bf16[2,16,4096]{2,1,0:T(8,128)(2,1)S(1)}, u32[]{:S(2)}, u32[]{:S(2)}) collective-permute-start(bf16[2,16,4096]{2,1,0:T(8,128)(2,1)S(1)} %pad_maximum_fusion.2), channel_id=1, source_target_pairs={{1,0},{2,1},{3,2},{4,3},{5,4},{6,5},{7,6},{8,7},{9,8},{10,9},{11,1... | collective-permute-start | bytes 786440 | tf_op jit(solution)/shard_map/ppermute | solution.py:583
  13.5 0.7 copy-start.4
  13.5 0.8 copy-start.5
  14.3 41.6 %all-to-all-start = ((bf16[32,336,128]{2,1,0:T(8,128)(2,1)}), bf16[32,336,128]{2,1,0:T(8,128)(2,1)S(1)}, u32[]{:S(2)}, u32[]{:S(2)}) async-start(bf16[32,336,128]{2,1,0:T(8,128)(2,1)} %filter.2), calls=%async_computation | async-start | bytes 5505024 | tf_op jit(solution)/shard_map/all_to_all | solution.py:578
  55.8 5.9 %copy-start = (bf16[32,336,128]{2,1,0:T(8,128)(2,1)}, bf16[32,336,128]{2,1,0:T(8,128)(2,1)S(1)}, u32[]{:S(2)}) copy-start(bf16[32,336,128]{2,1,0:T(8,128)(2,1)S(1)} %all-to-all-done.first_ref.refs_0_) | copy-start | bytes 8257540
  55.8 28.6 %all-to-all-start.1 = ((bf16[32,192,128]{2,1,0:T(8,128)(2,1)}), bf16[32,192,128]{2,1,0:T(8,128)(2,1)}, u32[]{:S(2)}, u32[]{:S(2)}) async-start(bf16[32,192,128]{2,1,0:T(8,128)(2,1)} %filter.3), calls=%async_computation.1 | async-start | bytes 3145728 | tf_op jit(solution)/shard_map/all_to_all | solution.py:578
  60.7 1.0 copy-start.3
  79.0 20.4 %collective-permute-start.5 = (bf16[8,128,128]{2,1,0:T(8,128)(2,1)}, bf16[8,128,128]{2,1,0:T(8,128)(2,1)S(1)}, u32[]{:S(2)}, u32[]{:S(2)}) collective-permute-start(bf16[8,128,128]{2,1,0:T(8,128)(2,1)} %get-tuple-element.32), channel_id=1, source_target_pairs={{0,64},{32,96},{64,0},{96,32},{1,65},{33,97},{65,1},{97,33},{2,66}... | collective-permute-start | bytes 786440 | tf_op jit(solution)/shard_map/ppermute | solution.py:616
  83.0 16.4 %collective-permute-start.6 = (bf16[8,128,128]{2,1,0:T(8,128)(2,1)}, bf16[8,128,128]{2,1,0:T(8,128)(2,1)S(1)}, u32[]{:S(2)}, u32[]{:S(2)}) collective-permute-start(bf16[8,128,128]{2,1,0:T(8,128)(2,1)} %get-tuple-element.33), channel_id=1, source_target_pairs={{0,32},{32,0},{64,96},{96,64},{1,33},{33,1},{65,97},{97,65},{2,34}... | collective-permute-start | bytes 786440 | tf_op jit(solution)/shard_map/ppermute | solution.py:616
  84.1 15.3 %collective-permute-start.7 = (bf16[8,128,128]{2,1,0:T(8,128)(2,1)}, bf16[8,128,128]{2,1,0:T(8,128)(2,1)S(1)}, u32[]{:S(2)}, u32[]{:S(2)}) collective-permute-start(bf16[8,128,128]{2,1,0:T(8,128)(2,1)} %get-tuple-element.34), channel_id=1, source_target_pairs={{0,96},{32,64},{64,32},{96,0},{1,97},{33,65},{65,33},{97,1},{2,98}... | collective-permute-start | bytes 786440 | tf_op jit(solution)/shard_map/ppermute | solution.py:616
  84.5 14.9 %copy-start.1 = (f32[8,128,128]{2,1,0:T(8,128)S(1)}, f32[8,128,128]{2,1,0:T(8,128)}, u32[]{:S(2)}) copy-start(f32[8,128,128]{2,1,0:T(8,128)} %get-tuple-element.31) | copy-start | bytes 1572868
  94.3 15.6 %copy-start.2 = (f32[8,128,128]{2,1,0:T(8,128)S(1)}, f32[8,128,128]{2,1,0:T(8,128)}, u32[]{:S(2)}) copy-start(f32[8,128,128]{2,1,0:T(8,128)} %get-tuple-element.27) | copy-start | bytes 1572868
  94.3 11.5 %collective-permute-start.2 = (bf16[8,128,128]{2,1,0:T(8,128)(2,1)}, bf16[8,128,128]{2,1,0:T(8,128)(2,1)S(1)}, u32[]{:S(2)}, u32[]{:S(2)}) collective-permute-start(bf16[8,128,128]{2,1,0:T(8,128)(2,1)} %get-tuple-element.28), channel_id=1, source_target_pairs={{0,64},{32,96},{64,0},{96,32},{1,65},{33,97},{65,1},{97,33},{2,66}... | collective-permute-start | bytes 786440 | tf_op jit(solution)/shard_map/ppermute | solution.py:616
  98.4 11.5 %collective-permute-start.3 = (bf16[8,128,128]{2,1,0:T(8,128)(2,1)}, bf16[8,128,128]{2,1,0:T(8,128)(2,1)S(1)}, u32[]{:S(2)}, u32[]{:S(2)}) collective-permute-start(bf16[8,128,128]{2,1,0:T(8,128)(2,1)} %get-tuple-element.29), channel_id=1, source_target_pairs={{0,32},{32,0},{64,96},{96,64},{1,33},{33,1},{65,97},{97,65},{2,34}... | collective-permute-start | bytes 786440 | tf_op jit(solution)/shard_map/ppermute | solution.py:616
  99.4 10.5 %collective-permute-start.4 = (bf16[8,128,128]{2,1,0:T(8,128)(2,1)}, bf16[8,128,128]{2,1,0:T(8,128)(2,1)S(1)}, u32[]{:S(2)}, u32[]{:S(2)}) collective-permute-start(bf16[8,128,128]{2,1,0:T(8,128)(2,1)} %get-tuple-element.30), channel_id=1, source_target_pairs={{0,96},{32,64},{64,32},{96,0},{1,97},{33,65},{65,33},{97,1},{2,98}... | collective-permute-start | bytes 786440 | tf_op jit(solution)/shard_map/ppermute | solution.py:616

commit v7 on v6

--- a/solution.py
+++ b/solution.py
@@ -579,8 +579,15 @@
 
     low = jnp.concatenate([exposure[:, rows - HALO :], variance[:, rows - HALO :]], axis=0)
     high = jnp.concatenate([exposure[:, :HALO], variance[:, :HALO]], axis=0)
-    top = lax.ppermute(low, "sky", [(i, (i + 1) % owners) for i in range(owners)])
-    bottom = lax.ppermute(high, "sky", [((i + 1) % owners, i) for i in range(owners)])
+    even = lax.axis_index("sky") % 2 == 0
+    near = lax.ppermute(
+        jnp.where(even, low, high), "sky", [(i, i ^ 1) for i in range(owners)]
+    )
+    far = lax.ppermute(
+        jnp.where(even, high, low),
+        "sky",
+        [(i, (i - 1 if i % 2 == 0 else i + 1) % owners) for i in range(owners)],
+    )
 
     facts = [
         pair_stretch.transpose(0, 1, 3, 4, 2).reshape(pairs, 2, block_count),
@@ -591,9 +598,10 @@
     images = [array.reshape(rows, columns) for array in (exposure, variance, pixel_mask)]
     common = (owners, block_owner, psf_kernel, images)
     inner_planes = filtered([(FROM, TO)], *common, facts=facts)
-    inner_planes, top, bottom = lax.optimization_barrier((inner_planes, top, bottom))
+    inner_planes, near, far = lax.optimization_barrier((inner_planes, near, far))
     first = exchange(inner_planes)
 
+    top, bottom = jnp.where(even, far, near), jnp.where(even, near, far)
     outer_planes = filtered([(0, FROM), (TO, rows)], *common, halos=(top, bottom))
     first, outer_planes = lax.optimization_barrier((first, outer_planes))
     second = exchange(outer_planes)

time: 111 us -> 111 us (level)
  transfers between devices with their start and end apart: 10 -> 10, of which waited for: 4 -> 4; matrix products, arithmetic and copies ran while one was open for 1% -> 2% of each run, Pallas kernels for 37% -> 37%
where the time goes in v7:
time: 111 us; the launch traced here: 110 us
  waiting for transfers between devices  40.8 us (37%)
  Pallas kernels  40.7 us (37%)
  starting transfers between devices  24.3 us (22%)
  other arithmetic  2.32 us (2%)
  local copies, waits for them, and re-layouts  2.03 us (2%)
    all_to_all x2, waiting for transfers between devices, exchange(): return lax.all_to_all(array, 'sky', split_axis=0, concat_axis=0, tiled=True)  30.5 us
    pallas_call x1, Pallas kernels, upper_warp(): pl.pallas_call(functools.partial(upper_kernel, pairs), grid=(1,), in_spec...  17.2 us
    pallas_call x2, Pallas kernels, filtered(): pl.pallas_call(functools.partial(filter_kernel, spans, owners, len(halos)...  13.6 us
    ppermute x6, waiting for transfers between devices, coadd(): whole = whole + lax.ppermute(sums[step], 'visit', ring).astype(jnp.float32)  10.3 us
    ppermute x6, starting transfers between devices, coadd(): whole = whole + lax.ppermute(sums[step], 'visit', ring).astype(jnp.float32)  10 us
    pallas_call x1, Pallas kernels, lower_warp(): pl.pallas_call(functools.partial(lower_kernel, pairs), in_specs=[pl.Block...  9.83 us
    all_to_all x2, starting transfers between devices, exchange(): return lax.all_to_all(array, 'sky', split_axis=0, concat_axis=0, tiled=True)  8.78 us
    ppermute x1, starting transfers between devices, local(): lax.ppermute(jnp.where(even, high, low), 'sky', [(i, (i - 1 if i % 2 == 0...  5.39 us
  transfers between devices with their start and end apart: 10, of which 4 were waited for; matrix products, arithmetic and copies ran while one was open for 2% of the time, Pallas kernels for 37%

profile of v7, /device:TPU:0, one launch (start us, length us, event | category | flops | bytes accessed | tf_op | source)
XLA Modules:
  0.0 110.4 jit_solution(5281193262393045740)
XLA Ops:
  0.0 1.1 %fusion.11 = (bf16[1,16,4096]{2,1,0:T(8,128)(2,1)S(1)}, bf16[1,16,4096]{2,1,0:T(8,128)(2,1)S(1)}, bf16[1,16,4096]{2,1,0:T(8,128)(2,1)S(1)}, bf16[1,16,4096]{2,1,0:T(8,128)(2,1)S(1)}) fusion(bf16[1,128,4096]{2,1,0:T(8,128)(2,1)} %param.8, bf16[1,128,4096]{2,1,0:T(8,128)(2,1)} %param.9), kind=kLoop, calls=%fused_computation.30 | loop fusion | bytes 1048576 | tf_op jit(solution)/shard_map/slice | solution.py:580
  1.3 5.4 %collective-permute-start.1 = (bf16[2,16,4096]{2,1,0:T(8,128)(2,1)S(1)}, bf16[2,16,4096]{2,1,0:T(8,128)(2,1)S(1)}, u32[]{:S(2)}, u32[]{:S(2)}) collective-permute-start(bf16[2,16,4096]{2,1,0:T(8,128)(2,1)S(1)} %get-tuple-element.41), channel_id=1, source_target_pairs={{0,31},{1,2},{2,1},{3,4},{4,3},{5,6},{6,5},{7,8},{8,7},{9,10},{10,... | collective-permute-start | bytes 786440 | tf_op jit(solution)/shard_map/ppermute | solution.py:586
  6.7 7.0 %filter.2 = bf16[32,336,128]{2,1,0:T(8,128)(2,1)} custom-call(s32[1,1,32]{2,1,0:T(1,128)} %owner_ref.3, bf16[1,2,21]{2,1,0:T(2,128)(2,1)} %taps_ref.3, bf16[128,4096]{1,0:T(8,128)(2,1)} %bitcast.15, bf16[128,4096]{1,0:T(8,128)(2,1)} %bitcast.17, s32[128,4096]{1,0:T(8,128)} %bitcast.19, bf16[4,2,32]{2,1,0:T(2,128)(2,1)} %bitcast.21, ...), custom_call_target="tpu_custom_call" | custom-call | flops 2000000000 | bytes 16777216 | tf_op jit(solution)/shard_map/filter/pallas_call | solution.py:229
  13.7 4.1 %all-to-all-start = ((bf16[32,336,128]{2,1,0:T(8,128)(2,1)}), bf16[32,336,128]{2,1,0:T(8,128)(2,1)S(1)}, u32[]{:S(2)}, u32[]{:S(2)}) async-start(bf16[32,336,128]{2,1,0:T(8,128)(2,1)} %filter.2), calls=%async_computation | async-start | bytes 5505024 | tf_op jit(solution)/shard_map/all_to_all | solution.py:578
  17.8 0.8 broadcast_select_fusion
  18.7 6.6 %filter.3 = bf16[32,192,128]{2,1,0:T(8,128)(2,1)} custom-call(s32[1,1,32]{2,1,0:T(1,128)} %owner_ref.3, bf16[1,2,21]{2,1,0:T(2,128)(2,1)} %taps_ref.3, bf16[128,4096]{1,0:T(8,128)(2,1)} %bitcast.16, bf16[128,4096]{1,0:T(8,128)(2,1)} %bitcast.18, s32[128,4096]{1,0:T(8,128)} %bitcast.20, bf16[2,16,4096]{2,1,0:T(8,128)(2,1)} %get-tuple-element.40.refs_3_, ...), custom_call_target="tpu_custom_call" | custom-call | flops 2000000000 | bytes 16777216 | tf_op jit(solution)/shard_map/filter/pallas_call | solution.py:229
  25.3 30.0 %all-to-all-done.first_ref.refs_0_ = bf16[32,336,128]{2,1,0:T(8,128)(2,1)S(1)} async-done(((bf16[32,336,128]{2,1,0:T(8,128)(2,1)}), bf16[32,336,128]{2,1,0:T(8,128)(2,1)S(1)}, u32[]{:S(2)}, u32[]{:S(2)}) %all-to-all-start) | async-done | bytes 2752544 | tf_op jit(solution)/shard_map/all_to_all | solution.py:578
  55.3 4.7 %all-to-all-start.1 = ((bf16[32,192,128]{2,1,0:T(8,128)(2,1)}), bf16[32,192,128]{2,1,0:T(8,128)(2,1)}, u32[]{:S(2)}, u32[]{:S(2)}) async-start(bf16[32,192,128]{2,1,0:T(8,128)(2,1)} %filter.3), calls=%async_computation.1 | async-start | bytes 3145728 | tf_op jit(solution)/shard_map/all_to_all | solution.py:578
  60.0 0.2 slice.43
  60.2 0.2 fusion.10
  60.4 0.1 fusion.5
  60.5 0.7 reshape.34.aim_ref
  61.2 17.2 %upper_warp.1 = (bf16[64,4,64,128]{3,2,1,0:T(8,128)(2,1)}, bf16[64,4,128,128]{3,2,1,0:T(8,128)(2,1)}, f32[8,128,128]{2,1,0:T(8,128)}, bf16[8,128,128]{2,1,0:T(8,...) custom-call(s32[256]{0:T(256)} %reshape.34.aim_ref, f32[64,128]{1,0:T(8,128)} %copy-done.3, ...), custom_call_target="tpu_custom_call" | custom-call | flops 10000000000 | bytes 33554432 | tf_op jit(solution)/shard_map/upper_warp/pallas_call | solution.py:429
  78.5 4.0 %collective-permute-start.5 = (bf16[8,128,128]{2,1,0:T(8,128)(2,1)}, bf16[8,128,128]{2,1,0:T(8,128)(2,1)S(1)}, u32[]{:S(2)}, u32[]{:S(2)}) collective-permute-start(bf16[8,128,128]{2,1,0:T(8,128)(2,1)} %get-tuple-element.32), channel_id=1, source_target_pairs={{0,64},{32,96},{64,0},{96,32},{1,65},{33,97},{65,1},{97,33},{2,66}... | collective-permute-start | bytes 786440 | tf_op jit(solution)/shard_map/ppermute | solution.py:624
  82.5 1.0 collective-permute-start.6
  83.5 0.5 all-to-all-done.1.refs_1_
  84.0 9.8 %lower_warp.1 = (f32[8,128,128]{2,1,0:T(8,128)}, bf16[8,128,128]{2,1,0:T(8,128)(2,1)}, bf16[8,128,128]{2,1,0:T(8,128)(2,1)}, bf16[8,128,128]{2,1,0:T(8,128)(2,1)}) custom-call(s32[256]{0:T(256)} %reshape.34.aim_ref, bf16[32,336,128]{2,1,0:T(8,128)(2,1)} %copy-done, bf16[32,192,128]{2,1,0:T(8,128)(2,1)} %all-to-all-done.1.refs_1_, ...), custom_call_target="tpu_custom_call" | custom-call | flops 6000000000 | bytes 33554432 | tf_op jit(solution)/shard_map/lower_warp/pallas_call | solution.py:540
  93.8 4.0 %collective-permute-start.2 = (bf16[8,128,128]{2,1,0:T(8,128)(2,1)}, bf16[8,128,128]{2,1,0:T(8,128)(2,1)S(1)}, u32[]{:S(2)}, u32[]{:S(2)}) collective-permute-start(bf16[8,128,128]{2,1,0:T(8,128)(2,1)} %get-tuple-element.28), channel_id=1, source_target_pairs={{0,64},{32,96},{64,0},{96,32},{1,65},{33,97},{65,1},{97,33},{2,66}... | collective-permute-start | bytes 786440 | tf_op jit(solution)/shard_map/ppermute | solution.py:624
  97.8 1.0 collective-permute-start.3
  98.8 0.1 convert_add_fusion
  99.0 6.2 %collective-permute-done.2 = bf16[8,128,128]{2,1,0:T(8,128)(2,1)S(1)} collective-permute-done((bf16[8,128,128]{2,1,0:T(8,128)(2,1)}, bf16[8,128,128]{2,1,0:T(8,128)(2,1)S(1)}, u32[]{:S(2)}, u32[]{:S(2)}) %collective-permute-start.2) | collective-permute-done | bytes 262176 | tf_op jit(solution)/shard_map/ppermute | solution.py:624
  105.2 4.1 %collective-permute-done.3 = bf16[8,128,128]{2,1,0:T(8,128)(2,1)S(1)} collective-permute-done((bf16[8,128,128]{2,1,0:T(8,128)(2,1)}, bf16[8,128,128]{2,1,0:T(8,128)(2,1)S(1)}, u32[]{:S(2)}, u32[]{:S(2)}) %collective-permute-start.3) | collective-permute-done | bytes 262176 | tf_op jit(solution)/shard_map/ppermute | solution.py:624
  109.3 0.1 convert_add_fusion.1
  109.5 0.8 pad_maximum_fusion
  (23 shorter events, 0.3 us)
Async XLA Ops:
  1.2 12.5 %collective-permute-start = (bf16[2,16,4096]{2,1,0:T(8,128)(2,1)S(1)}, bf16[2,16,4096]{2,1,0:T(8,128)(2,1)S(1)}, u32[]{:S(2)}, u32[]{:S(2)}) collective-permute-start(bf16[2,16,4096]{2,1,0:T(8,128)(2,1)S(1)} %get-tuple-element.42), channel_id=1, source_target_pairs={{0,1},{1,0},{2,3},{3,2},{4,5},{5,4},{6,7},{7,6},{8,9},{9,8},{10,11... | collective-permute-start | bytes 786440 | tf_op jit(solution)/shard_map/ppermute | solution.py:583
  1.3 12.5 %collective-permute-start.1 = (bf16[2,16,4096]{2,1,0:T(8,128)(2,1)S(1)}, bf16[2,16,4096]{2,1,0:T(8,128)(2,1)S(1)}, u32[]{:S(2)}, u32[]{:S(2)}) collective-permute-start(bf16[2,16,4096]{2,1,0:T(8,128)(2,1)S(1)} %get-tuple-element.41), channel_id=1, source_target_pairs={{0,31},{1,2},{2,1},{3,4},{4,3},{5,6},{6,5},{7,8},{8,7},{9,10},{10,... | collective-permute-start | bytes 786440 | tf_op jit(solution)/shard_map/ppermute | solution.py:586
  13.7 41.6 %all-to-all-start = ((bf16[32,336,128]{2,1,0:T(8,128)(2,1)}), bf16[32,336,128]{2,1,0:T(8,128)(2,1)S(1)}, u32[]{:S(2)}, u32[]{:S(2)}) async-start(bf16[32,336,128]{2,1,0:T(8,128)(2,1)} %filter.2), calls=%async_computation | async-start | bytes 5505024 | tf_op jit(solution)/shard_map/all_to_all | solution.py:578
  55.3 5.9 %copy-start = (bf16[32,336,128]{2,1,0:T(8,128)(2,1)}, bf16[32,336,128]{2,1,0:T(8,128)(2,1)S(1)}, u32[]{:S(2)}) copy-start(bf16[32,336,128]{2,1,0:T(8,128)(2,1)S(1)} %all-to-all-done.first_ref.refs_0_) | copy-start | bytes 8257540
  55.3 28.6 %all-to-all-start.1 = ((bf16[32,192,128]{2,1,0:T(8,128)(2,1)}), bf16[32,192,128]{2,1,0:T(8,128)(2,1)}, u32[]{:S(2)}, u32[]{:S(2)}) async-start(bf16[32,192,128]{2,1,0:T(8,128)(2,1)} %filter.3), calls=%async_computation.1 | async-start | bytes 3145728 | tf_op jit(solution)/shard_map/all_to_all | solution.py:578
  60.2 1.0 copy-start.3
  78.5 20.3 %collective-permute-start.5 = (bf16[8,128,128]{2,1,0:T(8,128)(2,1)}, bf16[8,128,128]{2,1,0:T(8,128)(2,1)S(1)}, u32[]{:S(2)}, u32[]{:S(2)}) collective-permute-start(bf16[8,128,128]{2,1,0:T(8,128)(2,1)} %get-tuple-element.32), channel_id=1, source_target_pairs={{0,64},{32,96},{64,0},{96,32},{1,65},{33,97},{65,1},{97,33},{2,66}... | collective-permute-start | bytes 786440 | tf_op jit(solution)/shard_map/ppermute | solution.py:624
  82.5 16.4 %collective-permute-start.6 = (bf16[8,128,128]{2,1,0:T(8,128)(2,1)}, bf16[8,128,128]{2,1,0:T(8,128)(2,1)S(1)}, u32[]{:S(2)}, u32[]{:S(2)}) collective-permute-start(bf16[8,128,128]{2,1,0:T(8,128)(2,1)} %get-tuple-element.33), channel_id=1, source_target_pairs={{0,32},{32,0},{64,96},{96,64},{1,33},{33,1},{65,97},{97,65},{2,34}... | collective-permute-start | bytes 786440 | tf_op jit(solution)/shard_map/ppermute | solution.py:624
  83.5 15.4 %collective-permute-start.7 = (bf16[8,128,128]{2,1,0:T(8,128)(2,1)}, bf16[8,128,128]{2,1,0:T(8,128)(2,1)S(1)}, u32[]{:S(2)}, u32[]{:S(2)}) collective-permute-start(bf16[8,128,128]{2,1,0:T(8,128)(2,1)} %get-tuple-element.34), channel_id=1, source_target_pairs={{0,96},{32,64},{64,32},{96,0},{1,97},{33,65},{65,33},{97,1},{2,98}... | collective-permute-start | bytes 786440 | tf_op jit(solution)/shard_map/ppermute | solution.py:624
  84.0 14.9 %copy-start.1 = (f32[8,128,128]{2,1,0:T(8,128)S(1)}, f32[8,128,128]{2,1,0:T(8,128)}, u32[]{:S(2)}) copy-start(f32[8,128,128]{2,1,0:T(8,128)} %get-tuple-element.31) | copy-start | bytes 1572868
  93.8 15.5 %copy-start.2 = (f32[8,128,128]{2,1,0:T(8,128)S(1)}, f32[8,128,128]{2,1,0:T(8,128)}, u32[]{:S(2)}) copy-start(f32[8,128,128]{2,1,0:T(8,128)} %get-tuple-element.27) | copy-start | bytes 1572868
  93.8 11.4 %collective-permute-start.2 = (bf16[8,128,128]{2,1,0:T(8,128)(2,1)}, bf16[8,128,128]{2,1,0:T(8,128)(2,1)S(1)}, u32[]{:S(2)}, u32[]{:S(2)}) collective-permute-start(bf16[8,128,128]{2,1,0:T(8,128)(2,1)} %get-tuple-element.28), channel_id=1, source_target_pairs={{0,64},{32,96},{64,0},{96,32},{1,65},{33,97},{65,1},{97,33},{2,66}... | collective-permute-start | bytes 786440 | tf_op jit(solution)/shard_map/ppermute | solution.py:624
  97.8 11.5 %collective-permute-start.3 = (bf16[8,128,128]{2,1,0:T(8,128)(2,1)}, bf16[8,128,128]{2,1,0:T(8,128)(2,1)S(1)}, u32[]{:S(2)}, u32[]{:S(2)}) collective-permute-start(bf16[8,128,128]{2,1,0:T(8,128)(2,1)} %get-tuple-element.29), channel_id=1, source_target_pairs={{0,32},{32,0},{64,96},{96,64},{1,33},{33,1},{65,97},{97,65},{2,34}... | collective-permute-start | bytes 786440 | tf_op jit(solution)/shard_map/ppermute | solution.py:624
  98.8 10.5 %collective-permute-start.4 = (bf16[8,128,128]{2,1,0:T(8,128)(2,1)}, bf16[8,128,128]{2,1,0:T(8,128)(2,1)S(1)}, u32[]{:S(2)}, u32[]{:S(2)}) collective-permute-start(bf16[8,128,128]{2,1,0:T(8,128)(2,1)} %get-tuple-element.30), channel_id=1, source_target_pairs={{0,96},{32,64},{64,32},{96,0},{1,97},{33,65},{65,33},{97,1},{2,98}... | collective-permute-start | bytes 786440 | tf_op jit(solution)/shard_map/ppermute | solution.py:624

commit v8 on v7

--- a/solution.py
+++ b/solution.py
@@ -20,7 +20,7 @@
 REACH = 16
 FACTS = 8
 FILTER_COLUMNS = 2048
-UPPER_PARTS = 4
+UPPER_PARTS = 8
 FILTER_VMEM = 60 * 1024 * 1024
 UPPER_VMEM = 60 * 1024 * 1024
 LOWER_VMEM = 58 * 1024 * 1024

time: 111 us -> 111 us (level)
  no operation moved by 1% of the time
where the time goes in v8:
time: 111 us; the launch traced here: 110 us
  waiting for transfers between devices  41.3 us (37%)
  Pallas kernels  40.4 us (36%)
  starting transfers between devices  24.1 us (22%)
  other arithmetic  2.32 us (2%)
  local copies, waits for them, and re-layouts  2.03 us (2%)
    all_to_all x2, waiting for transfers between devices, exchange(): return lax.all_to_all(array, 'sky', split_axis=0, concat_axis=0, tiled=True)  31 us
    pallas_call x1, Pallas kernels, upper_warp(): pl.pallas_call(functools.partial(upper_kernel, pairs), grid=(1,), in_spec...  16.9 us
    pallas_call x2, Pallas kernels, filtered(): pl.pallas_call(functools.partial(filter_kernel, spans, owners, len(halos)...  13.7 us
    ppermute x6, waiting for transfers between devices, coadd(): whole = whole + lax.ppermute(sums[step], 'visit', ring).astype(jnp.float32)  10.3 us
    ppermute x6, starting transfers between devices, coadd(): whole = whole + lax.ppermute(sums[step], 'visit', ring).astype(jnp.float32)  9.85 us
    pallas_call x1, Pallas kernels, lower_warp(): pl.pallas_call(functools.partial(lower_kernel, pairs), in_specs=[pl.Block...  9.83 us
    all_to_all x2, starting transfers between devices, exchange(): return lax.all_to_all(array, 'sky', split_axis=0, concat_axis=0, tiled=True)  8.78 us
    ppermute x1, starting transfers between devices, local(): lax.ppermute(jnp.where(even, high, low), 'sky', [(i, (i - 1 if i % 2 == 0...  5.39 us
  transfers between devices with their start and end apart: 10, of which 4 were waited for; matrix products, arithmetic and copies ran while one was open for 2% of the time, Pallas kernels for 37%

profile of v8, /device:TPU:0, one launch (start us, length us, event | category | flops | bytes accessed | tf_op | source)
XLA Modules:
  0.0 110.3 jit_solution(5938191964833936317)
XLA Ops:
  0.0 1.1 %fusion.11 = (bf16[1,16,4096]{2,1,0:T(8,128)(2,1)S(1)}, bf16[1,16,4096]{2,1,0:T(8,128)(2,1)S(1)}, bf16[1,16,4096]{2,1,0:T(8,128)(2,1)S(1)}, bf16[1,16,4096]{2,1,0:T(8,128)(2,1)S(1)}) fusion(bf16[1,128,4096]{2,1,0:T(8,128)(2,1)} %param.8, bf16[1,128,4096]{2,1,0:T(8,128)(2,1)} %param.9), kind=kLoop, calls=%fused_computation.30 | loop fusion | bytes 1048576 | tf_op jit(solution)/shard_map/slice | solution.py:580
  1.3 5.4 %collective-permute-start.1 = (bf16[2,16,4096]{2,1,0:T(8,128)(2,1)S(1)}, bf16[2,16,4096]{2,1,0:T(8,128)(2,1)S(1)}, u32[]{:S(2)}, u32[]{:S(2)}) collective-permute-start(bf16[2,16,4096]{2,1,0:T(8,128)(2,1)S(1)} %get-tuple-element.41), channel_id=1, source_target_pairs={{0,31},{1,2},{2,1},{3,4},{4,3},{5,6},{6,5},{7,8},{8,7},{9,10},{10,... | collective-permute-start | bytes 786440 | tf_op jit(solution)/shard_map/ppermute | solution.py:586
  6.7 7.1 %filter.2 = bf16[32,336,128]{2,1,0:T(8,128)(2,1)} custom-call(s32[1,1,32]{2,1,0:T(1,128)} %owner_ref.3, bf16[1,2,21]{2,1,0:T(2,128)(2,1)} %taps_ref.3, bf16[128,4096]{1,0:T(8,128)(2,1)} %bitcast.15, bf16[128,4096]{1,0:T(8,128)(2,1)} %bitcast.17, s32[128,4096]{1,0:T(8,128)} %bitcast.19, bf16[4,2,32]{2,1,0:T(2,128)(2,1)} %bitcast.21, ...), custom_call_target="tpu_custom_call" | custom-call | flops 2000000000 | bytes 16777216 | tf_op jit(solution)/shard_map/filter/pallas_call | solution.py:229
  13.8 4.1 %all-to-all-start = ((bf16[32,336,128]{2,1,0:T(8,128)(2,1)}), bf16[32,336,128]{2,1,0:T(8,128)(2,1)S(1)}, u32[]{:S(2)}, u32[]{:S(2)}) async-start(bf16[32,336,128]{2,1,0:T(8,128)(2,1)} %filter.2), calls=%async_computation | async-start | bytes 5505024 | tf_op jit(solution)/shard_map/all_to_all | solution.py:578
  17.9 0.8 broadcast_select_fusion
  18.7 6.6 %filter.3 = bf16[32,192,128]{2,1,0:T(8,128)(2,1)} custom-call(s32[1,1,32]{2,1,0:T(1,128)} %owner_ref.3, bf16[1,2,21]{2,1,0:T(2,128)(2,1)} %taps_ref.3, bf16[128,4096]{1,0:T(8,128)(2,1)} %bitcast.16, bf16[128,4096]{1,0:T(8,128)(2,1)} %bitcast.18, s32[128,4096]{1,0:T(8,128)} %bitcast.20, bf16[2,16,4096]{2,1,0:T(8,128)(2,1)} %get-tuple-element.40.refs_3_, ...), custom_call_target="tpu_custom_call" | custom-call | flops 2000000000 | bytes 16777216 | tf_op jit(solution)/shard_map/filter/pallas_call | solution.py:229
  25.3 30.1 %all-to-all-done.first_ref.refs_0_ = bf16[32,336,128]{2,1,0:T(8,128)(2,1)S(1)} async-done(((bf16[32,336,128]{2,1,0:T(8,128)(2,1)}), bf16[32,336,128]{2,1,0:T(8,128)(2,1)S(1)}, u32[]{:S(2)}, u32[]{:S(2)}) %all-to-all-start) | async-done | bytes 2752544 | tf_op jit(solution)/shard_map/all_to_all | solution.py:578
  55.4 4.7 %all-to-all-start.1 = ((bf16[32,192,128]{2,1,0:T(8,128)(2,1)}), bf16[32,192,128]{2,1,0:T(8,128)(2,1)}, u32[]{:S(2)}, u32[]{:S(2)}) async-start(bf16[32,192,128]{2,1,0:T(8,128)(2,1)} %filter.3), calls=%async_computation.1 | async-start | bytes 3145728 | tf_op jit(solution)/shard_map/all_to_all | solution.py:578
  60.1 0.2 slice.43
  60.3 0.2 fusion.10
  60.5 0.1 fusion.5
  60.6 0.7 reshape.34.aim_ref
  61.3 16.9 %upper_warp.1 = (bf16[64,4,64,128]{3,2,1,0:T(8,128)(2,1)}, bf16[64,4,128,128]{3,2,1,0:T(8,128)(2,1)}, f32[8,128,128]{2,1,0:T(8,128)}, bf16[8,128,128]{2,1,0:T(8,...) custom-call(s32[256]{0:T(256)} %reshape.34.aim_ref, f32[64,128]{1,0:T(8,128)} %copy-done.3, ...), custom_call_target="tpu_custom_call" | custom-call | flops 10000000000 | bytes 33554432 | tf_op jit(solution)/shard_map/upper_warp/pallas_call | solution.py:429
  78.2 3.9 %collective-permute-start.5 = (bf16[8,128,128]{2,1,0:T(8,128)(2,1)}, bf16[8,128,128]{2,1,0:T(8,128)(2,1)S(1)}, u32[]{:S(2)}, u32[]{:S(2)}) collective-permute-start(bf16[8,128,128]{2,1,0:T(8,128)(2,1)} %get-tuple-element.32), channel_id=1, source_target_pairs={{0,64},{32,96},{64,0},{96,32},{1,65},{33,97},{65,1},{97,33},{2,66}... | collective-permute-start | bytes 786440 | tf_op jit(solution)/shard_map/ppermute | solution.py:624
  82.1 1.0 collective-permute-start.6
  83.1 0.9 all-to-all-done.1.refs_1_
  84.0 9.8 %lower_warp.1 = (f32[8,128,128]{2,1,0:T(8,128)}, bf16[8,128,128]{2,1,0:T(8,128)(2,1)}, bf16[8,128,128]{2,1,0:T(8,128)(2,1)}, bf16[8,128,128]{2,1,0:T(8,128)(2,1)}) custom-call(s32[256]{0:T(256)} %reshape.34.aim_ref, bf16[32,336,128]{2,1,0:T(8,128)(2,1)} %copy-done, bf16[32,192,128]{2,1,0:T(8,128)(2,1)} %all-to-all-done.1.refs_1_, ...), custom_call_target="tpu_custom_call" | custom-call | flops 6000000000 | bytes 33554432 | tf_op jit(solution)/shard_map/lower_warp/pallas_call | solution.py:540
  93.9 3.9 %collective-permute-start.2 = (bf16[8,128,128]{2,1,0:T(8,128)(2,1)}, bf16[8,128,128]{2,1,0:T(8,128)(2,1)S(1)}, u32[]{:S(2)}, u32[]{:S(2)}) collective-permute-start(bf16[8,128,128]{2,1,0:T(8,128)(2,1)} %get-tuple-element.28), channel_id=1, source_target_pairs={{0,64},{32,96},{64,0},{96,32},{1,65},{33,97},{65,1},{97,33},{2,66}... | collective-permute-start | bytes 786440 | tf_op jit(solution)/shard_map/ppermute | solution.py:624
  97.8 1.0 collective-permute-start.3
  98.8 0.1 convert_add_fusion
  99.0 6.2 %collective-permute-done.2 = bf16[8,128,128]{2,1,0:T(8,128)(2,1)S(1)} collective-permute-done((bf16[8,128,128]{2,1,0:T(8,128)(2,1)}, bf16[8,128,128]{2,1,0:T(8,128)(2,1)S(1)}, u32[]{:S(2)}, u32[]{:S(2)}) %collective-permute-start.2) | collective-permute-done | bytes 262176 | tf_op jit(solution)/shard_map/ppermute | solution.py:624
  105.2 4.1 %collective-permute-done.3 = bf16[8,128,128]{2,1,0:T(8,128)(2,1)S(1)} collective-permute-done((bf16[8,128,128]{2,1,0:T(8,128)(2,1)}, bf16[8,128,128]{2,1,0:T(8,128)(2,1)S(1)}, u32[]{:S(2)}, u32[]{:S(2)}) %collective-permute-start.3) | collective-permute-done | bytes 262176 | tf_op jit(solution)/shard_map/ppermute | solution.py:624
  109.3 0.1 convert_add_fusion.1
  109.5 0.8 pad_maximum_fusion
  (23 shorter events, 0.3 us)
Async XLA Ops:
  1.2 12.6 %collective-permute-start = (bf16[2,16,4096]{2,1,0:T(8,128)(2,1)S(1)}, bf16[2,16,4096]{2,1,0:T(8,128)(2,1)S(1)}, u32[]{:S(2)}, u32[]{:S(2)}) collective-permute-start(bf16[2,16,4096]{2,1,0:T(8,128)(2,1)S(1)} %get-tuple-element.42), channel_id=1, source_target_pairs={{0,1},{1,0},{2,3},{3,2},{4,5},{5,4},{6,7},{7,6},{8,9},{9,8},{10,11... | collective-permute-start | bytes 786440 | tf_op jit(solution)/shard_map/ppermute | solution.py:583
  1.3 12.5 %collective-permute-start.1 = (bf16[2,16,4096]{2,1,0:T(8,128)(2,1)S(1)}, bf16[2,16,4096]{2,1,0:T(8,128)(2,1)S(1)}, u32[]{:S(2)}, u32[]{:S(2)}) collective-permute-start(bf16[2,16,4096]{2,1,0:T(8,128)(2,1)S(1)} %get-tuple-element.41), channel_id=1, source_target_pairs={{0,31},{1,2},{2,1},{3,4},{4,3},{5,6},{6,5},{7,8},{8,7},{9,10},{10,... | collective-permute-start | bytes 786440 | tf_op jit(solution)/shard_map/ppermute | solution.py:586
  13.8 41.6 %all-to-all-start = ((bf16[32,336,128]{2,1,0:T(8,128)(2,1)}), bf16[32,336,128]{2,1,0:T(8,128)(2,1)S(1)}, u32[]{:S(2)}, u32[]{:S(2)}) async-start(bf16[32,336,128]{2,1,0:T(8,128)(2,1)} %filter.2), calls=%async_computation | async-start | bytes 5505024 | tf_op jit(solution)/shard_map/all_to_all | solution.py:578
  55.4 5.9 %copy-start = (bf16[32,336,128]{2,1,0:T(8,128)(2,1)}, bf16[32,336,128]{2,1,0:T(8,128)(2,1)S(1)}, u32[]{:S(2)}) copy-start(bf16[32,336,128]{2,1,0:T(8,128)(2,1)S(1)} %all-to-all-done.first_ref.refs_0_) | copy-start | bytes 8257540
  55.4 28.6 %all-to-all-start.1 = ((bf16[32,192,128]{2,1,0:T(8,128)(2,1)}), bf16[32,192,128]{2,1,0:T(8,128)(2,1)}, u32[]{:S(2)}, u32[]{:S(2)}) async-start(bf16[32,192,128]{2,1,0:T(8,128)(2,1)} %filter.3), calls=%async_computation.1 | async-start | bytes 3145728 | tf_op jit(solution)/shard_map/all_to_all | solution.py:578
  60.3 1.0 copy-start.3
  78.2 20.6 %collective-permute-start.5 = (bf16[8,128,128]{2,1,0:T(8,128)(2,1)}, bf16[8,128,128]{2,1,0:T(8,128)(2,1)S(1)}, u32[]{:S(2)}, u32[]{:S(2)}) collective-permute-start(bf16[8,128,128]{2,1,0:T(8,128)(2,1)} %get-tuple-element.32), channel_id=1, source_target_pairs={{0,64},{32,96},{64,0},{96,32},{1,65},{33,97},{65,1},{97,33},{2,66}... | collective-permute-start | bytes 786440 | tf_op jit(solution)/shard_map/ppermute | solution.py:624
  82.1 16.7 %collective-permute-start.6 = (bf16[8,128,128]{2,1,0:T(8,128)(2,1)}, bf16[8,128,128]{2,1,0:T(8,128)(2,1)S(1)}, u32[]{:S(2)}, u32[]{:S(2)}) collective-permute-start(bf16[8,128,128]{2,1,0:T(8,128)(2,1)} %get-tuple-element.33), channel_id=1, source_target_pairs={{0,32},{32,0},{64,96},{96,64},{1,33},{33,1},{65,97},{97,65},{2,34}... | collective-permute-start | bytes 786440 | tf_op jit(solution)/shard_map/ppermute | solution.py:624
  83.1 15.7 %collective-permute-start.7 = (bf16[8,128,128]{2,1,0:T(8,128)(2,1)}, bf16[8,128,128]{2,1,0:T(8,128)(2,1)S(1)}, u32[]{:S(2)}, u32[]{:S(2)}) collective-permute-start(bf16[8,128,128]{2,1,0:T(8,128)(2,1)} %get-tuple-element.34), channel_id=1, source_target_pairs={{0,96},{32,64},{64,32},{96,0},{1,97},{33,65},{65,33},{97,1},{2,98}... | collective-permute-start | bytes 786440 | tf_op jit(solution)/shard_map/ppermute | solution.py:624
  84.0 14.8 %copy-start.1 = (f32[8,128,128]{2,1,0:T(8,128)S(1)}, f32[8,128,128]{2,1,0:T(8,128)}, u32[]{:S(2)}) copy-start(f32[8,128,128]{2,1,0:T(8,128)} %get-tuple-element.31) | copy-start | bytes 1572868
  93.9 15.4 %copy-start.2 = (f32[8,128,128]{2,1,0:T(8,128)S(1)}, f32[8,128,128]{2,1,0:T(8,128)}, u32[]{:S(2)}) copy-start(f32[8,128,128]{2,1,0:T(8,128)} %get-tuple-element.27) | copy-start | bytes 1572868
  93.9 11.4 %collective-permute-start.2 = (bf16[8,128,128]{2,1,0:T(8,128)(2,1)}, bf16[8,128,128]{2,1,0:T(8,128)(2,1)S(1)}, u32[]{:S(2)}, u32[]{:S(2)}) collective-permute-start(bf16[8,128,128]{2,1,0:T(8,128)(2,1)} %get-tuple-element.28), channel_id=1, source_target_pairs={{0,64},{32,96},{64,0},{96,32},{1,65},{33,97},{65,1},{97,33},{2,66}... | collective-permute-start | bytes 786440 | tf_op jit(solution)/shard_map/ppermute | solution.py:624
  97.8 11.5 %collective-permute-start.3 = (bf16[8,128,128]{2,1,0:T(8,128)(2,1)}, bf16[8,128,128]{2,1,0:T(8,128)(2,1)S(1)}, u32[]{:S(2)}, u32[]{:S(2)}) collective-permute-start(bf16[8,128,128]{2,1,0:T(8,128)(2,1)} %get-tuple-element.29), channel_id=1, source_target_pairs={{0,32},{32,0},{64,96},{96,64},{1,33},{33,1},{65,97},{97,65},{2,34}... | collective-permute-start | bytes 786440 | tf_op jit(solution)/shard_map/ppermute | solution.py:624
  98.8 10.5 %collective-permute-start.4 = (bf16[8,128,128]{2,1,0:T(8,128)(2,1)}, bf16[8,128,128]{2,1,0:T(8,128)(2,1)S(1)}, u32[]{:S(2)}, u32[]{:S(2)}) collective-permute-start(bf16[8,128,128]{2,1,0:T(8,128)(2,1)} %get-tuple-element.30), channel_id=1, source_target_pairs={{0,96},{32,64},{64,32},{96,0},{1,97},{33,65},{65,33},{97,1},{2,98}... | collective-permute-start | bytes 786440 | tf_op jit(solution)/shard_map/ppermute | solution.py:624
